TPU v7x, 768 devices: a whole 4x8x12 slice. The times are simulated.
768 devices in a mesh: row: 16 (over y, core), col: 12 (over z_lo, x), split: 4 (over z_hi).
Axes of the slice: x: 4, y: 8, z: 12 (z_hi: 4, z_lo: 3; z = z_hi * 3 + z_lo), core: 2. Of those that a mesh axis runs over, the one named last changes fastest.
Arguments:
- start_vectors: float32 [8, 98304], P(None, ('row', 'col', 'split')), may hold values from -16 to 16
- diag_energy: float32 [98304], P(('row', 'col', 'split')), may hold values from 0.35 to 6
- matrix_blocks: float32 [16, 12, 64, 128, 128], P('row', 'col', 'split'), may hold values from -0.125 to 0.125
- block_rows: int32 [16, 12, 64], P('row', 'col', 'split'), may hold values from 0 to 47, as said below
- block_cols: int32 [16, 12, 64], P('row', 'col', 'split'), may hold values from 0 to 63
- counts: int32 [16, 12, 4], P('row', 'col', 'split'), may hold values from 0 to 16, as said below
Outputs:
- residual_block: float32 [8, 98304], P(None, ('row', 'col', 'split'))
- second_image: float32 [8, 98304], P(None, ('row', 'col', 'split'))
Inputs may be any that keep to these rules, and one draw needn't show every extreme that they name: `block_rows`: every used slot names a block strictly above the block diagonal in the global numbering; slots at or past the count are unused and their entries are arbitrary within range. `counts`: some tile split holds exactly 16 used slots in every draw.
All inputs are finite; a program needn't handle non-finite values.
Results may differ from a plain program's by a relative error of at most 0.0003.
Values sent between devices are 32-bit elements; how exact they have to be, the bound alone decides.
No kernel may reach another device: no remote copies, remote signals or barrier semaphores. Data moves between devices by JAX's collectives and lax.ppermute only.
A program may use at most 32 MiB of HBM per device.

v0:
```python
import jax
import jax.numpy as jnp
from jax import lax
from jax.sharding import PartitionSpec as P


def apply_hamiltonian(vectors, diag_energy, block_tile, row_index, col_index, in_use):
    vector_count = vectors.shape[0]
    block_size = block_tile.shape[-1]
    row_piece = lax.all_gather(vectors, ("col", "split"), axis=1, tiled=True)
    col_piece = lax.all_gather(vectors, ("row", "split"), axis=1, tiled=True)
    row_piece = row_piece.reshape(vector_count, -1, block_size)
    col_piece = col_piece.reshape(vector_count, -1, block_size)
    row_blocks = row_piece.shape[1]
    col_blocks = col_piece.shape[1]
    col_inputs = jnp.take(col_piece, col_index, axis=1)
    upper_part = jnp.einsum("bij,kbj->kbi", block_tile, col_inputs, precision=lax.Precision.HIGHEST)
    upper_part = upper_part * in_use[None, :, None]
    row_inputs = jnp.take(row_piece, row_index, axis=1)
    lower_part = jnp.einsum("bji,kbj->kbi", block_tile, row_inputs, precision=lax.Precision.HIGHEST)
    lower_part = lower_part * in_use[None, :, None]
    row_hits = (row_index[None, :] == jnp.arange(row_blocks, dtype=jnp.int32)[:, None]).astype(
        jnp.float32
    )
    col_hits = (col_index[None, :] == jnp.arange(col_blocks, dtype=jnp.int32)[:, None]).astype(
        jnp.float32
    )
    row_terms = jnp.einsum("rb,kbi->kri", row_hits, upper_part, precision=lax.Precision.HIGHEST)
    col_terms = jnp.einsum("cb,kbi->kci", col_hits, lower_part, precision=lax.Precision.HIGHEST)
    row_share = lax.psum_scatter(
        row_terms.reshape(vector_count, row_blocks * block_size),
        ("col", "split"),
        scatter_dimension=1,
        tiled=True,
    )
    col_share = lax.psum_scatter(
        col_terms.reshape(vector_count, col_blocks * block_size),
        ("row", "split"),
        scatter_dimension=1,
        tiled=True,
    )
    return diag_energy[None, :] * vectors + row_share + col_share


def on_device(start_vectors, diag_energy, matrix_blocks, block_rows, block_cols, counts):
    slot_total = matrix_blocks.shape[2]
    block_size = matrix_blocks.shape[-1]
    block_tile = matrix_blocks.reshape(slot_total, block_size, block_size)
    row_index = block_rows.reshape(slot_total)
    col_index = block_cols.reshape(slot_total)
    in_use = (jnp.arange(slot_total, dtype=jnp.int32) < counts.reshape(())).astype(jnp.float32)
    total_rows = (
        start_vectors.shape[1]
        * lax.axis_size("row")
        * lax.axis_size("col")
        * lax.axis_size("split")
    )
    first_image = apply_hamiltonian(
        start_vectors, diag_energy, block_tile, row_index, col_index, in_use
    )
    local_terms = jnp.dot(start_vectors, first_image.T, precision=lax.Precision.HIGHEST)
    correlation = lax.psum(local_terms, ("row", "col", "split")) / total_rows
    residual_block = first_image - jnp.dot(
        correlation.T, start_vectors, precision=lax.Precision.HIGHEST
    )
    second_image = apply_hamiltonian(
        residual_block, diag_energy, block_tile, row_index, col_index, in_use
    )
    return (residual_block, second_image)


def solution(mesh):
    in_specs = (
        P(None, ("row", "col", "split")),
        P(("row", "col", "split")),
        P("row", "col", "split", None, None),
        P("row", "col", "split"),
        P("row", "col", "split"),
        P("row", "col", "split"),
    )
    out_specs = (P(None, ("row", "col", "split")), P(None, ("row", "col", "split")))
    return jax.shard_map(
        on_device, mesh=mesh, in_specs=in_specs, out_specs=out_specs, check_vma=False
    )
```

profile of v0, /device:TPU:6, one launch (start us, length us, event | category | flops | bytes accessed | tf_op | source)
XLA Modules:
  0.0 1290.7 jit_solution(10686688872259143598)
XLA Ops:
  7.2 0.0 copy-start
  7.2 0.0 copy-start.7
  7.2 0.0 reduce-scatter.7.cloned.1.call-start
  7.2 0.7 compare_select_fusion
  8.0 0.0 copy-done.7
  8.6 0.0 copy-start.1
  8.7 0.7 copy-done.1
  9.3 142.0 %all_gather.13 = f32[8,6144]{1,0:T(8,128)S(1)} all-gather(f32[8,128]{1,0:T(8,128)S(1)} %copy-done.1), channel_id=1, replica_groups=mesh['row'=16,'col'=12,'split'=4] {'col','split'}, dimensions={1}, use_global_device_ids=true | all-gather | bytes 200704 | tf_op jit(solution)/shard_map/all_gather | solution.py:10
  151.4 0.6 gather_fusion.1
  151.9 0.0 copy-done
  152.0 1.0 fusion.4
  153.0 0.7 copy-done.6
  153.6 0.4 convolution_bitcast_fusion.1
  154.0 0.9 copy.37
  154.9 0.0 reduce-scatter.7.cloned.1.call-update
  154.9 0.0 reduce-scatter.5.cloned.1.call-start
  154.9 155.3 %all_gather.12 = f32[8,8192]{1,0:T(8,128)S(1)} all-gather(f32[8,128]{1,0:T(8,128)S(1)} %copy-done.1), channel_id=1, replica_groups=mesh['row'=16,'col'=12,'split'=4] {'row','split'}, dimensions={1}, use_global_device_ids=true | all-gather | bytes 266240 | tf_op jit(solution)/shard_map/all_gather | solution.py:11
  310.3 0.6 gather_fusion
  310.9 1.8 fusion.6
  312.6 0.4 convolution_bitcast_fusion.3
  313.0 0.7 copy.39
  313.7 0.0 reduce-scatter.5.cloned.1.call-update
  313.8 0.0 reduce-scatter.11.cloned.1.call-start
  313.8 0.0 reduce-scatter.7.cloned.1.call-done
  313.8 283.8 %reduce-scatter.5.cloned.1.call-done = f32[8,128]{1,0:T(8,128)} async-done(((f32[8,6144]{1,0:T(8,128)}), f32[8,128]{1,0:T(8,128)}) %reduce-scatter.5.cloned.1.call-update) | async-done | bytes 4112 | tf_op jit(solution)/shard_map/reduce_scatter | solution.py:30
  597.6 0.0 copy-done.5
  597.6 0.8 convolution_bitcast_fusion.4
  598.4 109.1 %psum.7 = f32[8,8]{0,1:T(8,128)S(1)} all-reduce(f32[8,8]{0,1:T(8,128)S(1)} %convolution_bitcast_fusion.4), channel_id=1, replica_groups=mesh['row'=16,'col'=12,'split'=4] {'row','col','split'}, use_global_device_ids=true, to_apply=%region_2.5 | all-reduce | flops 64 | bytes 512 | tf_op jit(solution)/shard_map/psum | solution.py:62
  707.5 0.0 copy-done.3
  707.5 0.0 copy-done.4
  707.5 0.1 convolution_subtract_fusion
  707.6 130.5 %all_gather.15 = f32[8,6144]{1,0:T(8,128)S(1)} all-gather(f32[8,128]{1,0:T(8,128)S(1)} %convolution_subtract_fusion), channel_id=1, replica_groups=mesh['row'=16,'col'=12,'split'=4] {'col','split'}, dimensions={1}, use_global_device_ids=true | all-gather | bytes 200704 | tf_op jit(solution)/shard_map/all_gather | solution.py:10
  838.1 0.6 gather_fusion.3
  838.7 1.0 fusion
  839.7 0.4 convolution_bitcast_fusion
  840.1 0.9 copy.36
  840.9 0.0 reduce-scatter.11.cloned.1.call-update
  840.9 0.0 reduce-scatter.9.cloned.1.call-start
  841.0 158.3 %all_gather.14 = f32[8,8192]{1,0:T(8,128)S(1)} all-gather(f32[8,128]{1,0:T(8,128)S(1)} %convolution_subtract_fusion), channel_id=1, replica_groups=mesh['row'=16,'col'=12,'split'=4] {'row','split'}, dimensions={1}, use_global_device_ids=true | all-gather | bytes 266240 | tf_op jit(solution)/shard_map/all_gather | solution.py:11
  999.3 0.6 gather_fusion.2
  999.9 1.8 fusion.2
  1001.7 0.4 convolution_bitcast_fusion.2
  1002.0 0.7 copy.38
  1002.8 0.0 reduce-scatter.9.cloned.1.call-update
  1002.8 0.0 reduce-scatter.11.cloned.1.call-done
  1002.8 280.1 %reduce-scatter.9.cloned.1.call-done = f32[8,128]{1,0:T(8,128)} async-done(((f32[8,6144]{1,0:T(8,128)}), f32[8,128]{1,0:T(8,128)}) %reduce-scatter.9.cloned.1.call-update) | async-done | bytes 4112 | tf_op jit(solution)/shard_map/reduce_scatter | solution.py:30
  1282.9 0.0 copy-done.2
  1282.9 1.3 add_add_fusion
  (11 shorter events, 0.0 us)
Async XLA Ops:
  7.2 144.8 %copy-start = (f32[1,1,16,128,128]{4,3,2,1,0:T(8,128)S(1)}, f32[1,1,16,128,128]{4,3,2,1,0:T(8,128)}, u32[]{:S(2)}) copy-start(f32[1,1,16,128,128]{4,3,2,1,0:T(8,128)} %param.12) | copy-start | bytes 3145732
  7.2 0.8 copy-start.7
  7.2 306.6 %reduce-scatter.7.cloned.1.call-start = ((), (), s32[]{:S(2)}) async-start(), calls=%async_computation.5 | async-start | bytes 266240 | tf_op jit(solution)/shard_map/reduce_scatter | solution.py:36
  8.6 0.7 copy-start.1
  153.0 0.7 copy-start.6
  154.9 442.7 %reduce-scatter.5.cloned.1.call-start = ((), (), s32[]{:S(2)}) async-start(), calls=%async_computation.4 | async-start | bytes 200704 | tf_op jit(solution)/shard_map/reduce_scatter | solution.py:30
  313.7 283.9 %copy-start.5 = (f32[128]{0:T(128)S(1)}, f32[128]{0:T(128)}, u32[]{:S(2)}) copy-start(f32[128]{0:T(128)} %param.11) | copy-start | bytes 1540
  313.8 689.0 %reduce-scatter.11.cloned.1.call-start = ((), (), s32[]{:S(2)}) async-start(), calls=%async_computation.7 | async-start | bytes 266240 | tf_op jit(solution)/shard_map/reduce_scatter | solution.py:36
  598.4 109.1 %copy-start.3 = (f32[8,128]{1,0:T(8,128)S(1)}, f32[8,128]{1,0:T(8,128)}, u32[]{:S(2)}) copy-start(f32[8,128]{1,0:T(8,128)} %reduce-scatter.7.cloned.1.call-done) | copy-start | bytes 12292
  598.4 109.1 %copy-start.4 = (f32[8,128]{1,0:T(8,128)S(1)}, f32[8,128]{1,0:T(8,128)}, u32[]{:S(2)}) copy-start(f32[8,128]{1,0:T(8,128)} %reduce-scatter.5.cloned.1.call-done) | copy-start | bytes 12292
  707.6 575.2 %copy-start.2 = (f32[8,128]{1,0:T(8,128)}, f32[8,128]{1,0:T(8,128)S(1)}, u32[]{:S(2)}) copy-start(f32[8,128]{1,0:T(8,128)S(1)} %convolution_subtract_fusion) | copy-start | bytes 12292
  840.9 441.9 %reduce-scatter.9.cloned.1.call-start = ((), (), s32[]{:S(2)}) async-start(), calls=%async_computation.6 | async-start | bytes 200704 | tf_op jit(solution)/shard_map/reduce_scatter | solution.py:30
Sparse Core Ops, SparseCore 0:
  155.0 153.8 reduce-scatter.6
  313.9 283.6 reduce-scatter.4
  841.1 154.7 reduce-scatter.10
  1002.9 279.9 reduce-scatter.8
where the time goes:
time: 1300 us; the launch traced here: 1290 us
  blocking collectives  695 us (53%)
  waiting for transfers between devices  564 us (43%)
  between operations  14.6 us (1%)
    reduce_scatter x2, waiting for transfers between devices, apply_hamiltonian(): lax.psum_scatter(row_terms.reshape(vector_count, row_blocks * block_size)...  564 us
    all_gather x2, blocking collectives, apply_hamiltonian(): col_piece = lax.all_gather(vectors, ('row', 'split'), axis=1, tiled=True)  314 us
    all_gather x2, blocking collectives, apply_hamiltonian(): row_piece = lax.all_gather(vectors, ('col', 'split'), axis=1, tiled=True)  273 us
    psum x1, blocking collectives, on_device(): correlation = lax.psum(local_terms, ('row', 'col', 'split')) / total_rows  109 us
  transfers between devices with their start and end apart: 4, of which 2 were waited for; matrix products, arithmetic and copies ran while one was open for 1% of the time, Pallas kernels for 0%

commit v1 on v0

v1 whole, which is shorter than its diff:
```python
import jax
import jax.numpy as jnp
from jax import lax
from jax.experimental import pallas as pl
from jax.experimental.pallas import tpu as pltpu
from jax.sharding import PartitionSpec as P

HIGHEST = lax.Precision.HIGHEST


def block_products(blocks, row_index, col_index, count, row_in, col_in):
    slots = blocks.shape[0]

    def kernel(row_ids, col_ids, used, u_ref, row_ref, col_ref, row_out, col_out):
        row_out[...] = jnp.zeros_like(row_out)
        col_out[...] = jnp.zeros_like(col_out)
        for t in range(slots):
            keep = jnp.where(t < used[0], 1.0, 0.0).astype(jnp.float32)
            r, c = row_ids[t], col_ids[t]
            u = u_ref[t]
            upper = lax.dot_general(
                col_ref[c], u, (((1,), (1,)), ((), ())), precision=HIGHEST,
                preferred_element_type=jnp.float32,
            )
            lower = lax.dot_general(
                row_ref[r], u, (((1,), (0,)), ((), ())), precision=HIGHEST,
                preferred_element_type=jnp.float32,
            )
            row_out[r] += upper * keep
            col_out[c] += lower * keep

    smem = pl.BlockSpec(memory_space=pltpu.SMEM)
    vmem = pl.BlockSpec(memory_space=pltpu.VMEM)
    return pl.pallas_call(
        kernel,
        out_shape=(
            jax.ShapeDtypeStruct(row_in.shape, jnp.float32),
            jax.ShapeDtypeStruct(col_in.shape, jnp.float32),
        ),
        in_specs=[smem] * 3 + [vmem] * 3,
        out_specs=(vmem, vmem),
        compiler_params=pltpu.CompilerParams(vmem_limit_bytes=16 << 20),
        name="block_products",
    )(row_index, col_index, count, blocks, row_in, col_in)


def share(piece, axis):
    copies = jnp.broadcast_to(piece[None], (lax.axis_size(axis),) + piece.shape)
    return lax.all_to_all(copies, axis, 0, 0, tiled=True)


def exchange(parts, axis):
    return lax.all_to_all(parts, axis, 0, 0, tiled=True)


def on_device(start_vectors, diag_energy, matrix_blocks, block_rows, block_cols, counts):
    rows, cols, splits = (lax.axis_size(a) for a in ("row", "col", "split"))
    vectors, size = start_vectors.shape
    slots = matrix_blocks.shape[2]
    blocks = matrix_blocks.reshape(slots, size, size)
    row_index = block_rows.reshape(slots)
    col_index = block_cols.reshape(slots)
    count = counts.reshape(1)
    total = size * rows * cols * splits
    mine = lax.axis_index("split")
    is_mine = (jnp.arange(splits, dtype=jnp.int32) == mine).astype(jnp.float32)[:, None, None]

    start4 = share(start_vectors, "split")
    row_in = share(start4, "col").reshape(cols * splits, vectors, size)
    col_in = share(start4, "row").reshape(rows * splits, vectors, size)
    row_out, col_out = block_products(blocks, row_index, col_index, count, row_in, col_in)
    row_got = exchange(row_out.reshape(cols, splits, vectors, size), "col")
    col_got = exchange(col_out.reshape(rows, splits, vectors, size), "row")
    part = row_got.sum(0) + col_got.sum(0) + is_mine * (diag_energy[None, :] * start_vectors)[None]
    first4 = share(part, "split").sum(0)
    first = lax.dynamic_index_in_dim(first4, mine, 0, keepdims=False)

    group = jnp.einsum("skg,slg->kl", start4, first4, precision=HIGHEST)
    group = jnp.pad(group, ((0, 0), (0, size - vectors)))
    row_all = share(jnp.concatenate([first4, group[None]], 0), "col")
    tile_corr = row_all[:, splits].sum(0)
    row_in = row_all[:, :splits].reshape(cols * splits, vectors, size)
    col_in = share(first4, "row").reshape(rows * splits, vectors, size)
    row_out, col_out = block_products(blocks, row_index, col_index, count, row_in, col_in)
    row_got = exchange(row_out.reshape(cols, splits, vectors, size), "col")
    col_out = col_out.reshape(rows, splits, vectors, size)
    corr_out = jnp.broadcast_to(tile_corr[None, None], (rows, 1, vectors, size))
    col_got = exchange(jnp.concatenate([col_out, corr_out], 1), "row").sum(0)
    correlation = col_got[splits, :, :vectors] / total
    part = row_got.sum(0) + col_got[:splits]
    image = exchange(part, "split").sum(0) + diag_energy[None, :] * first
    residual = first - jnp.dot(correlation.T, start_vectors, precision=HIGHEST)
    second = image - jnp.dot(correlation.T, first, precision=HIGHEST)
    return residual, second


def solution(mesh):
    in_specs = (
        P(None, ("row", "col", "split")),
        P(("row", "col", "split")),
        P("row", "col", "split", None, None),
        P("row", "col", "split"),
        P("row", "col", "split"),
        P("row", "col", "split"),
    )
    out_specs = (P(None, ("row", "col", "split")), P(None, ("row", "col", "split")))
    return jax.shard_map(
        on_device, mesh=mesh, in_specs=in_specs, out_specs=out_specs, check_vma=False
    )
```

time: 1300 us -> 182 us (0.14)
  blocking collectives: 695 us -> 83 us
  waiting for transfers between devices: 564 us -> 53.5 us
  starting transfers between devices: 0.16 us -> 27.8 us
  between operations: 14.6 us -> 1.39 us
    all_gather x4 -> x0, blocking collectives: 586 us -> none  [the longest x2 314 us: apply_hamiltonian(): col_piece = lax.all_gather(vectors, ('row', 'split'), axis=1, tiled=True)]
    reduce_scatter x4 -> x0, waiting for transfers between devices: 564 us -> none  [the longest x2 564 us: apply_hamiltonian(): lax.psum_scatter(row_terms.reshape(vector_count, row_blocks * block_size)...]
    psum x1 -> x0, blocking collectives: 109 us -> none  [on_device(): correlation = lax.psum(local_terms, ('row', 'col', 'split')) / total_rows]
    all_to_all x0 -> x5, blocking collectives: none -> 83 us  [the longest x4 69.4 us: share(): return lax.all_to_all(copies, axis, 0, 0, tiled=True)]
    all_to_all x0 -> x6, waiting for transfers between devices: none -> 53.5 us  [the longest x4 35.6 us: exchange(): return lax.all_to_all(parts, axis, 0, 0, tiled=True)]
    all_to_all x0 -> x6, starting transfers between devices: none -> 27.8 us  [the longest x4 18.2 us: exchange(): return lax.all_to_all(parts, axis, 0, 0, tiled=True)]
  transfers between devices with their start and end apart: 4 -> 6, of which waited for: 2 -> 6; matrix products, arithmetic and copies ran while one was open for 1% -> 1% of each run, Pallas kernels for 0% -> 0%
where the time goes in v1:
time: 182 us; the launch traced here: 180 us
  blocking collectives  83 us (46%)
  waiting for transfers between devices  53.5 us (29%)
  starting transfers between devices  27.8 us (15%)
  Pallas kernels  7.56 us (4%)
  local copies, waits for them, and re-layouts  3.6 us (2%)
    all_to_all x4, blocking collectives, share(): return lax.all_to_all(copies, axis, 0, 0, tiled=True)  69.4 us
    all_to_all x4, waiting for transfers between devices, exchange(): return lax.all_to_all(parts, axis, 0, 0, tiled=True)  35.6 us
    all_to_all x4, starting transfers between devices, exchange(): return lax.all_to_all(parts, axis, 0, 0, tiled=True)  18.2 us
    all_to_all x2, waiting for transfers between devices, share(): return lax.all_to_all(copies, axis, 0, 0, tiled=True)  17.8 us
    all_to_all x1, blocking collectives, exchange(): return lax.all_to_all(parts, axis, 0, 0, tiled=True)  13.6 us
    all_to_all x2, starting transfers between devices, share(): return lax.all_to_all(copies, axis, 0, 0, tiled=True)  9.55 us
    pallas_call x2, Pallas kernels, block_products(): pl.pallas_call(kernel, out_shape=(jax.ShapeDtypeStruct(row_in.shape, jnp....  7.56 us
  transfers between devices with their start and end apart: 6, of which 6 were waited for; matrix products, arithmetic and copies ran while one was open for 1% of the time, Pallas kernels for 0%

profile of v1, /device:TPU:6, one launch (start us, length us, event | category | flops | bytes accessed | tf_op | source)
XLA Modules:
  0.0 180.0 jit_solution(14707572995235750577)
XLA Ops:
  0.6 0.0 copy-start
  0.6 0.8 broadcast_in_dim.16
  1.4 24.5 %all_to_all.55 = f32[4,8,128]{2,1,0:T(8,128)S(1)} all-to-all(f32[4,8,128]{2,1,0:T(8,128)S(1)} %broadcast_in_dim.16), channel_id=1, replica_groups=mesh['row'=16,'col'=12,'split'=4] {'split'}, dimensions={0} | all-to-all | bytes 32768 | tf_op jit(solution)/shard_map/all_to_all | solution.py:49
  25.9 18.2 %all_to_all.56 = f32[16,4,8,128]{3,2,1,0:T(8,128)S(1)} all-to-all(f32[16,4,8,128]{3,2,1,0:T(8,128)S(1)} %broadcast_in_dim.18), channel_id=1, replica_groups=mesh['row'=16,'col'=12,'split'=4] {'row'}, dimensions={0} | all-to-all | bytes 524288 | tf_op jit(solution)/shard_map/all_to_all | solution.py:49
  44.1 0.7 broadcast_in_dim.17
  44.8 6.0 %all-to-all-start.1 = ((f32[12,4,8,128]{3,2,1,0:T(8,128)}), f32[12,4,8,128]{3,2,1,0:T(8,128)S(1)}, u32[]{:S(2)}, u32[]{:S(2)}) async-start(f32[12,4,8,128]{3,2,1,0:T(8,128)} %broadcast_in_dim.17), calls=%async_computation.1 | async-start | bytes 393216 | tf_op jit(solution)/shard_map/all_to_all | solution.py:49
  51.5 6.9 %all-to-all-done.1 = f32[12,4,8,128]{3,2,1,0:T(8,128)S(1)} async-done(((f32[12,4,8,128]{3,2,1,0:T(8,128)}), f32[12,4,8,128]{3,2,1,0:T(8,128)S(1)}, u32[]{:S(2)}, u32[]{:S(2)}) %all-to-all-start.1) | async-done | bytes 196640 | tf_op jit(solution)/shard_map/all_to_all | solution.py:49
  58.3 0.0 copy-start.1
  58.3 0.0 copy-start.2
  58.3 0.0 copy-done
  58.3 0.6 copy-done.1
  59.0 0.0 copy-done.2
  59.0 3.8 %block_products.2 = (f32[48,8,128]{2,1,0:T(8,128)}, f32[64,8,128]{2,1,0:T(8,128)S(1)}) custom-call(s32[16]{0:T(128)S(1)} %bitcast.44, s32[16]{0:T(128)S(1)} %bitcast.46, s32[1]{0:T(128)} %bitcast.34.used, f32[16,128,128]{2,1,0:T(8,128)S(1)} %bitcast.36, f32[48,8,128]{2,1,0:T(8,128)S(1)} %bitcast.40, f32[64,8,128]{2,1,0:T(8,128)S(1)} %bitcast.38), custom_call_target="tpu_custom_call" | custom-call | tf_op jit(solution)/shard_map/block_products/pallas_call | solution.py:34
  62.8 13.6 %all_to_all.57 = f32[16,4,8,128]{3,2,1,0:T(8,128)S(1)} all-to-all(f32[16,4,8,128]{3,2,1,0:T(8,128)S(1)} %bitcast.43), channel_id=1, replica_groups=mesh['row'=16,'col'=12,'split'=4] {'row'}, dimensions={0} | all-to-all | bytes 524288 | tf_op jit(solution)/shard_map/all_to_all | solution.py:53
  76.4 4.7 %all-to-all-start.3 = ((f32[12,4,8,128]{3,2,1,0:T(8,128)}), f32[12,4,8,128]{3,2,1,0:T(8,128)S(1)}, u32[]{:S(2)}, u32[]{:S(2)}) async-start(f32[12,4,8,128]{3,2,1,0:T(8,128)} %bitcast.6), calls=%async_computation.3 | async-start | bytes 393216 | tf_op jit(solution)/shard_map/all_to_all | solution.py:53
  81.1 0.0 copy-start.3
  81.1 0.0 copy-start.4
  81.1 0.7 copy-done.3
  81.8 0.0 copy-done.4
  81.8 7.1 %all-to-all-done.3 = f32[12,4,8,128]{3,2,1,0:T(8,128)S(1)} async-done(((f32[12,4,8,128]{3,2,1,0:T(8,128)}), f32[12,4,8,128]{3,2,1,0:T(8,128)S(1)}, u32[]{:S(2)}, u32[]{:S(2)}) %all-to-all-start.3) | async-done | bytes 196640 | tf_op jit(solution)/shard_map/all_to_all | solution.py:53
  88.9 0.1 multiply_add_fusion
  89.0 15.7 %all_to_all.58 = f32[4,4,8,128]{3,2,1,0:T(8,128)S(1)} all-to-all(f32[4,4,8,128]{3,2,1,0:T(8,128)S(1)} %broadcast_in_dim.19), channel_id=1, replica_groups=mesh['row'=16,'col'=12,'split'=4] {'split'}, dimensions={0} | all-to-all | bytes 131072 | tf_op jit(solution)/shard_map/all_to_all | solution.py:49
  104.7 0.1 convolution_bitcast_fusion
  104.8 11.1 %all_to_all.59 = f32[12,5,8,128]{3,2,1,0:T(8,128)S(1)} all-to-all(f32[12,5,8,128]{3,2,1,0:T(8,128)S(1)} %broadcast_in_dim.21), channel_id=1, replica_groups=mesh['row'=16,'col'=12,'split'=4] {'col'}, dimensions={0} | all-to-all | bytes 491520 | tf_op jit(solution)/shard_map/all_to_all | solution.py:49
  115.9 0.7 broadcast_in_dim.22
  116.6 3.5 %all-to-all-start.7 = ((f32[16,4,8,128]{3,2,1,0:T(8,128)}), f32[16,4,8,128]{3,2,1,0:T(8,128)S(1)}, u32[]{:S(2)}, u32[]{:S(2)}) async-start(f32[16,4,8,128]{3,2,1,0:T(8,128)} %broadcast_in_dim.22), calls=%async_computation.7 | async-start | bytes 524288 | tf_op jit(solution)/shard_map/all_to_all | solution.py:49
  120.2 11.0 %all-to-all-done.7 = f32[16,4,8,128]{3,2,1,0:T(8,128)S(1)} async-done(((f32[16,4,8,128]{3,2,1,0:T(8,128)}), f32[16,4,8,128]{3,2,1,0:T(8,128)S(1)}, u32[]{:S(2)}, u32[]{:S(2)}) %all-to-all-start.7) | async-done | bytes 262176 | tf_op jit(solution)/shard_map/all_to_all | solution.py:49
  131.2 3.8 %block_products.3 = (f32[48,8,128]{2,1,0:T(8,128)}, f32[64,8,128]{2,1,0:T(8,128)S(1)}) custom-call(s32[16]{0:T(128)S(1)} %bitcast.45, s32[16]{0:T(128)S(1)} %bitcast.47, s32[1]{0:T(128)} %bitcast.35.used, f32[16,128,128]{2,1,0:T(8,128)S(1)} %bitcast.37, f32[48,8,128]{2,1,0:T(8,128)S(1)} %bitcast.41, f32[64,8,128]{2,1,0:T(8,128)S(1)} %bitcast.39), custom_call_target="tpu_custom_call" | custom-call | tf_op jit(solution)/shard_map/block_products/pallas_call | solution.py:34
  135.0 4.6 %all-to-all-start.9 = ((f32[12,4,8,128]{3,2,1,0:T(8,128)}), f32[12,4,8,128]{3,2,1,0:T(8,128)S(1)}, u32[]{:S(2)}, u32[]{:S(2)}) async-start(f32[12,4,8,128]{3,2,1,0:T(8,128)} %bitcast.16), calls=%async_computation.9 | async-start | bytes 393216 | tf_op jit(solution)/shard_map/all_to_all | solution.py:53
  139.6 0.7 pad_maximum_fusion
  140.3 6.9 %all-to-all-done.9 = f32[12,4,8,128]{3,2,1,0:T(8,128)S(1)} async-done(((f32[12,4,8,128]{3,2,1,0:T(8,128)}), f32[12,4,8,128]{3,2,1,0:T(8,128)S(1)}, u32[]{:S(2)}, u32[]{:S(2)}) %all-to-all-start.9) | async-done | bytes 196640 | tf_op jit(solution)/shard_map/all_to_all | solution.py:53
  147.2 3.5 %all-to-all-start.8 = ((f32[16,5,8,128]{3,2,1,0:T(8,128)}), f32[16,5,8,128]{3,2,1,0:T(8,128)S(1)}, u32[]{:S(2)}, u32[]{:S(2)}) async-start(f32[16,5,8,128]{3,2,1,0:T(8,128)} %pad_maximum_fusion), calls=%async_computation.8 | async-start | bytes 655360 | tf_op jit(solution)/shard_map/all_to_all | solution.py:53
  150.8 12.2 %all-to-all-done.8 = f32[16,5,8,128]{3,2,1,0:T(8,128)S(1)} async-done(((f32[16,5,8,128]{3,2,1,0:T(8,128)}), f32[16,5,8,128]{3,2,1,0:T(8,128)S(1)}, u32[]{:S(2)}, u32[]{:S(2)}) %all-to-all-start.8) | async-done | bytes 327712 | tf_op jit(solution)/shard_map/all_to_all | solution.py:53
  163.1 0.6 slice_add_fusion
  163.7 5.4 %all-to-all-start.10 = ((f32[4,8,128]{2,1,0:T(8,128)}), f32[4,8,128]{2,1,0:T(8,128)S(1)}, u32[]{:S(2)}, u32[]{:S(2)}) async-start(f32[4,8,128]{2,1,0:T(8,128)} %slice_add_fusion), calls=%async_computation.10 | async-start | bytes 32768 | tf_op jit(solution)/shard_map/all_to_all | solution.py:53
  169.1 0.8 convolution_subtract_fusion.1
  169.8 9.4 %all-to-all-done.10 = f32[4,8,128]{2,1,0:T(8,128)S(1)} async-done(((f32[4,8,128]{2,1,0:T(8,128)}), f32[4,8,128]{2,1,0:T(8,128)S(1)}, u32[]{:S(2)}, u32[]{:S(2)}) %all-to-all-start.10) | async-done | bytes 16416 | tf_op jit(solution)/shard_map/all_to_all | solution.py:53
  179.2 0.8 convolution_subtract_fusion
  (16 shorter events, 0.2 us)
Async XLA Ops:
  0.6 57.7 %copy-start = (f32[1,1,16,128,128]{4,3,2,1,0:T(8,128)S(1)}, f32[1,1,16,128,128]{4,3,2,1,0:T(8,128)}, u32[]{:S(2)}) copy-start(f32[1,1,16,128,128]{4,3,2,1,0:T(8,128)} %param.8) | copy-start | bytes 3145732
  44.8 13.5 %all-to-all-start.1 = ((f32[12,4,8,128]{3,2,1,0:T(8,128)}), f32[12,4,8,128]{3,2,1,0:T(8,128)S(1)}, u32[]{:S(2)}, u32[]{:S(2)}) async-start(f32[12,4,8,128]{3,2,1,0:T(8,128)} %broadcast_in_dim.17), calls=%async_computation.1 | async-start | bytes 393216 | tf_op jit(solution)/shard_map/all_to_all | solution.py:49
  58.3 0.7 copy-start.1
  58.3 0.7 copy-start.2
  76.4 12.5 %all-to-all-start.3 = ((f32[12,4,8,128]{3,2,1,0:T(8,128)}), f32[12,4,8,128]{3,2,1,0:T(8,128)S(1)}, u32[]{:S(2)}, u32[]{:S(2)}) async-start(f32[12,4,8,128]{3,2,1,0:T(8,128)} %bitcast.6), calls=%async_computation.3 | async-start | bytes 393216 | tf_op jit(solution)/shard_map/all_to_all | solution.py:53
  81.1 0.7 copy-start.3
  81.1 0.7 copy-start.4
  116.6 14.5 %all-to-all-start.7 = ((f32[16,4,8,128]{3,2,1,0:T(8,128)}), f32[16,4,8,128]{3,2,1,0:T(8,128)S(1)}, u32[]{:S(2)}, u32[]{:S(2)}) async-start(f32[16,4,8,128]{3,2,1,0:T(8,128)} %broadcast_in_dim.22), calls=%async_computation.7 | async-start | bytes 524288 | tf_op jit(solution)/shard_map/all_to_all | solution.py:49
  135.0 12.2 %all-to-all-start.9 = ((f32[12,4,8,128]{3,2,1,0:T(8,128)}), f32[12,4,8,128]{3,2,1,0:T(8,128)S(1)}, u32[]{:S(2)}, u32[]{:S(2)}) async-start(f32[12,4,8,128]{3,2,1,0:T(8,128)} %bitcast.16), calls=%async_computation.9 | async-start | bytes 393216 | tf_op jit(solution)/shard_map/all_to_all | solution.py:53
  147.2 15.8 %all-to-all-start.8 = ((f32[16,5,8,128]{3,2,1,0:T(8,128)}), f32[16,5,8,128]{3,2,1,0:T(8,128)S(1)}, u32[]{:S(2)}, u32[]{:S(2)}) async-start(f32[16,5,8,128]{3,2,1,0:T(8,128)} %pad_maximum_fusion), calls=%async_computation.8 | async-start | bytes 655360 | tf_op jit(solution)/shard_map/all_to_all | solution.py:53
  163.7 15.6 %all-to-all-start.10 = ((f32[4,8,128]{2,1,0:T(8,128)}), f32[4,8,128]{2,1,0:T(8,128)S(1)}, u32[]{:S(2)}, u32[]{:S(2)}) async-start(f32[4,8,128]{2,1,0:T(8,128)} %slice_add_fusion), calls=%async_computation.10 | async-start | bytes 32768 | tf_op jit(solution)/shard_map/all_to_all | solution.py:53

commit v2 on v1

v2 whole, which is shorter than its diff:
```python
import jax
import jax.numpy as jnp
from jax import lax
from jax.experimental import pallas as pl
from jax.experimental.pallas import tpu as pltpu
from jax.sharding import PartitionSpec as P

HIGHEST = lax.Precision.HIGHEST
SMEM = pl.BlockSpec(memory_space=pltpu.SMEM)
VMEM = pl.BlockSpec(memory_space=pltpu.VMEM)
PARAMS = pltpu.CompilerParams(vmem_limit_bytes=16 << 20)


def arrays(*shapes):
    return tuple(jax.ShapeDtypeStruct(s, jnp.float32) for s in shapes)


def products(ids_from, ids_to, used, u_ref, in_ref, out_ref, block_dim):
    out_ref[...] = jnp.zeros_like(out_ref)
    for t in range(u_ref.shape[0]):
        term = lax.dot_general(
            in_ref[ids_from[t]], u_ref[t], (((1,), (block_dim,)), ((), ())), precision=HIGHEST,
            preferred_element_type=jnp.float32,
        )
        out_ref[ids_to[t]] += term * jnp.where(t < used[0], 1.0, 0.0).astype(jnp.float32)


def block_products(ids_from, ids_to, count, blocks, pieces, out_blocks, block_dim, name):
    slots, size, _ = blocks.shape
    vectors = pieces.shape[1]

    def kernel(a, b, n, u, x, o):
        products(a, b, n, u, x, o, block_dim)

    return pl.pallas_call(
        kernel,
        out_shape=jax.ShapeDtypeStruct((out_blocks, vectors, size), jnp.float32),
        in_specs=[SMEM] * 3 + [VMEM] * 2,
        out_specs=VMEM,
        compiler_params=PARAMS,
        cost_estimate=pl.CostEstimate(
            flops=12 * slots * size * size * vectors, bytes_accessed=4 * slots * size * size,
            transcendentals=0,
        ),
        name=name,
    )(ids_from, ids_to, count, blocks, pieces)


def own_copies(row_piece, place, splits, copies):
    _, vectors, size = row_piece.shape

    def kernel(at, piece, out):
        for s in range(splits):
            block = piece[at[0] * splits + s]
            for i in range(copies):
                out[i, s] = block

    return pl.pallas_call(
        kernel, out_shape=arrays((copies, splits, vectors, size))[0],
        in_specs=[SMEM, VMEM], out_specs=VMEM, compiler_params=PARAMS, name="own_copies",
    )(place, row_piece)


def group_part(row_got, col_got, vectors, diag, place):
    splits = row_got.shape[1]

    def kernel(at, rows, cols, v, d, out):
        own = v[...] * d[...]
        for s in range(splits):
            total = rows[0, s]
            for j in range(1, rows.shape[0]):
                total += rows[j, s]
            for i in range(cols.shape[0]):
                total += cols[i, s]
            total += own * jnp.where(at[0] == s, 1.0, 0.0).astype(jnp.float32)
            for k in range(splits):
                out[k, s] = total

    return pl.pallas_call(
        kernel, out_shape=arrays((splits,) + row_got.shape[1:])[0],
        in_specs=[SMEM] + [VMEM] * 4, out_specs=VMEM, compiler_params=PARAMS, name="group_part",
    )(place, row_got, col_got, vectors, diag)


def image_copies(parts, rows, cols, place):
    splits, _, vectors, size = parts.shape

    def kernel(at, p, col_out, row_out, own):
        for s in range(splits):
            total = p[0, s]
            for k in range(1, splits):
                total += p[k, s]
            for j in range(cols):
                col_out[j, s] = total
            for i in range(rows):
                row_out[i, s] = total
        own[...] = row_out[0, at[0]]

    return pl.pallas_call(
        kernel,
        out_shape=arrays((cols, splits, vectors, size), (rows, splits, vectors, size), (vectors, size)),
        in_specs=[SMEM, VMEM], out_specs=(VMEM,) * 3, compiler_params=PARAMS, name="image_copies",
    )(place, parts)


def products_and_correlation(
    ids_from, ids_to, count, blocks, pieces, start_piece, rows, splits
):
    slots, size, _ = blocks.shape
    tile, vectors, _ = pieces.shape

    def kernel(a, b, n, u, x, v, out):
        out[...] = jnp.zeros_like(out)
        term = jnp.zeros((vectors, vectors), jnp.float32)
        for g in range(tile):
            term += lax.dot_general(
                x[g], v[g], (((1,), (1,)), ((), ())), precision=HIGHEST,
                preferred_element_type=jnp.float32,
            )
        for i in range(rows):
            out[i, splits, :, :vectors] = term
        for t in range(slots):
            product = lax.dot_general(
                x[a[t]], u[t], (((1,), (0,)), ((), ())), precision=HIGHEST,
                preferred_element_type=jnp.float32,
            )
            keep = jnp.where(t < n[0], 1.0, 0.0).astype(jnp.float32)
            to, at = lax.div(b[t], jnp.int32(splits)), lax.rem(b[t], jnp.int32(splits))
            out[to, at] += product * keep

    return pl.pallas_call(
        kernel,
        out_shape=arrays((rows, splits + 1, vectors, size))[0],
        in_specs=[SMEM] * 3 + [VMEM] * 3,
        out_specs=VMEM,
        compiler_params=PARAMS,
        cost_estimate=pl.CostEstimate(
            flops=12 * slots * size * size * vectors, bytes_accessed=4 * slots * size * size,
            transcendentals=0,
        ),
        name="lower_and_correlation",
    )(ids_from, ids_to, count, blocks, pieces, start_piece)


def add_to_messages(col_got, row_out, place):
    rows, more, vectors, size = col_got.shape
    splits = more - 1

    def kernel(at, got, sums, out, corr):
        out[...] = sums[...]
        for s in range(more):
            total = got[0, s]
            for i in range(1, rows):
                total += got[i, s]
            if s < splits:
                out[at[0] * splits + s] += total
            else:
                corr[...] = total

    return pl.pallas_call(
        kernel, out_shape=arrays(row_out.shape, (vectors, size)),
        in_specs=[SMEM, VMEM, VMEM], out_specs=(VMEM, VMEM), compiler_params=PARAMS,
        name="add_to_messages",
    )(place, col_got, row_out)


def subtract(corr, base, value, total):
    scaled = corr[:, : value.shape[0]] * (1.0 / total)
    return base - lax.dot_general(
        scaled, value, (((1,), (0,)), ((), ())), precision=HIGHEST,
        preferred_element_type=jnp.float32,
    )


def residual_of(corr, first, start, total):
    def kernel(c, f, v, out):
        out[...] = subtract(c[...], f[...], v[...], total)

    return pl.pallas_call(
        kernel, out_shape=arrays(first.shape)[0], in_specs=[VMEM] * 3, out_specs=VMEM,
        compiler_params=PARAMS, name="residual",
    )(corr, first, start)


def second_of(got, corr, first, diag, total):
    def kernel(g, c, f, d, out):
        value = f[...]
        image = d[...] * value
        for k in range(g.shape[0]):
            image += g[k]
        out[...] = subtract(c[...], image, value, total)

    return pl.pallas_call(
        kernel, out_shape=arrays(first.shape)[0], in_specs=[VMEM] * 4, out_specs=VMEM,
        compiler_params=PARAMS, name="second",
    )(got, corr, first, diag)


def exchange(parts, axis):
    return lax.all_to_all(parts, axis, 0, 0, tiled=True)


def on_device(start_vectors, diag_energy, matrix_blocks, block_rows, block_cols, counts):
    rows, cols, splits = (lax.axis_size(a) for a in ("row", "col", "split"))
    vectors, size = start_vectors.shape
    slots = matrix_blocks.shape[2]
    blocks = matrix_blocks.reshape(slots, size, size)
    row_ids = block_rows.reshape(slots)
    col_ids = block_cols.reshape(slots)
    count = counts.reshape(1)
    diag = diag_energy.reshape(1, size)
    total = size * rows * cols * splits
    at_col = lax.axis_index("col").astype(jnp.int32).reshape(1)
    at_split = lax.axis_index("split").astype(jnp.int32).reshape(1)
    plane = ("col", "split")

    copies = jnp.broadcast_to(start_vectors[None], (cols * splits, vectors, size))
    start_row = exchange(copies, plane)
    start_col = exchange(own_copies(start_row, at_col, splits, rows), "row")
    lower = block_products(row_ids, col_ids, count, blocks, start_row, rows * splits, 0, "lower")
    col_got = exchange(lower.reshape(rows, splits, vectors, size), "row")
    start_col = start_col.reshape(rows * splits, vectors, size)
    upper = block_products(col_ids, row_ids, count, blocks, start_col, cols * splits, 1, "upper")
    row_got = exchange(upper.reshape(cols, splits, vectors, size), "col")
    parts = exchange(group_part(row_got, col_got, start_vectors, diag, at_split), "split")

    col_copies, row_copies, first = image_copies(parts, rows, cols, at_split)
    first_row = exchange(col_copies, "col").reshape(cols * splits, vectors, size)
    first_col = exchange(row_copies, "row").reshape(rows * splits, vectors, size)
    lower = products_and_correlation(row_ids, col_ids, count, blocks, first_row, start_row, rows, splits)
    col_got = exchange(lower, "row")
    upper = block_products(col_ids, row_ids, count, blocks, first_col, cols * splits, 1, "upper")
    messages, corr = add_to_messages(col_got, upper, at_col)
    got = exchange(messages, plane)
    residual = residual_of(corr, first, start_vectors, total)
    return residual, second_of(got, corr, first, diag, total)


def solution(mesh):
    in_specs = (
        P(None, ("row", "col", "split")),
        P(("row", "col", "split")),
        P("row", "col", "split", None, None),
        P("row", "col", "split"),
        P("row", "col", "split"),
        P("row", "col", "split"),
    )
    out_specs = (P(None, ("row", "col", "split")), P(None, ("row", "col", "split")))
    return jax.shard_map(
        on_device, mesh=mesh, in_specs=in_specs, out_specs=out_specs, check_vma=False
    )
```

time: 182 us -> 166 us (0.912)
  blocking collectives: 83 us -> 26.8 us
  starting transfers between devices: 27.8 us -> 47.5 us
  waiting for transfers between devices: 53.5 us -> 70.9 us
  Pallas kernels: 7.56 us -> 14.4 us
    all_to_all x4 -> x0, blocking collectives: 69.4 us -> none  [share(): return lax.all_to_all(copies, axis, 0, 0, tiled=True)]
    all_to_all x4 -> x7, waiting for transfers between devices: 35.6 us -> 70.9 us  [exchange(): return lax.all_to_all(parts, axis, 0, 0, tiled=True)]
    all_to_all x4 -> x7, starting transfers between devices: 18.2 us -> 47.5 us  [exchange(): return lax.all_to_all(parts, axis, 0, 0, tiled=True)]
    all_to_all x2 -> x0, waiting for transfers between devices: 17.8 us -> none  [share(): return lax.all_to_all(copies, axis, 0, 0, tiled=True)]
    all_to_all x1 -> x2, blocking collectives: 13.6 us -> 26.8 us  [exchange(): return lax.all_to_all(parts, axis, 0, 0, tiled=True)]
    all_to_all x2 -> x0, starting transfers between devices: 9.55 us -> none  [share(): return lax.all_to_all(copies, axis, 0, 0, tiled=True)]
    pallas_call x2 -> x10, Pallas kernels: 7.56 us -> 14.4 us  [the longest x3 7.4 us: block_products(): pl.pallas_call(kernel, out_shape=jax.ShapeDtypeStruct((out_blocks, vector...]
  transfers between devices with their start and end apart: 6 -> 7, of which waited for: 6 -> 7; matrix products, arithmetic and copies ran while one was open for 1% -> 0% of each run, Pallas kernels for 0% -> 7%
where the time goes in v2:
time: 166 us; the launch traced here: 164 us
  waiting for transfers between devices  70.9 us (43%)
  starting transfers between devices  47.5 us (29%)
  blocking collectives  26.8 us (16%)
  Pallas kernels  14.4 us (9%)
  local copies, waits for them, and re-layouts  2.76 us (2%)
    all_to_all x7, waiting for transfers between devices, exchange(): return lax.all_to_all(parts, axis, 0, 0, tiled=True)  70.9 us
    all_to_all x7, starting transfers between devices, exchange(): return lax.all_to_all(parts, axis, 0, 0, tiled=True)  47.5 us
    all_to_all x2, blocking collectives, exchange(): return lax.all_to_all(parts, axis, 0, 0, tiled=True)  26.8 us
    pallas_call x3, Pallas kernels, block_products(): pl.pallas_call(kernel, out_shape=jax.ShapeDtypeStruct((out_blocks, vector...  7.4 us
    pallas_call x1, Pallas kernels, products_and_correlation(): pl.pallas_call(kernel, out_shape=arrays((rows, splits + 1, vectors, size)...  3.35 us
  transfers between devices with their start and end apart: 7, of which 7 were waited for; matrix products, arithmetic and copies ran while one was open for 0% of the time, Pallas kernels for 7%

profile of v2, /device:TPU:6, one launch (start us, length us, event | category | flops | bytes accessed | tf_op | source)
XLA Modules:
  0.0 163.7 jit_solution(9074783485775397575)
XLA Ops:
  0.6 0.0 copy-start
  0.6 1.5 broadcast_in_dim.2
  2.1 18.4 %all-to-all-start = ((f32[48,8,128]{2,1,0:T(8,128)}), f32[48,8,128]{2,1,0:T(8,128)S(1)}, u32[]{:S(2)}, u32[]{:S(2)}) async-start(f32[48,8,128]{2,1,0:T(8,128)} %broadcast_in_dim.2), calls=%async_computation | async-start | bytes 393216 | tf_op jit(solution)/shard_map/all_to_all | solution.py:200
  20.5 14.6 %all-to-all-done.piece.x.v = f32[48,8,128]{2,1,0:T(8,128)S(1)} async-done(((f32[48,8,128]{2,1,0:T(8,128)}), f32[48,8,128]{2,1,0:T(8,128)S(1)}, u32[]{:S(2)}, u32[]{:S(2)}) %all-to-all-start) | async-done | bytes 196640 | tf_op jit(solution)/shard_map/all_to_all | solution.py:200
  35.2 0.7 own_copies.1
  35.9 7.2 %all-to-all-start.1 = ((f32[16,4,8,128]{3,2,1,0:T(8,128)}), f32[16,4,8,128]{3,2,1,0:T(8,128)S(1)}, u32[]{:S(2)}, u32[]{:S(2)}) async-start(f32[16,4,8,128]{3,2,1,0:T(8,128)} %own_copies.1), calls=%async_computation.1 | async-start | bytes 524288 | tf_op jit(solution)/shard_map/all_to_all | solution.py:200
  43.7 0.0 copy-start.2
  43.8 0.0 copy-start.3
  43.8 0.0 copy-done
  43.8 0.6 copy-done.2
  44.4 0.0 copy-done.3
  44.4 2.2 %lower.1 = f32[64,8,128]{2,1,0:T(8,128)} custom-call(s32[16]{0:T(128)S(1)} %bitcast.23, s32[16]{0:T(128)S(1)} %bitcast.27, s32[1]{0:T(128)} %bitcast.13.n, f32[16,128,128]{2,1,0:T(8,128)S(1)} %bitcast.16, f32[48,8,128]{2,1,0:T(8,128)S(1)} %all-to-all-done.piece.x.v), custom_call_target="tpu_custom_call" | custom-call | flops 25165824 | bytes 1048576 | tf_op jit(solution)/shard_map/lower/pallas_call | solution.py:35
  46.6 7.7 %all-to-all-done.1 = f32[16,4,8,128]{3,2,1,0:T(8,128)S(1)} async-done(((f32[16,4,8,128]{3,2,1,0:T(8,128)}), f32[16,4,8,128]{3,2,1,0:T(8,128)S(1)}, u32[]{:S(2)}, u32[]{:S(2)}) %all-to-all-start.1) | async-done | bytes 262176 | tf_op jit(solution)/shard_map/all_to_all | solution.py:200
  54.3 3.5 %all-to-all-start.3 = ((f32[16,4,8,128]{3,2,1,0:T(8,128)}), f32[16,4,8,128]{3,2,1,0:T(8,128)S(1)}, u32[]{:S(2)}, u32[]{:S(2)}) async-start(f32[16,4,8,128]{3,2,1,0:T(8,128)} %bitcast.8), calls=%async_computation.3 | async-start | bytes 524288 | tf_op jit(solution)/shard_map/all_to_all | solution.py:200
  57.8 3.0 %upper.2 = f32[48,8,128]{2,1,0:T(8,128)} custom-call(s32[16]{0:T(128)S(1)} %bitcast.28, s32[16]{0:T(128)S(1)} %bitcast.24, s32[1]{0:T(128)} %bitcast.12.n, f32[16,128,128]{2,1,0:T(8,128)S(1)} %bitcast.17, f32[64,8,128]{2,1,0:T(8,128)S(1)} %bitcast.21), custom_call_target="tpu_custom_call" | custom-call | flops 25165824 | bytes 1048576 | tf_op jit(solution)/shard_map/upper/pallas_call | solution.py:35
  60.8 8.4 %all-to-all-done.3.cols = f32[16,4,8,128]{3,2,1,0:T(8,128)S(1)} async-done(((f32[16,4,8,128]{3,2,1,0:T(8,128)}), f32[16,4,8,128]{3,2,1,0:T(8,128)S(1)}, u32[]{:S(2)}, u32[]{:S(2)}) %all-to-all-start.3) | async-done | bytes 262176 | tf_op jit(solution)/shard_map/all_to_all | solution.py:200
  69.1 4.8 %all-to-all-start.2 = ((f32[12,4,8,128]{3,2,1,0:T(8,128)}), f32[12,4,8,128]{3,2,1,0:T(8,128)S(1)}, u32[]{:S(2)}, u32[]{:S(2)}) async-start(f32[12,4,8,128]{3,2,1,0:T(8,128)} %bitcast.7), calls=%async_computation.2 | async-start | bytes 393216 | tf_op jit(solution)/shard_map/all_to_all | solution.py:200
  73.9 0.0 copy-start.1
  73.9 7.4 %all-to-all-done.2.rows = f32[12,4,8,128]{3,2,1,0:T(8,128)S(1)} async-done(((f32[12,4,8,128]{3,2,1,0:T(8,128)}), f32[12,4,8,128]{3,2,1,0:T(8,128)S(1)}, u32[]{:S(2)}, u32[]{:S(2)}) %all-to-all-start.2) | async-done | bytes 196640 | tf_op jit(solution)/shard_map/all_to_all | solution.py:200
  81.3 0.0 copy-start.4
  81.3 0.0 copy-done.1
  81.3 0.7 copy-done.4
  82.0 16.1 %all_to_all.45.p = f32[4,4,8,128]{3,2,1,0:T(8,128)S(1)} all-to-all(f32[4,4,8,128]{3,2,1,0:T(8,128)S(1)} %group_part.1), channel_id=1, replica_groups=mesh['row'=16,'col'=12,'split'=4] {'split'}, dimensions={0} | all-to-all | bytes 131072 | tf_op jit(solution)/shard_map/all_to_all | solution.py:200
  98.1 0.8 image_copies.1
  98.8 10.7 %all_to_all.46 = f32[12,4,8,128]{3,2,1,0:T(8,128)S(1)} all-to-all(f32[12,4,8,128]{3,2,1,0:T(8,128)S(1)} %get-tuple-element.7), channel_id=1, replica_groups=mesh['row'=16,'col'=12,'split'=4] {'col'}, dimensions={0} | all-to-all | bytes 393216 | tf_op jit(solution)/shard_map/all_to_all | solution.py:200
  109.5 3.5 %all-to-all-start.7 = ((f32[16,4,8,128]{3,2,1,0:T(8,128)}), f32[16,4,8,128]{3,2,1,0:T(8,128)S(1)}, u32[]{:S(2)}, u32[]{:S(2)}) async-start(f32[16,4,8,128]{3,2,1,0:T(8,128)} %get-tuple-element.8), calls=%async_computation.7 | async-start | bytes 524288 | tf_op jit(solution)/shard_map/all_to_all | solution.py:200
  113.1 3.4 %lower_and_correlation.1 = f32[16,5,8,128]{3,2,1,0:T(8,128)} custom-call(s32[16]{0:T(128)S(1)} %bitcast.25, s32[16]{0:T(128)S(1)} %bitcast.29, s32[1]{0:T(128)} %bitcast.14.n, f32[16,128,128]{2,1,0:T(8,128)S(1)} %bitcast.18, f32[48,8,128]{2,1,0:T(8,128)S(1)} %bitcast.22, f32[48,8,128]{2,1,0:T(8,128)S(1)} %all-to-all-done.piece.x.v), custom_call_target="tpu_custom_call" | custom-call | flops 25165824 | bytes 1048576 | tf_op jit(solution)/shard_map/lower_and_correlation/pallas_call | solution.py:131
  116.4 7.6 %all-to-all-done.7 = f32[16,4,8,128]{3,2,1,0:T(8,128)S(1)} async-done(((f32[16,4,8,128]{3,2,1,0:T(8,128)}), f32[16,4,8,128]{3,2,1,0:T(8,128)S(1)}, u32[]{:S(2)}, u32[]{:S(2)}) %all-to-all-start.7) | async-done | bytes 262176 | tf_op jit(solution)/shard_map/all_to_all | solution.py:200
  124.1 3.5 %all-to-all-start.6 = ((f32[16,5,8,128]{3,2,1,0:T(8,128)}), f32[16,5,8,128]{3,2,1,0:T(8,128)S(1)}, u32[]{:S(2)}, u32[]{:S(2)}) async-start(f32[16,5,8,128]{3,2,1,0:T(8,128)} %lower_and_correlation.1), calls=%async_computation.6 | async-start | bytes 655360 | tf_op jit(solution)/shard_map/all_to_all | solution.py:200
  127.6 2.3 %upper.3.sums = f32[48,8,128]{2,1,0:T(8,128)S(1)} custom-call(s32[16]{0:T(128)S(1)} %bitcast.30, s32[16]{0:T(128)S(1)} %bitcast.26, s32[1]{0:T(128)} %bitcast.15.n, f32[16,128,128]{2,1,0:T(8,128)S(1)} %bitcast.19, f32[64,8,128]{2,1,0:T(8,128)S(1)} %bitcast.20), custom_call_target="tpu_custom_call" | custom-call | flops 25165824 | bytes 1048576 | tf_op jit(solution)/shard_map/upper/pallas_call | solution.py:35
  129.9 10.3 %all-to-all-done.6.got = f32[16,5,8,128]{3,2,1,0:T(8,128)S(1)} async-done(((f32[16,5,8,128]{3,2,1,0:T(8,128)}), f32[16,5,8,128]{3,2,1,0:T(8,128)S(1)}, u32[]{:S(2)}, u32[]{:S(2)}) %all-to-all-start.6) | async-done | bytes 327712 | tf_op jit(solution)/shard_map/all_to_all | solution.py:200
  140.2 0.7 add_to_messages.1
  140.9 6.5 %all-to-all-start.8 = ((f32[48,8,128]{2,1,0:T(8,128)}), f32[48,8,128]{2,1,0:T(8,128)S(1)}, u32[]{:S(2)}, u32[]{:S(2)}) async-start(f32[48,8,128]{2,1,0:T(8,128)} %get-tuple-element.11), calls=%async_computation.8 | async-start | bytes 393216 | tf_op jit(solution)/shard_map/all_to_all | solution.py:200
  147.4 0.7 residual.1
  148.1 14.8 %all-to-all-done.8.g = f32[48,8,128]{2,1,0:T(8,128)S(1)} async-done(((f32[48,8,128]{2,1,0:T(8,128)}), f32[48,8,128]{2,1,0:T(8,128)S(1)}, u32[]{:S(2)}, u32[]{:S(2)}) %all-to-all-start.8) | async-done | bytes 196640 | tf_op jit(solution)/shard_map/all_to_all | solution.py:200
  163.0 0.7 second.1
  (1 shorter events, 0.0 us)
Async XLA Ops:
  0.6 43.1 %copy-start = (f32[1,1,16,128,128]{4,3,2,1,0:T(8,128)S(1)}, f32[1,1,16,128,128]{4,3,2,1,0:T(8,128)}, u32[]{:S(2)}) copy-start(f32[1,1,16,128,128]{4,3,2,1,0:T(8,128)} %param.8) | copy-start | bytes 3145732
  2.1 33.1 %all-to-all-start = ((f32[48,8,128]{2,1,0:T(8,128)}), f32[48,8,128]{2,1,0:T(8,128)S(1)}, u32[]{:S(2)}, u32[]{:S(2)}) async-start(f32[48,8,128]{2,1,0:T(8,128)} %broadcast_in_dim.2), calls=%async_computation | async-start | bytes 393216 | tf_op jit(solution)/shard_map/all_to_all | solution.py:200
  35.9 18.4 %all-to-all-start.1 = ((f32[16,4,8,128]{3,2,1,0:T(8,128)}), f32[16,4,8,128]{3,2,1,0:T(8,128)S(1)}, u32[]{:S(2)}, u32[]{:S(2)}) async-start(f32[16,4,8,128]{3,2,1,0:T(8,128)} %own_copies.1), calls=%async_computation.1 | async-start | bytes 524288 | tf_op jit(solution)/shard_map/all_to_all | solution.py:200
  43.7 0.7 copy-start.2
  43.8 0.7 copy-start.3
  54.3 14.9 %all-to-all-start.3 = ((f32[16,4,8,128]{3,2,1,0:T(8,128)}), f32[16,4,8,128]{3,2,1,0:T(8,128)S(1)}, u32[]{:S(2)}, u32[]{:S(2)}) async-start(f32[16,4,8,128]{3,2,1,0:T(8,128)} %bitcast.8), calls=%async_computation.3 | async-start | bytes 524288 | tf_op jit(solution)/shard_map/all_to_all | solution.py:200
  69.1 12.2 %all-to-all-start.2 = ((f32[12,4,8,128]{3,2,1,0:T(8,128)}), f32[12,4,8,128]{3,2,1,0:T(8,128)S(1)}, u32[]{:S(2)}, u32[]{:S(2)}) async-start(f32[12,4,8,128]{3,2,1,0:T(8,128)} %bitcast.7), calls=%async_computation.2 | async-start | bytes 393216 | tf_op jit(solution)/shard_map/all_to_all | solution.py:200
  73.9 7.4 %copy-start.1 = (f32[8,128]{1,0:T(8,128)S(1)}, f32[8,128]{1,0:T(8,128)}, u32[]{:S(2)}) copy-start(f32[8,128]{1,0:T(8,128)} %v.3) | copy-start | bytes 12292
  81.3 0.7 copy-start.4
  109.5 14.5 %all-to-all-start.7 = ((f32[16,4,8,128]{3,2,1,0:T(8,128)}), f32[16,4,8,128]{3,2,1,0:T(8,128)S(1)}, u32[]{:S(2)}, u32[]{:S(2)}) async-start(f32[16,4,8,128]{3,2,1,0:T(8,128)} %get-tuple-element.8), calls=%async_computation.7 | async-start | bytes 524288 | tf_op jit(solution)/shard_map/all_to_all | solution.py:200
  124.1 16.1 %all-to-all-start.6 = ((f32[16,5,8,128]{3,2,1,0:T(8,128)}), f32[16,5,8,128]{3,2,1,0:T(8,128)S(1)}, u32[]{:S(2)}, u32[]{:S(2)}) async-start(f32[16,5,8,128]{3,2,1,0:T(8,128)} %lower_and_correlation.1), calls=%async_computation.6 | async-start | bytes 655360 | tf_op jit(solution)/shard_map/all_to_all | solution.py:200
  140.9 22.1 %all-to-all-start.8 = ((f32[48,8,128]{2,1,0:T(8,128)}), f32[48,8,128]{2,1,0:T(8,128)S(1)}, u32[]{:S(2)}, u32[]{:S(2)}) async-start(f32[48,8,128]{2,1,0:T(8,128)} %get-tuple-element.11), calls=%async_computation.8 | async-start | bytes 393216 | tf_op jit(solution)/shard_map/all_to_all | solution.py:200

commit v3 on v2

v3 whole, which is shorter than its diff:
```python
import jax
import jax.numpy as jnp
from jax import lax
from jax.experimental import pallas as pl
from jax.experimental.pallas import tpu as pltpu
from jax.sharding import PartitionSpec as P

HIGHEST = lax.Precision.HIGHEST
SMEM = pl.BlockSpec(memory_space=pltpu.SMEM)
VMEM = pl.BlockSpec(memory_space=pltpu.VMEM)
PARAMS = pltpu.CompilerParams(vmem_limit_bytes=16 << 20)


def arrays(*shapes):
    return tuple(jax.ShapeDtypeStruct(s, jnp.float32) for s in shapes)


def add_products(ids_from, ids_to, used, u_ref, in_ref, out_ref, block_dim, from_slot, to_slot):
    for t in range(u_ref.shape[0]):
        term = lax.dot_general(
            in_ref[from_slot(ids_from[t])], u_ref[t], (((1,), (block_dim,)), ((), ())),
            precision=HIGHEST, preferred_element_type=jnp.float32,
        )
        keep = jnp.where(t < used[0], 1.0, 0.0).astype(jnp.float32)
        out_ref[to_slot(ids_to[t])] += term * keep


def same(block):
    return block


def column_slot(splits):
    core = lax.axis_index("core")

    def slot(c):
        row, s = lax.div(c, jnp.int32(splits)), lax.rem(c, jnp.int32(splits))
        y, its_core = lax.div(row, jnp.int32(2)), lax.rem(row, jnp.int32(2))
        other = jnp.where(its_core == core, 0, 1)
        return other, y, s

    return slot


def cost(blocks, vectors):
    return pl.CostEstimate(
        flops=12 * blocks.size * vectors, bytes_accessed=4 * blocks.size, transcendentals=0
    )


def start_copies(start, copies):
    def kernel(v, out):
        block = v[...]
        for i in range(copies):
            out[i] = block

    return pl.pallas_call(
        kernel, out_shape=arrays((copies,) + start.shape)[0], in_specs=[VMEM], out_specs=VMEM,
        compiler_params=PARAMS, name="start_copies",
    )(start)


def upper_products(col_ids, row_ids, count, blocks, own_cols, other_cols, row_blocks):
    ys, splits, vectors, size = own_cols.shape

    def kernel(a, b, n, u, own, other, out, both):
        both[0], both[1] = own[...], other[...]
        out[...] = jnp.zeros_like(out)
        add_products(a, b, n, u, both, out, 1, column_slot(splits), same)

    return pl.pallas_call(
        kernel,
        out_shape=arrays((row_blocks, vectors, size))[0],
        in_specs=[SMEM] * 3 + [VMEM] * 3,
        out_specs=VMEM,
        scratch_shapes=[pltpu.VMEM((2, ys, splits, vectors, size), jnp.float32)],
        compiler_params=PARAMS,
        cost_estimate=cost(blocks, vectors),
        name="upper",
    )(col_ids, row_ids, count, blocks, own_cols, other_cols)


def lower_products(row_ids, col_ids, count, blocks, row_piece, start_piece, ys, splits):
    tile, vectors, size = row_piece.shape
    with_corr = start_piece is not None
    each = splits + 1 if with_corr else splits

    def kernel(a, b, n, u, x, *rest):
        v = rest[0] if with_corr else None
        own, other, both = rest[-3:]
        both[...] = jnp.zeros_like(both)
        if with_corr:
            term = jnp.zeros((vectors, vectors), jnp.float32)
            for g in range(tile):
                term += lax.dot_general(
                    x[g], v[g], (((1,), (1,)), ((), ())), precision=HIGHEST,
                    preferred_element_type=jnp.float32,
                )
            for y in range(ys):
                both[0, y, splits, :, :vectors] = term
                both[1, y, splits, :, :vectors] = term
        add_products(a, b, n, u, x, both, 0, same, column_slot(splits))
        own[...], other[...] = both[0], both[1]

    shape = (ys, each, vectors, size)
    return pl.pallas_call(
        kernel,
        out_shape=arrays(shape, shape),
        in_specs=[SMEM] * 3 + [VMEM] * (3 if with_corr else 2),
        out_specs=(VMEM, VMEM),
        scratch_shapes=[pltpu.VMEM((2,) + shape, jnp.float32)],
        compiler_params=PARAMS,
        cost_estimate=cost(blocks, vectors),
        name="lower",
    )(row_ids, col_ids, count, blocks, row_piece, *((start_piece,) if with_corr else ()))


def add(one, two):
    def kernel(a, b, out):
        out[...] = a[...] + b[...]

    return pl.pallas_call(
        kernel, out_shape=arrays(one.shape)[0], in_specs=[VMEM] * 2, out_specs=VMEM,
        compiler_params=PARAMS, name="add",
    )(one, two)


def own_copies(row_piece, splits, copies):
    _, vectors, size = row_piece.shape

    def kernel(piece, out):
        first = lax.axis_index("col") * splits
        for s in range(splits):
            block = piece[first + s]
            for i in range(copies):
                out[i, s] = block

    return pl.pallas_call(
        kernel, out_shape=arrays((copies, splits, vectors, size))[0],
        in_specs=[VMEM], out_specs=VMEM, compiler_params=PARAMS, name="own_copies",
    )(row_piece)


def group_part(row_got, col_got, vectors, diag):
    splits = row_got.shape[1]

    def kernel(rows, cols, v, d, out):
        own = v[...] * d[...]
        mine = lax.axis_index("split")
        for s in range(splits):
            total = rows[0, s]
            for j in range(1, rows.shape[0]):
                total += rows[j, s]
            for i in range(cols.shape[0]):
                total += cols[i, s]
            total += own * jnp.where(mine == s, 1.0, 0.0).astype(jnp.float32)
            for k in range(splits):
                out[k, s] = total

    return pl.pallas_call(
        kernel, out_shape=arrays((splits,) + row_got.shape[1:])[0],
        in_specs=[VMEM] * 4, out_specs=VMEM, compiler_params=PARAMS, name="group_part",
    )(row_got, col_got, vectors, diag)


def image_copies(parts, ys, cols):
    splits, _, vectors, size = parts.shape

    def kernel(p, col_out, row_out, own):
        for s in range(splits):
            total = p[0, s]
            for k in range(1, splits):
                total += p[k, s]
            for j in range(cols):
                col_out[j, s] = total
            for i in range(ys):
                row_out[i, s] = total
        own[...] = row_out[0, lax.axis_index("split")]

    return pl.pallas_call(
        kernel,
        out_shape=arrays((cols, splits, vectors, size), (ys, splits, vectors, size), (vectors, size)),
        in_specs=[VMEM], out_specs=(VMEM,) * 3, compiler_params=PARAMS, name="image_copies",
    )(parts)


def add_to_messages(col_got, row_out):
    rows, more, vectors, size = col_got.shape
    splits = more - 1

    def kernel(got, sums, out, corr):
        out[...] = sums[...]
        first = lax.axis_index("col") * splits
        for s in range(more):
            total = got[0, s]
            for i in range(1, rows):
                total += got[i, s]
            if s < splits:
                out[first + s] += total
            else:
                corr[...] = total

    return pl.pallas_call(
        kernel, out_shape=arrays(row_out.shape, (vectors, size)),
        in_specs=[VMEM, VMEM], out_specs=(VMEM, VMEM), compiler_params=PARAMS,
        name="add_to_messages",
    )(col_got, row_out)


def subtract(corr, base, value, total):
    scaled = corr[:, : value.shape[0]] * (1.0 / total)
    return base - lax.dot_general(
        scaled, value, (((1,), (0,)), ((), ())), precision=HIGHEST,
        preferred_element_type=jnp.float32,
    )


def residual_of(corr, first, start, total):
    def kernel(c, f, v, out):
        out[...] = subtract(c[...], f[...], v[...], total)

    return pl.pallas_call(
        kernel, out_shape=arrays(first.shape)[0], in_specs=[VMEM] * 3, out_specs=VMEM,
        compiler_params=PARAMS, name="residual",
    )(corr, first, start)


def second_of(got, corr, first, diag, total):
    def kernel(g, c, f, d, out):
        value = f[...]
        image = d[...] * value
        for k in range(g.shape[0]):
            image += g[k]
        out[...] = subtract(c[...], image, value, total)

    return pl.pallas_call(
        kernel, out_shape=arrays(first.shape)[0], in_specs=[VMEM] * 4, out_specs=VMEM,
        compiler_params=PARAMS, name="second",
    )(got, corr, first, diag)


def exchange(parts, axis):
    return lax.all_to_all(parts, axis, 0, 0, tiled=True)


def swap_cores(piece):
    return lax.ppermute(piece, "core", [(0, 1), (1, 0)])


def on_device(start_vectors, diag_energy, matrix_blocks, block_rows, block_cols, counts):
    ys, cols, splits = (lax.axis_size(a) for a in ("y", "col", "split"))
    vectors, size = start_vectors.shape
    slots = matrix_blocks.shape[2]
    blocks = matrix_blocks.reshape(slots, size, size)
    row_ids = block_rows.reshape(slots)
    col_ids = block_cols.reshape(slots)
    count = counts.reshape(1)
    diag = diag_energy.reshape(1, size)
    total = size * ys * 2 * cols * splits
    plane = ("col", "split")

    start_row = exchange(start_copies(start_vectors, cols * splits), plane)
    own_cols = exchange(own_copies(start_row, splits, ys), "y")
    own, other = lower_products(row_ids, col_ids, count, blocks, start_row, None, ys, splits)
    col_got = exchange(add(own, swap_cores(other)), "y")
    upper = upper_products(
        col_ids, row_ids, count, blocks, own_cols, swap_cores(own_cols), cols * splits
    )
    row_got = exchange(upper.reshape(cols, splits, vectors, size), "col")
    parts = exchange(group_part(row_got, col_got, start_vectors, diag), "split")

    col_copies, y_copies, first = image_copies(parts, ys, cols)
    first_row = exchange(col_copies, "col").reshape(cols * splits, vectors, size)
    own_cols = exchange(y_copies, "y")
    own, other = lower_products(row_ids, col_ids, count, blocks, first_row, start_row, ys, splits)
    col_got = exchange(add(own, swap_cores(other)), "y")
    upper = upper_products(
        col_ids, row_ids, count, blocks, own_cols, swap_cores(own_cols), cols * splits
    )
    messages, corr = add_to_messages(col_got, upper)
    got = exchange(messages, plane)
    residual = residual_of(corr, first, start_vectors, total)
    return residual, second_of(got, corr, first, diag, total)


def solution(mesh):
    rows, cols, splits = mesh.devices.shape
    axes = ("y", "core", "col", "split")
    mesh = jax.sharding.Mesh(mesh.devices.reshape(rows // 2, 2, cols, splits), axes)
    row = ("y", "core")
    in_specs = (
        P(None, axes),
        P(axes),
        P(row, "col", "split", None, None),
        P(row, "col", "split"),
        P(row, "col", "split"),
        P(row, "col", "split"),
    )
    out_specs = (P(None, axes), P(None, axes))
    return jax.shard_map(
        on_device, mesh=mesh, in_specs=in_specs, out_specs=out_specs, check_vma=False
    )
```

time: 166 us -> 155 us (0.934)
  blocking collectives: 26.8 us -> 70.9 us
  waiting for transfers between devices: 70.9 us -> 31 us
  starting transfers between devices: 47.5 us -> 34.5 us
    all_to_all x7 -> x5, waiting for transfers between devices: 70.9 us -> 25.7 us  [exchange(): return lax.all_to_all(parts, axis, 0, 0, tiled=True)]
    all_to_all x2 -> x4, blocking collectives: 26.8 us -> 70.9 us  [exchange(): return lax.all_to_all(parts, axis, 0, 0, tiled=True)]
    all_to_all x7 -> x5, starting transfers between devices: 47.5 us -> 26.9 us  [exchange(): return lax.all_to_all(parts, axis, 0, 0, tiled=True)]
    ppermute x0 -> x4, starting transfers between devices: none -> 7.66 us  [swap_cores(): return lax.ppermute(piece, 'core', [(0, 1), (1, 0)])]
    ppermute x0 -> x4, waiting for transfers between devices: none -> 5.3 us  [swap_cores(): return lax.ppermute(piece, 'core', [(0, 1), (1, 0)])]
    pallas_call x5 -> x8, Pallas kernels: 11.5 us -> 10.7 us  [the longest x2 4.54 us: upper_products(): pl.pallas_call(kernel, out_shape=arrays((row_blocks, vectors, size))[0],...]
  transfers between devices with their start and end apart: 7 -> 9, of which waited for: 7 -> 9; matrix products, arithmetic and copies ran while one was open for 0% -> 0% of each run, Pallas kernels for 7% -> 7%
where the time goes in v3:
time: 155 us; the launch traced here: 154 us
  blocking collectives  70.9 us (46%)
  starting transfers between devices  34.5 us (22%)
  waiting for transfers between devices  31 us (20%)
  Pallas kernels  13.6 us (9%)
  local copies, waits for them, and re-layouts  2.08 us (1%)
    all_to_all x4, blocking collectives, exchange(): return lax.all_to_all(parts, axis, 0, 0, tiled=True)  70.9 us
    all_to_all x5, starting transfers between devices, exchange(): return lax.all_to_all(parts, axis, 0, 0, tiled=True)  26.9 us
    all_to_all x5, waiting for transfers between devices, exchange(): return lax.all_to_all(parts, axis, 0, 0, tiled=True)  25.7 us
    ppermute x4, starting transfers between devices, swap_cores(): return lax.ppermute(piece, 'core', [(0, 1), (1, 0)])  7.66 us
    ppermute x4, waiting for transfers between devices, swap_cores(): return lax.ppermute(piece, 'core', [(0, 1), (1, 0)])  5.3 us
    pallas_call x2, Pallas kernels, upper_products(): pl.pallas_call(kernel, out_shape=arrays((row_blocks, vectors, size))[0],...  4.54 us
    pallas_call x2, Pallas kernels, lower_products(): pl.pallas_call(kernel, out_shape=arrays(shape, shape), in_specs=[SMEM] *...  4.13 us
  transfers between devices with their start and end apart: 9, of which 9 were waited for; matrix products, arithmetic and copies ran while one was open for 0% of the time, Pallas kernels for 7%

profile of v3, /device:TPU:6, one launch (start us, length us, event | category | flops | bytes accessed | tf_op | source)
XLA Modules:
  0.0 153.6 jit_solution(16557740701485174622)
XLA Ops:
  0.6 0.0 copy-start
  0.6 0.0 copy-start.1
  0.7 0.8 copy-done.1
  1.4 32.9 %all_to_all.45.piece.x.rest_0_ = f32[48,8,128]{2,1,0:T(8,128)S(1)} all-to-all(f32[48,8,128]{2,1,0:T(8,128)S(1)} %start_copies.1), channel_id=1, replica_groups=mesh['y'=8,'core'=2,'col'=12,'split'=4] {'col','split'}, dimensions={0} | all-to-all | bytes 393216 | tf_op jit(solution)/shard_map/all_to_all | solution.py:242
  34.3 0.7 own_copies.1
  35.0 7.1 %all-to-all-start.1 = ((f32[8,4,8,128]{3,2,1,0:T(8,128)}), f32[8,4,8,128]{3,2,1,0:T(8,128)S(1)}, u32[]{:S(2)}, u32[]{:S(2)}) async-start(f32[8,4,8,128]{3,2,1,0:T(8,128)} %own_copies.1), calls=%async_computation.1 | async-start | bytes 262144 | tf_op jit(solution)/shard_map/all_to_all | solution.py:242
  42.7 0.0 copy-start.3
  42.7 0.0 copy-start.4
  42.7 0.0 copy-done
  42.8 0.6 copy-done.3
  43.4 0.0 copy-done.4
  43.4 1.5 lower.2
  44.9 1.9 %collective-permute-start.1 = (f32[8,4,8,128]{3,2,1,0:T(8,128)S(1)}, f32[8,4,8,128]{3,2,1,0:T(8,128)S(1)}, u32[]{:S(2)}, u32[]{:S(2)}) collective-permute-start(f32[8,4,8,128]{3,2,1,0:T(8,128)S(1)} %get-tuple-element.12), channel_id=1, source_target_pairs={{0,48},{48,0},{1,49},{49,1},{2,50},{50,2},{3,51},{51,3},{4,52},{52... | collective-permute-start | bytes 393224 | tf_op jit(solution)/shard_map/ppermute | solution.py:246
  46.8 1.3 collective-permute-done.1.b
  48.1 0.7 add.2
  48.8 2.3 %all-to-all-done.1.own = f32[8,4,8,128]{3,2,1,0:T(8,128)S(1)} async-done(((f32[8,4,8,128]{3,2,1,0:T(8,128)}), f32[8,4,8,128]{3,2,1,0:T(8,128)S(1)}, u32[]{:S(2)}, u32[]{:S(2)}) %all-to-all-start.1) | async-done | bytes 131104 | tf_op jit(solution)/shard_map/all_to_all | solution.py:242
  51.1 4.9 %all-to-all-start.3 = ((f32[8,4,8,128]{3,2,1,0:T(8,128)}), f32[8,4,8,128]{3,2,1,0:T(8,128)S(1)}, u32[]{:S(2)}, u32[]{:S(2)}) async-start(f32[8,4,8,128]{3,2,1,0:T(8,128)} %add.2), calls=%async_computation.3 | async-start | bytes 262144 | tf_op jit(solution)/shard_map/all_to_all | solution.py:242
  56.0 1.9 %collective-permute-start = (f32[8,4,8,128]{3,2,1,0:T(8,128)S(1)}, f32[8,4,8,128]{3,2,1,0:T(8,128)S(1)}, u32[]{:S(2)}, u32[]{:S(2)}) collective-permute-start(f32[8,4,8,128]{3,2,1,0:T(8,128)S(1)} %all-to-all-done.1.own), channel_id=1, source_target_pairs={{0,48},{48,0},{1,49},{49,1},{2,50},{50,2},{3,51},{51,3},{4,52},{52... | collective-permute-start | bytes 393224 | tf_op jit(solution)/shard_map/ppermute | solution.py:246
  57.9 1.3 collective-permute-done.other
  59.2 2.3 %upper.2 = f32[48,8,128]{2,1,0:T(8,128)S(1)} custom-call(s32[16]{0:T(128)S(1)} %bitcast.22, s32[16]{0:T(128)S(1)} %bitcast.18, s32[1]{0:T(128)} %bitcast.7.n, f32[16,128,128]{2,1,0:T(8,128)S(1)} %bitcast.12, f32[8,4,8,128]{3,2,1,0:T(8,128)S(1)} %all-to-all-done.1.own, f32[8,4,8,128]{3,2,1,0:T(8,128)S(1)} %collective-permute-done.other), custom_call_target="tpu_custom_call" | custom-call | flops 25165824 | bytes 1048576 | tf_op jit(solution)/shard_map/upper/pallas_call | solution.py:70
  61.5 3.9 %all-to-all-done.3.cols = f32[8,4,8,128]{3,2,1,0:T(8,128)S(1)} async-done(((f32[8,4,8,128]{3,2,1,0:T(8,128)}), f32[8,4,8,128]{3,2,1,0:T(8,128)S(1)}, u32[]{:S(2)}, u32[]{:S(2)}) %all-to-all-start.3) | async-done | bytes 131104 | tf_op jit(solution)/shard_map/all_to_all | solution.py:242
  65.4 0.0 copy-start.2
  65.4 11.1 %all_to_all.46.rows = f32[12,4,8,128]{3,2,1,0:T(8,128)S(1)} all-to-all(f32[12,4,8,128]{3,2,1,0:T(8,128)S(1)} %bitcast.16), channel_id=1, replica_groups=mesh['y'=8,'core'=2,'col'=12,'split'=4] {'col'}, dimensions={0} | all-to-all | bytes 393216 | tf_op jit(solution)/shard_map/all_to_all | solution.py:242
  76.5 0.0 copy-start.5
  76.5 0.0 copy-done.2
  76.5 0.7 copy-done.5
  77.2 16.3 %all_to_all.47.p = f32[4,4,8,128]{3,2,1,0:T(8,128)S(1)} all-to-all(f32[4,4,8,128]{3,2,1,0:T(8,128)S(1)} %group_part.1), channel_id=1, replica_groups=mesh['y'=8,'core'=2,'col'=12,'split'=4] {'split'}, dimensions={0} | all-to-all | bytes 131072 | tf_op jit(solution)/shard_map/all_to_all | solution.py:242
  93.5 0.7 image_copies.1
  94.1 10.7 %all_to_all.48 = f32[12,4,8,128]{3,2,1,0:T(8,128)S(1)} all-to-all(f32[12,4,8,128]{3,2,1,0:T(8,128)S(1)} %get-tuple-element.13), channel_id=1, replica_groups=mesh['y'=8,'core'=2,'col'=12,'split'=4] {'col'}, dimensions={0} | all-to-all | bytes 393216 | tf_op jit(solution)/shard_map/all_to_all | solution.py:242
  104.9 3.7 %all-to-all-start.7 = ((f32[8,4,8,128]{3,2,1,0:T(8,128)}), f32[8,4,8,128]{3,2,1,0:T(8,128)S(1)}, u32[]{:S(2)}, u32[]{:S(2)}) async-start(f32[8,4,8,128]{3,2,1,0:T(8,128)} %get-tuple-element.16), calls=%async_computation.7 | async-start | bytes 262144 | tf_op jit(solution)/shard_map/all_to_all | solution.py:242
  108.5 2.6 %lower.3 = (f32[8,5,8,128]{3,2,1,0:T(8,128)S(1)}, f32[8,5,8,128]{3,2,1,0:T(8,128)S(1)}) custom-call(s32[16]{0:T(128)S(1)} %bitcast.19, s32[16]{0:T(128)S(1)} %bitcast.23, s32[1]{0:T(128)} %bitcast.9.n, f32[16,128,128]{2,1,0:T(8,128)S(1)} %bitcast.13, f32[48,8,128]{2,1,0:T(8,128)S(1)} %bitcast.15, f32[48,8,128]{2,1,0:T(8,128)S(1)} %all_to_all.45.piece.x.rest_0_), custom_call_target="tpu_custom_call" | custom-call | flops 25165824 | bytes 1048576 | tf_op jit(solution)/shard_map/lower/pallas_call | solution.py:105
  111.2 1.9 %collective-permute-start.2 = (f32[8,5,8,128]{3,2,1,0:T(8,128)S(1)}, f32[8,5,8,128]{3,2,1,0:T(8,128)S(1)}, u32[]{:S(2)}, u32[]{:S(2)}) collective-permute-start(f32[8,5,8,128]{3,2,1,0:T(8,128)S(1)} %get-tuple-element.15), channel_id=1, source_target_pairs={{0,48},{48,0},{1,49},{49,1},{2,50},{50,2},{3,51},{51,3},{4,52},{52... | collective-permute-start | bytes 491528 | tf_op jit(solution)/shard_map/ppermute | solution.py:246
  113.1 1.4 collective-permute-done.2.b
  114.4 0.7 add.3
  115.1 2.5 %all-to-all-done.7.own = f32[8,4,8,128]{3,2,1,0:T(8,128)S(1)} async-done(((f32[8,4,8,128]{3,2,1,0:T(8,128)}), f32[8,4,8,128]{3,2,1,0:T(8,128)S(1)}, u32[]{:S(2)}, u32[]{:S(2)}) %all-to-all-start.7) | async-done | bytes 131104 | tf_op jit(solution)/shard_map/all_to_all | solution.py:242
  117.6 4.7 %all-to-all-start.6 = ((f32[8,5,8,128]{3,2,1,0:T(8,128)}), f32[8,5,8,128]{3,2,1,0:T(8,128)S(1)}, u32[]{:S(2)}, u32[]{:S(2)}) async-start(f32[8,5,8,128]{3,2,1,0:T(8,128)} %add.3), calls=%async_computation.6 | async-start | bytes 327680 | tf_op jit(solution)/shard_map/all_to_all | solution.py:242
  122.3 1.9 %collective-permute-start.3 = (f32[8,4,8,128]{3,2,1,0:T(8,128)S(1)}, f32[8,4,8,128]{3,2,1,0:T(8,128)S(1)}, u32[]{:S(2)}, u32[]{:S(2)}) collective-permute-start(f32[8,4,8,128]{3,2,1,0:T(8,128)S(1)} %all-to-all-done.7.own), channel_id=1, source_target_pairs={{0,48},{48,0},{1,49},{49,1},{2,50},{50,2},{3,51},{51,3},{4,52},{52... | collective-permute-start | bytes 393224 | tf_op jit(solution)/shard_map/ppermute | solution.py:246
  124.2 1.3 collective-permute-done.3.other
  125.6 2.3 %upper.3.sums = f32[48,8,128]{2,1,0:T(8,128)S(1)} custom-call(s32[16]{0:T(128)S(1)} %bitcast.24, s32[16]{0:T(128)S(1)} %bitcast.20, s32[1]{0:T(128)} %bitcast.10.n, f32[16,128,128]{2,1,0:T(8,128)S(1)} %bitcast.14, f32[8,4,8,128]{3,2,1,0:T(8,128)S(1)} %all-to-all-done.7.own, f32[8,4,8,128]{3,2,1,0:T(8,128)S(1)} %collective-permute-done.3.other), custom_call_target="tpu_custom_call" | custom-call | flops 25165824 | bytes 1048576 | tf_op jit(solution)/shard_map/upper/pallas_call | solution.py:70
  127.8 4.6 %all-to-all-done.6.got = f32[8,5,8,128]{3,2,1,0:T(8,128)S(1)} async-done(((f32[8,5,8,128]{3,2,1,0:T(8,128)}), f32[8,5,8,128]{3,2,1,0:T(8,128)S(1)}, u32[]{:S(2)}, u32[]{:S(2)}) %all-to-all-start.6) | async-done | bytes 163872 | tf_op jit(solution)/shard_map/all_to_all | solution.py:242
  132.4 0.7 add_to_messages.1
  133.1 6.5 %all-to-all-start.8 = ((f32[48,8,128]{2,1,0:T(8,128)}), f32[48,8,128]{2,1,0:T(8,128)S(1)}, u32[]{:S(2)}, u32[]{:S(2)}) async-start(f32[48,8,128]{2,1,0:T(8,128)} %get-tuple-element.19), calls=%async_computation.8 | async-start | bytes 393216 | tf_op jit(solution)/shard_map/all_to_all | solution.py:242
  139.6 0.7 residual.1
  140.4 12.5 %all-to-all-done.8.g = f32[48,8,128]{2,1,0:T(8,128)S(1)} async-done(((f32[48,8,128]{2,1,0:T(8,128)}), f32[48,8,128]{2,1,0:T(8,128)S(1)}, u32[]{:S(2)}, u32[]{:S(2)}) %all-to-all-start.8) | async-done | bytes 196640 | tf_op jit(solution)/shard_map/all_to_all | solution.py:242
  152.8 0.7 second.1
  (2 shorter events, 0.0 us)
Async XLA Ops:
  0.6 42.1 %copy-start = (f32[1,1,16,128,128]{4,3,2,1,0:T(8,128)S(1)}, f32[1,1,16,128,128]{4,3,2,1,0:T(8,128)}, u32[]{:S(2)}) copy-start(f32[1,1,16,128,128]{4,3,2,1,0:T(8,128)} %param.8) | copy-start | bytes 3145732
  0.6 0.8 copy-start.1
  35.0 16.2 %all-to-all-start.1 = ((f32[8,4,8,128]{3,2,1,0:T(8,128)}), f32[8,4,8,128]{3,2,1,0:T(8,128)S(1)}, u32[]{:S(2)}, u32[]{:S(2)}) async-start(f32[8,4,8,128]{3,2,1,0:T(8,128)} %own_copies.1), calls=%async_computation.1 | async-start | bytes 262144 | tf_op jit(solution)/shard_map/all_to_all | solution.py:242
  42.7 0.7 copy-start.3
  42.7 0.7 copy-start.4
  44.9 3.2 %collective-permute-start.1 = (f32[8,4,8,128]{3,2,1,0:T(8,128)S(1)}, f32[8,4,8,128]{3,2,1,0:T(8,128)S(1)}, u32[]{:S(2)}, u32[]{:S(2)}) collective-permute-start(f32[8,4,8,128]{3,2,1,0:T(8,128)S(1)} %get-tuple-element.12), channel_id=1, source_target_pairs={{0,48},{48,0},{1,49},{49,1},{2,50},{50,2},{3,51},{51,3},{4,52},{52... | collective-permute-start | bytes 393224 | tf_op jit(solution)/shard_map/ppermute | solution.py:246
  51.1 14.3 %all-to-all-start.3 = ((f32[8,4,8,128]{3,2,1,0:T(8,128)}), f32[8,4,8,128]{3,2,1,0:T(8,128)S(1)}, u32[]{:S(2)}, u32[]{:S(2)}) async-start(f32[8,4,8,128]{3,2,1,0:T(8,128)} %add.2), calls=%async_computation.3 | async-start | bytes 262144 | tf_op jit(solution)/shard_map/all_to_all | solution.py:242
  56.0 3.2 %collective-permute-start = (f32[8,4,8,128]{3,2,1,0:T(8,128)S(1)}, f32[8,4,8,128]{3,2,1,0:T(8,128)S(1)}, u32[]{:S(2)}, u32[]{:S(2)}) collective-permute-start(f32[8,4,8,128]{3,2,1,0:T(8,128)S(1)} %all-to-all-done.1.own), channel_id=1, source_target_pairs={{0,48},{48,0},{1,49},{49,1},{2,50},{50,2},{3,51},{51,3},{4,52},{52... | collective-permute-start | bytes 393224 | tf_op jit(solution)/shard_map/ppermute | solution.py:246
  65.4 11.1 %copy-start.2 = (f32[8,128]{1,0:T(8,128)S(1)}, f32[8,128]{1,0:T(8,128)}, u32[]{:S(2)}) copy-start(f32[8,128]{1,0:T(8,128)} %v.5) | copy-start | bytes 12292
  76.5 0.7 copy-start.5
  104.9 12.7 %all-to-all-start.7 = ((f32[8,4,8,128]{3,2,1,0:T(8,128)}), f32[8,4,8,128]{3,2,1,0:T(8,128)S(1)}, u32[]{:S(2)}, u32[]{:S(2)}) async-start(f32[8,4,8,128]{3,2,1,0:T(8,128)} %get-tuple-element.16), calls=%async_computation.7 | async-start | bytes 262144 | tf_op jit(solution)/shard_map/all_to_all | solution.py:242
  111.2 3.3 %collective-permute-start.2 = (f32[8,5,8,128]{3,2,1,0:T(8,128)S(1)}, f32[8,5,8,128]{3,2,1,0:T(8,128)S(1)}, u32[]{:S(2)}, u32[]{:S(2)}) collective-permute-start(f32[8,5,8,128]{3,2,1,0:T(8,128)S(1)} %get-tuple-element.15), channel_id=1, source_target_pairs={{0,48},{48,0},{1,49},{49,1},{2,50},{50,2},{3,51},{51,3},{4,52},{52... | collective-permute-start | bytes 491528 | tf_op jit(solution)/shard_map/ppermute | solution.py:246
  117.6 14.8 %all-to-all-start.6 = ((f32[8,5,8,128]{3,2,1,0:T(8,128)}), f32[8,5,8,128]{3,2,1,0:T(8,128)S(1)}, u32[]{:S(2)}, u32[]{:S(2)}) async-start(f32[8,5,8,128]{3,2,1,0:T(8,128)} %add.3), calls=%async_computation.6 | async-start | bytes 327680 | tf_op jit(solution)/shard_map/all_to_all | solution.py:242
  122.3 3.2 %collective-permute-start.3 = (f32[8,4,8,128]{3,2,1,0:T(8,128)S(1)}, f32[8,4,8,128]{3,2,1,0:T(8,128)S(1)}, u32[]{:S(2)}, u32[]{:S(2)}) collective-permute-start(f32[8,4,8,128]{3,2,1,0:T(8,128)S(1)} %all-to-all-done.7.own), channel_id=1, source_target_pairs={{0,48},{48,0},{1,49},{49,1},{2,50},{50,2},{3,51},{51,3},{4,52},{52... | collective-permute-start | bytes 393224 | tf_op jit(solution)/shard_map/ppermute | solution.py:246
  133.1 19.7 %all-to-all-start.8 = ((f32[48,8,128]{2,1,0:T(8,128)}), f32[48,8,128]{2,1,0:T(8,128)S(1)}, u32[]{:S(2)}, u32[]{:S(2)}) async-start(f32[48,8,128]{2,1,0:T(8,128)} %get-tuple-element.19), calls=%async_computation.8 | async-start | bytes 393216 | tf_op jit(solution)/shard_map/all_to_all | solution.py:242

commit v4 on v3

v4 whole, which is shorter than its diff:
```python
import jax
import jax.numpy as jnp
from jax import lax
from jax.experimental import pallas as pl
from jax.experimental.pallas import tpu as pltpu
from jax.sharding import PartitionSpec as P

HIGHEST = lax.Precision.HIGHEST
SMEM = pl.BlockSpec(memory_space=pltpu.SMEM)
VMEM = pl.BlockSpec(memory_space=pltpu.VMEM)
PARAMS = pltpu.CompilerParams(vmem_limit_bytes=16 << 20)


def arrays(*shapes):
    return tuple(jax.ShapeDtypeStruct(s, jnp.float32) for s in shapes)


def add_products(ids_from, ids_to, used, u_ref, in_ref, out_ref, block_dim, from_slot, to_slot):
    for t in range(u_ref.shape[0]):
        term = lax.dot_general(
            in_ref[from_slot(ids_from[t])], u_ref[t], (((1,), (block_dim,)), ((), ())),
            precision=HIGHEST, preferred_element_type=jnp.float32,
        )
        keep = jnp.where(t < used[0], 1.0, 0.0).astype(jnp.float32)
        out_ref[to_slot(ids_to[t])] += term * keep


def same(block):
    return block


def column_slot(splits):
    core = lax.axis_index("core")

    def slot(c):
        row, s = lax.div(c, jnp.int32(splits)), lax.rem(c, jnp.int32(splits))
        y, its_core = lax.div(row, jnp.int32(2)), lax.rem(row, jnp.int32(2))
        return y, jnp.where(its_core == core, 0, splits) + s

    return slot


def cost(blocks, vectors):
    return pl.CostEstimate(
        flops=12 * blocks.size * vectors, bytes_accessed=4 * blocks.size, transcendentals=0
    )


def start_copies(start, copies):
    def kernel(v, out):
        block = v[...]
        for i in range(copies):
            out[i] = block

    return pl.pallas_call(
        kernel, out_shape=arrays((copies,) + start.shape)[0], in_specs=[VMEM], out_specs=VMEM,
        compiler_params=PARAMS, name="start_copies",
    )(start)


def upper_products(col_ids, row_ids, count, blocks, col_pieces, row_blocks, splits):
    ys, _, vectors, size = col_pieces[0].shape
    parts = len(col_pieces)
    each = 2 * splits // parts

    def kernel(a, b, n, u, *rest):
        pieces, out = rest[:parts], rest[parts]
        both = pieces[0]
        if parts > 1:
            both = rest[-1]
            for k in range(parts):
                both[:, k * each : (k + 1) * each] = pieces[k][...]
        out[...] = jnp.zeros_like(out)
        add_products(a, b, n, u, both, out, 1, column_slot(splits), same)

    scratch = pltpu.VMEM((ys, 2 * splits, vectors, size), jnp.float32)
    return pl.pallas_call(
        kernel,
        out_shape=arrays((row_blocks, vectors, size))[0],
        in_specs=[SMEM] * 3 + [VMEM] * (1 + parts),
        out_specs=VMEM,
        scratch_shapes=[scratch] if parts > 1 else [],
        compiler_params=PARAMS,
        cost_estimate=cost(blocks, vectors),
        name="upper",
    )(col_ids, row_ids, count, blocks, *col_pieces)


def lower_products(row_ids, col_ids, count, blocks, row_piece, ys, splits):
    _, vectors, size = row_piece.shape

    def kernel(a, b, n, u, x, out):
        out[...] = jnp.zeros_like(out)
        add_products(a, b, n, u, x, out, 0, same, column_slot(splits))

    return pl.pallas_call(
        kernel,
        out_shape=arrays((ys, 2 * splits, vectors, size))[0],
        in_specs=[SMEM] * 3 + [VMEM] * 2,
        out_specs=VMEM,
        compiler_params=PARAMS,
        cost_estimate=cost(blocks, vectors),
        name="lower",
    )(row_ids, col_ids, count, blocks, row_piece)


def lower_and_correlation(row_ids, col_ids, count, blocks, row_piece, start_piece, ys, splits):
    tile, vectors, size = row_piece.shape

    def kernel(a, b, n, u, x, v, own, other, both):
        both[...] = jnp.zeros_like(both)
        add_products(a, b, n, u, x, both, 0, same, column_slot(splits))
        term = jnp.zeros((vectors, vectors), jnp.float32)
        for g in range(tile):
            term += lax.dot_general(
                x[g], v[g], (((1,), (1,)), ((), ())), precision=HIGHEST,
                preferred_element_type=jnp.float32,
            )
        for k, out in enumerate((own, other)):
            out[:, :splits] = both[:, k * splits : (k + 1) * splits]
            out[:, splits] = jnp.zeros((ys, vectors, size), jnp.float32)
            for y in range(ys):
                out[y, splits, :, :vectors] = term

    shape = (ys, splits + 1, vectors, size)
    return pl.pallas_call(
        kernel,
        out_shape=arrays(shape, shape),
        in_specs=[SMEM] * 3 + [VMEM] * 3,
        out_specs=(VMEM, VMEM),
        scratch_shapes=[pltpu.VMEM((ys, 2 * splits, vectors, size), jnp.float32)],
        compiler_params=PARAMS,
        cost_estimate=cost(blocks, vectors),
        name="lower_and_correlation",
    )(row_ids, col_ids, count, blocks, row_piece, start_piece)


def column_sums(col_got, splits):
    ys, _, vectors, size = col_got.shape

    def kernel(got, own, other):
        for k, out in enumerate((own, other)):
            for s in range(splits):
                total = got[0, k * splits + s]
                for y in range(1, ys):
                    total += got[y, k * splits + s]
                out[s] = total

    shape = (splits, vectors, size)
    return pl.pallas_call(
        kernel, out_shape=arrays(shape, shape), in_specs=[VMEM], out_specs=(VMEM, VMEM),
        compiler_params=PARAMS, name="column_sums",
    )(col_got)


def add(one, two):
    def kernel(a, b, out):
        out[...] = a[...] + b[...]

    return pl.pallas_call(
        kernel, out_shape=arrays(one.shape)[0], in_specs=[VMEM] * 2, out_specs=VMEM,
        compiler_params=PARAMS, name="add",
    )(one, two)


def own_copies(row_piece, diag, splits, copies):
    _, vectors, size = row_piece.shape

    def kernel(piece, d, out, scaled):
        first = lax.axis_index("col") * splits
        for s in range(splits):
            block = piece[first + s]
            for i in range(copies):
                out[i, s] = block
        scaled[...] = piece[first + lax.axis_index("split")] * d[...]

    return pl.pallas_call(
        kernel, out_shape=arrays((copies, splits, vectors, size), (vectors, size)),
        in_specs=[VMEM] * 2, out_specs=(VMEM,) * 2, compiler_params=PARAMS, name="own_copies",
    )(row_piece, diag)


def group_part(row_got, own_sum, other_sum, scaled):
    splits = row_got.shape[1]

    def kernel(rows, one, two, own, out):
        mine = lax.axis_index("split")
        for s in range(splits):
            total = one[s] + two[s]
            for j in range(rows.shape[0]):
                total += rows[j, s]
            total += own[...] * jnp.where(mine == s, 1.0, 0.0).astype(jnp.float32)
            for k in range(splits):
                out[k, s] = total

    return pl.pallas_call(
        kernel, out_shape=arrays((splits,) + row_got.shape[1:])[0],
        in_specs=[VMEM] * 4, out_specs=VMEM, compiler_params=PARAMS, name="group_part",
    )(row_got, own_sum, other_sum, scaled)


def image_copies(parts, cols):
    splits, _, vectors, size = parts.shape

    def kernel(p, col_out, image, own):
        for s in range(splits):
            total = p[0, s]
            for k in range(1, splits):
                total += p[k, s]
            image[s] = total
            for j in range(cols):
                col_out[j, s] = total
        own[...] = image[lax.axis_index("split")]

    group = (splits, vectors, size)
    return pl.pallas_call(
        kernel, out_shape=arrays((cols,) + group, group, (vectors, size)),
        in_specs=[VMEM], out_specs=(VMEM,) * 3, compiler_params=PARAMS, name="image_copies",
    )(parts)


def y_copies(own, other, ys):
    splits, vectors, size = own.shape

    def kernel(one, two, out):
        for y in range(ys):
            out[y, :splits] = one[...]
            out[y, splits:] = two[...]

    return pl.pallas_call(
        kernel, out_shape=arrays((ys, 2 * splits, vectors, size))[0], in_specs=[VMEM] * 2,
        out_specs=VMEM, compiler_params=PARAMS, name="y_copies",
    )(own, other)


def add_to_messages(col_got, row_out):
    rows, more, vectors, size = col_got.shape
    splits = more - 1

    def kernel(got, sums, out, corr):
        out[...] = sums[...]
        first = lax.axis_index("col") * splits
        for s in range(more):
            total = got[0, s]
            for i in range(1, rows):
                total += got[i, s]
            if s < splits:
                out[first + s] += total
            else:
                corr[...] = total

    return pl.pallas_call(
        kernel, out_shape=arrays(row_out.shape, (vectors, size)),
        in_specs=[VMEM, VMEM], out_specs=(VMEM, VMEM), compiler_params=PARAMS,
        name="add_to_messages",
    )(col_got, row_out)


def subtract(corr, base, value, total):
    scaled = corr[:, : value.shape[0]] * (1.0 / total)
    return base - lax.dot_general(
        scaled, value, (((1,), (0,)), ((), ())), precision=HIGHEST,
        preferred_element_type=jnp.float32,
    )


def results(got, corr, first, start, diag, total):
    def kernel(g, c, f, v, d, residual, second):
        value = f[...]
        image = d[...] * value
        for k in range(g.shape[0]):
            image += g[k]
        residual[...] = subtract(c[...], value, v[...], total)
        second[...] = subtract(c[...], image, value, total)

    return pl.pallas_call(
        kernel, out_shape=arrays(first.shape, first.shape), in_specs=[VMEM] * 5,
        out_specs=(VMEM, VMEM), compiler_params=PARAMS, name="results",
    )(got, corr, first, start, diag)


def exchange(parts, axis):
    return lax.all_to_all(parts, axis, 0, 0, tiled=True)


def swap_cores(piece):
    return lax.ppermute(piece, "core", [(0, 1), (1, 0)])


def on_device(start_vectors, diag_energy, matrix_blocks, block_rows, block_cols, counts):
    ys, cols, splits = (lax.axis_size(a) for a in ("y", "col", "split"))
    vectors, size = start_vectors.shape
    slots = matrix_blocks.shape[2]
    blocks = matrix_blocks.reshape(slots, size, size)
    row_ids = block_rows.reshape(slots)
    col_ids = block_cols.reshape(slots)
    count = counts.reshape(1)
    diag = diag_energy.reshape(1, size)
    total = size * ys * 2 * cols * splits
    plane = ("col", "split")

    start_row = exchange(start_copies(start_vectors, cols * splits), plane)
    copies, scaled = own_copies(start_row, diag, splits, ys)
    own_cols = exchange(copies, "y")
    lower = lower_products(row_ids, col_ids, count, blocks, start_row, ys, splits)
    col_got = exchange(lower, "y")
    upper = upper_products(
        col_ids, row_ids, count, blocks, (own_cols, swap_cores(own_cols)), cols * splits, splits
    )
    row_got = exchange(upper.reshape(cols, splits, vectors, size), "col")
    own_sum, other_sum = column_sums(col_got, splits)
    parts = exchange(group_part(row_got, own_sum, swap_cores(other_sum), scaled), "split")

    col_copies, image, first = image_copies(parts, cols)
    first_row = exchange(col_copies, "col").reshape(cols * splits, vectors, size)
    both_cols = exchange(y_copies(image, swap_cores(image), ys), "y")
    own, other = lower_and_correlation(
        row_ids, col_ids, count, blocks, first_row, start_row, ys, splits
    )
    col_got = exchange(add(own, swap_cores(other)), "y")
    upper = upper_products(col_ids, row_ids, count, blocks, (both_cols,), cols * splits, splits)
    messages, corr = add_to_messages(col_got, upper)
    got = exchange(messages, plane)
    return results(got, corr, first, start_vectors, diag, total)


def solution(mesh):
    rows, cols, splits = mesh.devices.shape
    axes = ("y", "core", "col", "split")
    mesh = jax.sharding.Mesh(mesh.devices.reshape(rows // 2, 2, cols, splits), axes)
    row = ("y", "core")
    in_specs = (
        P(None, axes),
        P(axes),
        P(row, "col", "split", None, None),
        P(row, "col", "split"),
        P(row, "col", "split"),
        P(row, "col", "split"),
    )
    out_specs = (P(None, axes), P(None, axes))
    return jax.shard_map(
        on_device, mesh=mesh, in_specs=in_specs, out_specs=out_specs, check_vma=False
    )
```

time: 155 us -> 156 us (level)
    all_to_all x5 -> x6, waiting for transfers between devices: 25.7 us -> 27.3 us  [exchange(): return lax.all_to_all(parts, axis, 0, 0, tiled=True)]
    pallas_call x6 -> x7, Pallas kernels: 6.94 us -> 7.59 us  [the longest x1 2.59 us: lower_and_correlation(): pl.pallas_call(kernel, out_shape=arrays(shape, shape), in_specs=[SMEM] *...]
    all_to_all x4 -> x3, blocking collectives: 70.9 us -> 71.1 us  [exchange(): return lax.all_to_all(parts, axis, 0, 0, tiled=True)]
    all_to_all x5 -> x6, starting transfers between devices: 26.9 us -> 26.8 us  [exchange(): return lax.all_to_all(parts, axis, 0, 0, tiled=True)]
  transfers between devices with their start and end apart: 9 -> 10, of which waited for: 9 -> 10; matrix products, arithmetic and copies ran while one was open for 0% -> 0% of each run, Pallas kernels for 7% -> 7%
where the time goes in v4:
time: 156 us; the launch traced here: 155 us
  blocking collectives  71.1 us (46%)
  starting transfers between devices  34.5 us (22%)
  waiting for transfers between devices  32.3 us (21%)
  Pallas kernels  13.5 us (9%)
  local copies, waits for them, and re-layouts  2.65 us (2%)
    all_to_all x3, blocking collectives, exchange(): return lax.all_to_all(parts, axis, 0, 0, tiled=True)  71.1 us
    all_to_all x6, waiting for transfers between devices, exchange(): return lax.all_to_all(parts, axis, 0, 0, tiled=True)  27.3 us
    all_to_all x6, starting transfers between devices, exchange(): return lax.all_to_all(parts, axis, 0, 0, tiled=True)  26.8 us
    ppermute x4, starting transfers between devices, swap_cores(): return lax.ppermute(piece, 'core', [(0, 1), (1, 0)])  7.68 us
    pallas_call x2, Pallas kernels, upper_products(): pl.pallas_call(kernel, out_shape=arrays((row_blocks, vectors, size))[0],...  5.22 us
    ppermute x4, waiting for transfers between devices, swap_cores(): return lax.ppermute(piece, 'core', [(0, 1), (1, 0)])  4.97 us
  transfers between devices with their start and end apart: 10, of which 10 were waited for; matrix products, arithmetic and copies ran while one was open for 0% of the time, Pallas kernels for 7%

profile of v4, /device:TPU:6, one launch (start us, length us, event | category | flops | bytes accessed | tf_op | source)
XLA Modules:
  0.0 155.4 jit_solution(17110522820176617361)
XLA Ops:
  0.6 0.0 copy-start.1
  0.6 0.7 copy-done.1
  1.3 0.0 copy-start
  1.3 33.0 %all_to_all.45.piece.x.v = f32[48,8,128]{2,1,0:T(8,128)S(1)} all-to-all(f32[48,8,128]{2,1,0:T(8,128)S(1)} %start_copies.1), channel_id=1, replica_groups=mesh['y'=8,'core'=2,'col'=12,'split'=4] {'col','split'}, dimensions={0} | all-to-all | bytes 393216 | tf_op jit(solution)/shard_map/all_to_all | solution.py:283
  34.3 0.0 copy-start.5
  34.3 0.7 copy-done.5
  35.0 0.7 own_copies.1
  35.7 7.1 %all-to-all-start.1 = ((f32[8,4,8,128]{3,2,1,0:T(8,128)}), f32[8,4,8,128]{3,2,1,0:T(8,128)S(1)}, u32[]{:S(2)}, u32[]{:S(2)}) async-start(f32[8,4,8,128]{3,2,1,0:T(8,128)} %get-tuple-element.13), calls=%async_computation.1 | async-start | bytes 262144 | tf_op jit(solution)/shard_map/all_to_all | solution.py:283
  43.4 0.0 copy-start.3
  43.4 0.0 copy-start.4
  43.4 0.0 copy-done
  43.4 0.6 copy-done.3
  44.1 0.0 copy-done.4
  44.1 2.2 %lower.1 = f32[8,8,8,128]{3,2,1,0:T(8,128)} custom-call(s32[16]{0:T(128)S(1)} %bitcast.16, s32[16]{0:T(128)S(1)} %bitcast.20, s32[1]{0:T(128)} %bitcast.8.n, f32[16,128,128]{2,1,0:T(8,128)S(1)} %bitcast.11, f32[48,8,128]{2,1,0:T(8,128)S(1)} %all_to_all.45.piece.x.v), custom_call_target="tpu_custom_call" | custom-call | flops 25165824 | bytes 1048576 | tf_op jit(solution)/shard_map/lower/pallas_call | solution.py:96
  46.3 5.6 %all-to-all-done.1.rest_0_ = f32[8,4,8,128]{3,2,1,0:T(8,128)S(1)} async-done(((f32[8,4,8,128]{3,2,1,0:T(8,128)}), f32[8,4,8,128]{3,2,1,0:T(8,128)S(1)}, u32[]{:S(2)}, u32[]{:S(2)}) %all-to-all-start.1) | async-done | bytes 131104 | tf_op jit(solution)/shard_map/all_to_all | solution.py:283
  51.8 3.4 %all-to-all-start.3 = ((f32[8,8,8,128]{3,2,1,0:T(8,128)}), f32[8,8,8,128]{3,2,1,0:T(8,128)S(1)}, u32[]{:S(2)}, u32[]{:S(2)}) async-start(f32[8,8,8,128]{3,2,1,0:T(8,128)} %lower.1), calls=%async_computation.3 | async-start | bytes 524288 | tf_op jit(solution)/shard_map/all_to_all | solution.py:283
  55.3 1.9 %collective-permute-start = (f32[8,4,8,128]{3,2,1,0:T(8,128)S(1)}, f32[8,4,8,128]{3,2,1,0:T(8,128)S(1)}, u32[]{:S(2)}, u32[]{:S(2)}) collective-permute-start(f32[8,4,8,128]{3,2,1,0:T(8,128)S(1)} %all-to-all-done.1.rest_0_), channel_id=1, source_target_pairs={{0,48},{48,0},{1,49},{49,1},{2,50},{50,2},{3,51},{51,3},{4,52},{52... | collective-permute-start | bytes 393224 | tf_op jit(solution)/shard_map/ppermute | solution.py:287
  57.2 1.3 collective-permute-done.rest_1_
  58.5 3.0 %upper.2 = f32[48,8,128]{2,1,0:T(8,128)} custom-call(s32[16]{0:T(128)S(1)} %bitcast.21, s32[16]{0:T(128)S(1)} %bitcast.17, s32[1]{0:T(128)} %bitcast.7.n, f32[16,128,128]{2,1,0:T(8,128)S(1)} %bitcast.12, f32[8,4,8,128]{3,2,1,0:T(8,128)S(1)} %all-to-all-done.1.rest_0_, f32[8,4,8,128]{3,2,1,0:T(8,128)S(1)} %collective-permute-done.rest_1_), custom_call_target="tpu_custom_call" | custom-call | flops 25165824 | bytes 1048576 | tf_op jit(solution)/shard_map/upper/pallas_call | solution.py:77
  61.5 4.2 %all-to-all-done.3.got = f32[8,8,8,128]{3,2,1,0:T(8,128)S(1)} async-done(((f32[8,8,8,128]{3,2,1,0:T(8,128)}), f32[8,8,8,128]{3,2,1,0:T(8,128)S(1)}, u32[]{:S(2)}, u32[]{:S(2)}) %all-to-all-start.3) | async-done | bytes 262176 | tf_op jit(solution)/shard_map/all_to_all | solution.py:283
  65.6 4.8 %all-to-all-start.2 = ((f32[12,4,8,128]{3,2,1,0:T(8,128)}), f32[12,4,8,128]{3,2,1,0:T(8,128)S(1)}, u32[]{:S(2)}, u32[]{:S(2)}) async-start(f32[12,4,8,128]{3,2,1,0:T(8,128)} %bitcast.5), calls=%async_computation.2 | async-start | bytes 393216 | tf_op jit(solution)/shard_map/all_to_all | solution.py:283
  70.4 1.9 %collective-permute-start.1 = (f32[4,8,128]{2,1,0:T(8,128)S(1)}, f32[4,8,128]{2,1,0:T(8,128)S(1)}, u32[]{:S(2)}, u32[]{:S(2)}) collective-permute-start(f32[4,8,128]{2,1,0:T(8,128)S(1)} %get-tuple-element.15), channel_id=1, source_target_pairs={{0,48},{48,0},{1,49},{49,1},{2,50},{50,2},{3,51},{51,3},{4,52},{52... | collective-permute-start | bytes 49160 | tf_op jit(solution)/shard_map/ppermute | solution.py:287
  72.4 1.1 collective-permute-done.1.two
  73.5 3.3 %all-to-all-done.2.rows = f32[12,4,8,128]{3,2,1,0:T(8,128)S(1)} async-done(((f32[12,4,8,128]{3,2,1,0:T(8,128)}), f32[12,4,8,128]{3,2,1,0:T(8,128)S(1)}, u32[]{:S(2)}, u32[]{:S(2)}) %all-to-all-start.2) | async-done | bytes 196640 | tf_op jit(solution)/shard_map/all_to_all | solution.py:283
  76.9 16.3 %all_to_all.46.p = f32[4,4,8,128]{3,2,1,0:T(8,128)S(1)} all-to-all(f32[4,4,8,128]{3,2,1,0:T(8,128)S(1)} %group_part.1), channel_id=1, replica_groups=mesh['y'=8,'core'=2,'col'=12,'split'=4] {'split'}, dimensions={0} | all-to-all | bytes 131072 | tf_op jit(solution)/shard_map/all_to_all | solution.py:283
  93.1 0.7 image_copies.1
  93.8 4.8 %all-to-all-start.5 = ((f32[12,4,8,128]{3,2,1,0:T(8,128)}), f32[12,4,8,128]{3,2,1,0:T(8,128)S(1)}, u32[]{:S(2)}, u32[]{:S(2)}) async-start(f32[12,4,8,128]{3,2,1,0:T(8,128)} %get-tuple-element.17), calls=%async_computation.5 | async-start | bytes 393216 | tf_op jit(solution)/shard_map/all_to_all | solution.py:283
  98.6 1.9 %collective-permute-start.3 = (f32[4,8,128]{2,1,0:T(8,128)S(1)}, f32[4,8,128]{2,1,0:T(8,128)S(1)}, u32[]{:S(2)}, u32[]{:S(2)}) collective-permute-start(f32[4,8,128]{2,1,0:T(8,128)S(1)} %get-tuple-element.20.one), channel_id=1, source_target_pairs={{0,48},{48,0},{1,49},{49,1},{2,50},{50,2},{3,51},{51,3},{4,52},{52... | collective-permute-start | bytes 49160 | tf_op jit(solution)/shard_map/ppermute | solution.py:287
  100.5 1.1 collective-permute-done.3.two
  101.6 0.7 y_copies.1
  102.3 2.7 %all-to-all-done.5 = f32[12,4,8,128]{3,2,1,0:T(8,128)S(1)} async-done(((f32[12,4,8,128]{3,2,1,0:T(8,128)}), f32[12,4,8,128]{3,2,1,0:T(8,128)S(1)}, u32[]{:S(2)}, u32[]{:S(2)}) %all-to-all-start.5) | async-done | bytes 196640 | tf_op jit(solution)/shard_map/all_to_all | solution.py:283
  105.0 3.4 %all-to-all-start.7 = ((f32[8,8,8,128]{3,2,1,0:T(8,128)}), f32[8,8,8,128]{3,2,1,0:T(8,128)S(1)}, u32[]{:S(2)}, u32[]{:S(2)}) async-start(f32[8,8,8,128]{3,2,1,0:T(8,128)} %y_copies.1), calls=%async_computation.7 | async-start | bytes 524288 | tf_op jit(solution)/shard_map/all_to_all | solution.py:283
  108.4 2.6 %lower_and_correlation.1 = (f32[8,5,8,128]{3,2,1,0:T(8,128)S(1)}, f32[8,5,8,128]{3,2,1,0:T(8,128)S(1)}) custom-call(s32[16]{0:T(128)S(1)} %bitcast.18, s32[16]{0:T(128)S(1)} %bitcast.22, s32[1]{0:T(128)} %bitcast.9.n, f32[16,128,128]{2,1,0:T(8,128)S(1)} %bitcast.13, f32[48,8,128]{2,1,0:T(8,128)S(1)} %bitcast.15, f32[48,8,128]{2,1,0:T(8,128)S(1)} %all_to_all.45.piece.x.v), custom_call_target="tpu_custom_call" | custom-call | flops 25165824 | bytes 1048576 | tf_op jit(solution)/shard_map/lower_and_correlation/pallas_call | solution.py:126
  111.0 1.9 %collective-permute-start.2 = (f32[8,5,8,128]{3,2,1,0:T(8,128)S(1)}, f32[8,5,8,128]{3,2,1,0:T(8,128)S(1)}, u32[]{:S(2)}, u32[]{:S(2)}) collective-permute-start(f32[8,5,8,128]{3,2,1,0:T(8,128)S(1)} %get-tuple-element.19), channel_id=1, source_target_pairs={{0,48},{48,0},{1,49},{49,1},{2,50},{50,2},{3,51},{51,3},{4,52},{52... | collective-permute-start | bytes 491528 | tf_op jit(solution)/shard_map/ppermute | solution.py:287
  113.0 1.4 collective-permute-done.2.b
  114.3 0.7 add.1
  115.0 3.8 %all-to-all-done.7.rest_0_ = f32[8,8,8,128]{3,2,1,0:T(8,128)S(1)} async-done(((f32[8,8,8,128]{3,2,1,0:T(8,128)}), f32[8,8,8,128]{3,2,1,0:T(8,128)S(1)}, u32[]{:S(2)}, u32[]{:S(2)}) %all-to-all-start.7) | async-done | bytes 262176 | tf_op jit(solution)/shard_map/all_to_all | solution.py:283
  118.8 3.4 %all-to-all-start.6 = ((f32[8,5,8,128]{3,2,1,0:T(8,128)}), f32[8,5,8,128]{3,2,1,0:T(8,128)S(1)}, u32[]{:S(2)}, u32[]{:S(2)}) async-start(f32[8,5,8,128]{3,2,1,0:T(8,128)} %add.1), calls=%async_computation.6 | async-start | bytes 327680 | tf_op jit(solution)/shard_map/all_to_all | solution.py:283
  122.2 2.3 %upper.3.sums = f32[48,8,128]{2,1,0:T(8,128)S(1)} custom-call(s32[16]{0:T(128)S(1)} %bitcast.23, s32[16]{0:T(128)S(1)} %bitcast.19, s32[1]{0:T(128)} %bitcast.10.n, f32[16,128,128]{2,1,0:T(8,128)S(1)} %bitcast.14, f32[8,8,8,128]{3,2,1,0:T(8,128)S(1)} %all-to-all-done.7.rest_0_), custom_call_target="tpu_custom_call" | custom-call | flops 25165824 | bytes 1048576 | tf_op jit(solution)/shard_map/upper/pallas_call | solution.py:77
  124.5 7.7 %all-to-all-done.6.got = f32[8,5,8,128]{3,2,1,0:T(8,128)S(1)} async-done(((f32[8,5,8,128]{3,2,1,0:T(8,128)}), f32[8,5,8,128]{3,2,1,0:T(8,128)S(1)}, u32[]{:S(2)}, u32[]{:S(2)}) %all-to-all-start.6) | async-done | bytes 163872 | tf_op jit(solution)/shard_map/all_to_all | solution.py:283
  132.2 0.0 copy-start.2
  132.2 21.8 %all_to_all.47.g = f32[48,8,128]{2,1,0:T(8,128)S(1)} all-to-all(f32[48,8,128]{2,1,0:T(8,128)S(1)} %get-tuple-element.21), channel_id=1, replica_groups=mesh['y'=8,'core'=2,'col'=12,'split'=4] {'col','split'}, dimensions={0} | all-to-all | bytes 393216 | tf_op jit(solution)/shard_map/all_to_all | solution.py:283
  154.0 0.0 copy-start.6
  154.0 0.0 copy-done.2
  154.0 0.7 copy-done.6
  154.7 0.7 results.1
  (4 shorter events, 0.1 us)
Async XLA Ops:
  0.6 0.7 copy-start.1
  1.3 42.1 %copy-start = (f32[1,1,16,128,128]{4,3,2,1,0:T(8,128)S(1)}, f32[1,1,16,128,128]{4,3,2,1,0:T(8,128)}, u32[]{:S(2)}) copy-start(f32[1,1,16,128,128]{4,3,2,1,0:T(8,128)} %param.8) | copy-start | bytes 3145732
  34.3 0.7 copy-start.5
  35.7 16.2 %all-to-all-start.1 = ((f32[8,4,8,128]{3,2,1,0:T(8,128)}), f32[8,4,8,128]{3,2,1,0:T(8,128)S(1)}, u32[]{:S(2)}, u32[]{:S(2)}) async-start(f32[8,4,8,128]{3,2,1,0:T(8,128)} %get-tuple-element.13), calls=%async_computation.1 | async-start | bytes 262144 | tf_op jit(solution)/shard_map/all_to_all | solution.py:283
  43.4 0.7 copy-start.3
  43.4 0.7 copy-start.4
  51.8 13.8 %all-to-all-start.3 = ((f32[8,8,8,128]{3,2,1,0:T(8,128)}), f32[8,8,8,128]{3,2,1,0:T(8,128)S(1)}, u32[]{:S(2)}, u32[]{:S(2)}) async-start(f32[8,8,8,128]{3,2,1,0:T(8,128)} %lower.1), calls=%async_computation.3 | async-start | bytes 524288 | tf_op jit(solution)/shard_map/all_to_all | solution.py:283
  55.3 3.2 %collective-permute-start = (f32[8,4,8,128]{3,2,1,0:T(8,128)S(1)}, f32[8,4,8,128]{3,2,1,0:T(8,128)S(1)}, u32[]{:S(2)}, u32[]{:S(2)}) collective-permute-start(f32[8,4,8,128]{3,2,1,0:T(8,128)S(1)} %all-to-all-done.1.rest_0_), channel_id=1, source_target_pairs={{0,48},{48,0},{1,49},{49,1},{2,50},{50,2},{3,51},{51,3},{4,52},{52... | collective-permute-start | bytes 393224 | tf_op jit(solution)/shard_map/ppermute | solution.py:287
  65.6 11.2 %all-to-all-start.2 = ((f32[12,4,8,128]{3,2,1,0:T(8,128)}), f32[12,4,8,128]{3,2,1,0:T(8,128)S(1)}, u32[]{:S(2)}, u32[]{:S(2)}) async-start(f32[12,4,8,128]{3,2,1,0:T(8,128)} %bitcast.5), calls=%async_computation.2 | async-start | bytes 393216 | tf_op jit(solution)/shard_map/all_to_all | solution.py:283
  70.4 3.1 %collective-permute-start.1 = (f32[4,8,128]{2,1,0:T(8,128)S(1)}, f32[4,8,128]{2,1,0:T(8,128)S(1)}, u32[]{:S(2)}, u32[]{:S(2)}) collective-permute-start(f32[4,8,128]{2,1,0:T(8,128)S(1)} %get-tuple-element.15), channel_id=1, source_target_pairs={{0,48},{48,0},{1,49},{49,1},{2,50},{50,2},{3,51},{51,3},{4,52},{52... | collective-permute-start | bytes 49160 | tf_op jit(solution)/shard_map/ppermute | solution.py:287
  93.8 11.2 %all-to-all-start.5 = ((f32[12,4,8,128]{3,2,1,0:T(8,128)}), f32[12,4,8,128]{3,2,1,0:T(8,128)S(1)}, u32[]{:S(2)}, u32[]{:S(2)}) async-start(f32[12,4,8,128]{3,2,1,0:T(8,128)} %get-tuple-element.17), calls=%async_computation.5 | async-start | bytes 393216 | tf_op jit(solution)/shard_map/all_to_all | solution.py:283
  98.6 3.1 %collective-permute-start.3 = (f32[4,8,128]{2,1,0:T(8,128)S(1)}, f32[4,8,128]{2,1,0:T(8,128)S(1)}, u32[]{:S(2)}, u32[]{:S(2)}) collective-permute-start(f32[4,8,128]{2,1,0:T(8,128)S(1)} %get-tuple-element.20.one), channel_id=1, source_target_pairs={{0,48},{48,0},{1,49},{49,1},{2,50},{50,2},{3,51},{51,3},{4,52},{52... | collective-permute-start | bytes 49160 | tf_op jit(solution)/shard_map/ppermute | solution.py:287
  105.0 13.8 %all-to-all-start.7 = ((f32[8,8,8,128]{3,2,1,0:T(8,128)}), f32[8,8,8,128]{3,2,1,0:T(8,128)S(1)}, u32[]{:S(2)}, u32[]{:S(2)}) async-start(f32[8,8,8,128]{3,2,1,0:T(8,128)} %y_copies.1), calls=%async_computation.7 | async-start | bytes 524288 | tf_op jit(solution)/shard_map/all_to_all | solution.py:283
  111.0 3.3 %collective-permute-start.2 = (f32[8,5,8,128]{3,2,1,0:T(8,128)S(1)}, f32[8,5,8,128]{3,2,1,0:T(8,128)S(1)}, u32[]{:S(2)}, u32[]{:S(2)}) collective-permute-start(f32[8,5,8,128]{3,2,1,0:T(8,128)S(1)} %get-tuple-element.19), channel_id=1, source_target_pairs={{0,48},{48,0},{1,49},{49,1},{2,50},{50,2},{3,51},{51,3},{4,52},{52... | collective-permute-start | bytes 491528 | tf_op jit(solution)/shard_map/ppermute | solution.py:287
  118.8 13.4 %all-to-all-start.6 = ((f32[8,5,8,128]{3,2,1,0:T(8,128)}), f32[8,5,8,128]{3,2,1,0:T(8,128)S(1)}, u32[]{:S(2)}, u32[]{:S(2)}) async-start(f32[8,5,8,128]{3,2,1,0:T(8,128)} %add.1), calls=%async_computation.6 | async-start | bytes 327680 | tf_op jit(solution)/shard_map/all_to_all | solution.py:283
  132.2 21.8 %copy-start.2 = (f32[8,128]{1,0:T(8,128)S(1)}, f32[8,128]{1,0:T(8,128)}, u32[]{:S(2)}) copy-start(f32[8,128]{1,0:T(8,128)} %v.3) | copy-start | bytes 12292
  154.0 0.7 copy-start.6

commit v5 on v3

--- a/solution.py
+++ b/solution.py
@@ -15,35 +15,76 @@
     return tuple(jax.ShapeDtypeStruct(s, jnp.float32) for s in shapes)
 
 
-def add_products(ids_from, ids_to, used, u_ref, in_ref, out_ref, block_dim, from_slot, to_slot):
-    for t in range(u_ref.shape[0]):
-        term = lax.dot_general(
-            in_ref[from_slot(ids_from[t])], u_ref[t], (((1,), (block_dim,)), ((), ())),
-            precision=HIGHEST, preferred_element_type=jnp.float32,
-        )
-        keep = jnp.where(t < used[0], 1.0, 0.0).astype(jnp.float32)
-        out_ref[to_slot(ids_to[t])] += term * keep
-
-
-def same(block):
-    return block
-
-
-def column_slot(splits):
-    core = lax.axis_index("core")
-
-    def slot(c):
-        row, s = lax.div(c, jnp.int32(splits)), lax.rem(c, jnp.int32(splits))
-        y, its_core = lax.div(row, jnp.int32(2)), lax.rem(row, jnp.int32(2))
-        other = jnp.where(its_core == core, 0, 1)
-        return other, y, s
-
-    return slot
+def halves(x):
+    high = x.astype(jnp.bfloat16)
+    return high, (x - high.astype(jnp.float32)).astype(jnp.bfloat16)
+
+
+def prepare(row_ids, col_ids, count, blocks, start, diag, splits):
+    slots, size, _ = blocks.shape
+
+    def kernel(r, c, n, u, v, d, lower, upper, table, scaled):
+        core = lax.axis_index("core")
+        for t in range(slots):
+            row, split = lax.div(c[t], jnp.int32(splits)), lax.rem(c[t], jnp.int32(splits))
+            table[t] = r[t]
+            table[slots + t] = jnp.where(lax.rem(row, jnp.int32(2)) == core, 0, 1)
+            table[2 * slots + t] = lax.div(row, jnp.int32(2))
+            table[3 * slots + t] = split
+            block = u[t] * jnp.where(t < n[0], 1.0, 0.0).astype(jnp.float32)
+            for out, x in ((lower, block), (upper, block.T)):
+                high, low = halves(x)
+                out[t, :, :size] = high
+                out[t, :, size:] = low
+        scaled[...] = v[...] * d[...]
+
+    both = jax.ShapeDtypeStruct((slots, size, 2 * size), jnp.bfloat16)
+    return pl.pallas_call(
+        kernel,
+        out_shape=(
+            both, both, jax.ShapeDtypeStruct((4 * slots,), jnp.int32),
+            jax.ShapeDtypeStruct(start.shape, jnp.float32),
+        ),
+        in_specs=[SMEM] * 3 + [VMEM] * 3,
+        out_specs=(VMEM, VMEM, SMEM, VMEM),
+        compiler_params=PARAMS,
+        cost_estimate=pl.CostEstimate(
+            flops=8 * blocks.size, bytes_accessed=12 * blocks.size, transcendentals=0
+        ),
+        name="prepare",
+    )(row_ids, col_ids, count, blocks, start, diag)
+
+
+def product(x, block):
+    rows, size = x.shape
+    high = x.astype(jnp.bfloat16).astype(jnp.float32)
+    pair = jnp.concatenate([high, x - high], 0).astype(jnp.bfloat16)
+    terms = lax.dot_general(
+        pair, block, (((1,), (0,)), ((), ())), preferred_element_type=jnp.float32
+    )
+    terms = terms[:rows] + terms[rows:]
+    return terms[:, :size] + terms[:, size:]
+
+
+def pair_sums(one, two):
+    blocks, vectors, size = one.shape
+    sums = [jnp.zeros((vectors, size), jnp.float32) for _ in range(vectors)]
+    for g in range(blocks):
+        x, v = one[g], two[g]
+        for r in range(vectors):
+            sums[r] += x * (pltpu.roll(v, r, 0) if r else v)
+    l = lax.broadcasted_iota(jnp.int32, (vectors, vectors), 0)
+    k = lax.broadcasted_iota(jnp.int32, (vectors, vectors), 1)
+    out = jnp.zeros((vectors, vectors), jnp.float32)
+    for r in range(vectors):
+        its = (l - k == r) | (l - k == r - vectors)
+        out += jnp.where(its, jnp.sum(sums[r], axis=1, keepdims=True), 0.0)
+    return out
 
 
 def cost(blocks, vectors):
     return pl.CostEstimate(
-        flops=12 * blocks.size * vectors, bytes_accessed=4 * blocks.size, transcendentals=0
+        flops=4 * blocks.size * vectors, bytes_accessed=2 * blocks.size, transcendentals=0
     )
 
 
@@ -59,59 +100,59 @@
     )(start)
 
 
-def upper_products(col_ids, row_ids, count, blocks, own_cols, other_cols, row_blocks):
+def upper_products(table, blocks, own_cols, other_cols, row_blocks):
     ys, splits, vectors, size = own_cols.shape
-
-    def kernel(a, b, n, u, own, other, out, both):
+    slots = blocks.shape[0]
+
+    def kernel(at, u, own, other, out, both):
         both[0], both[1] = own[...], other[...]
         out[...] = jnp.zeros_like(out)
-        add_products(a, b, n, u, both, out, 1, column_slot(splits), same)
+        for t in range(slots):
+            x = both[at[slots + t], at[2 * slots + t], at[3 * slots + t]]
+            out[at[t]] += product(x, u[t])
 
     return pl.pallas_call(
         kernel,
         out_shape=arrays((row_blocks, vectors, size))[0],
-        in_specs=[SMEM] * 3 + [VMEM] * 3,
+        in_specs=[SMEM] + [VMEM] * 3,
         out_specs=VMEM,
         scratch_shapes=[pltpu.VMEM((2, ys, splits, vectors, size), jnp.float32)],
         compiler_params=PARAMS,
         cost_estimate=cost(blocks, vectors),
         name="upper",
-    )(col_ids, row_ids, count, blocks, own_cols, other_cols)
-
-
-def lower_products(row_ids, col_ids, count, blocks, row_piece, start_piece, ys, splits):
-    tile, vectors, size = row_piece.shape
+    )(table, blocks, own_cols, other_cols)
+
+
+def lower_products(table, blocks, row_piece, start_piece, ys, splits):
+    _, vectors, size = row_piece.shape
+    slots = blocks.shape[0]
     with_corr = start_piece is not None
     each = splits + 1 if with_corr else splits
 
-    def kernel(a, b, n, u, x, *rest):
-        v = rest[0] if with_corr else None
+    def kernel(at, u, x, *rest):
         own, other, both = rest[-3:]
         both[...] = jnp.zeros_like(both)
+        for t in range(slots):
+            place = at[slots + t], at[2 * slots + t], at[3 * slots + t]
+            both[place] += product(x[at[t]], u[t])
         if with_corr:
-            term = jnp.zeros((vectors, vectors), jnp.float32)
-            for g in range(tile):
-                term += lax.dot_general(
-                    x[g], v[g], (((1,), (1,)), ((), ())), precision=HIGHEST,
-                    preferred_element_type=jnp.float32,
-                )
+            term = pair_sums(x, rest[0])
             for y in range(ys):
                 both[0, y, splits, :, :vectors] = term
                 both[1, y, splits, :, :vectors] = term
-        add_products(a, b, n, u, x, both, 0, same, column_slot(splits))
         own[...], other[...] = both[0], both[1]
 
     shape = (ys, each, vectors, size)
     return pl.pallas_call(
         kernel,
         out_shape=arrays(shape, shape),
-        in_specs=[SMEM] * 3 + [VMEM] * (3 if with_corr else 2),
+        in_specs=[SMEM] + [VMEM] * (3 if with_corr else 2),
         out_specs=(VMEM, VMEM),
         scratch_shapes=[pltpu.VMEM((2,) + shape, jnp.float32)],
         compiler_params=PARAMS,
         cost_estimate=cost(blocks, vectors),
         name="lower",
-    )(row_ids, col_ids, count, blocks, row_piece, *((start_piece,) if with_corr else ()))
+    )(table, blocks, row_piece, *((start_piece,) if with_corr else ()))
 
 
 def add(one, two):
@@ -124,10 +165,10 @@
     )(one, two)
 
 
-def own_copies(row_piece, splits, copies):
+def own_copies(row_piece, prepared, splits, copies):
     _, vectors, size = row_piece.shape
 
-    def kernel(piece, out):
+    def kernel(piece, _, out):
         first = lax.axis_index("col") * splits
         for s in range(splits):
             block = piece[first + s]
@@ -136,15 +177,14 @@
 
     return pl.pallas_call(
         kernel, out_shape=arrays((copies, splits, vectors, size))[0],
-        in_specs=[VMEM], out_specs=VMEM, compiler_params=PARAMS, name="own_copies",
-    )(row_piece)
-
-
-def group_part(row_got, col_got, vectors, diag):
+        in_specs=[VMEM] * 2, out_specs=VMEM, compiler_params=PARAMS, name="own_copies",
+    )(row_piece, prepared)
+
+
+def group_part(row_got, col_got, scaled):
     splits = row_got.shape[1]
 
-    def kernel(rows, cols, v, d, out):
-        own = v[...] * d[...]
+    def kernel(rows, cols, own, out):
         mine = lax.axis_index("split")
         for s in range(splits):
             total = rows[0, s]
@@ -152,14 +192,14 @@
                 total += rows[j, s]
             for i in range(cols.shape[0]):
                 total += cols[i, s]
-            total += own * jnp.where(mine == s, 1.0, 0.0).astype(jnp.float32)
+            total += own[...] * jnp.where(mine == s, 1.0, 0.0).astype(jnp.float32)
             for k in range(splits):
                 out[k, s] = total
 
     return pl.pallas_call(
         kernel, out_shape=arrays((splits,) + row_got.shape[1:])[0],
-        in_specs=[VMEM] * 4, out_specs=VMEM, compiler_params=PARAMS, name="group_part",
-    )(row_got, col_got, vectors, diag)
+        in_specs=[VMEM] * 3, out_specs=VMEM, compiler_params=PARAMS, name="group_part",
+    )(row_got, col_got, scaled)
 
 
 def image_copies(parts, ys, cols):
@@ -259,24 +299,23 @@
     plane = ("col", "split")
 
     start_row = exchange(start_copies(start_vectors, cols * splits), plane)
-    own_cols = exchange(own_copies(start_row, splits, ys), "y")
-    own, other = lower_products(row_ids, col_ids, count, blocks, start_row, None, ys, splits)
+    lower, upper, table, scaled = prepare(
+        row_ids, col_ids, count, blocks, start_vectors, diag, splits
+    )
+    own_cols = exchange(own_copies(start_row, scaled, splits, ys), "y")
+    own, other = lower_products(table, lower, start_row, None, ys, splits)
     col_got = exchange(add(own, swap_cores(other)), "y")
-    upper = upper_products(
-        col_ids, row_ids, count, blocks, own_cols, swap_cores(own_cols), cols * splits
-    )
-    row_got = exchange(upper.reshape(cols, splits, vectors, size), "col")
-    parts = exchange(group_part(row_got, col_got, start_vectors, diag), "split")
+    rows = upper_products(table, upper, own_cols, swap_cores(own_cols), cols * splits)
+    row_got = exchange(rows.reshape(cols, splits, vectors, size), "col")
+    parts = exchange(group_part(row_got, col_got, scaled), "split")
 
     col_copies, y_copies, first = image_copies(parts, ys, cols)
     first_row = exchange(col_copies, "col").reshape(cols * splits, vectors, size)
     own_cols = exchange(y_copies, "y")
-    own, other = lower_products(row_ids, col_ids, count, blocks, first_row, start_row, ys, splits)
+    own, other = lower_products(table, lower, first_row, start_row, ys, splits)
     col_got = exchange(add(own, swap_cores(other)), "y")
-    upper = upper_products(
-        col_ids, row_ids, count, blocks, own_cols, swap_cores(own_cols), cols * splits
-    )
-    messages, corr = add_to_messages(col_got, upper)
+    rows = upper_products(table, upper, own_cols, swap_cores(own_cols), cols * splits)
+    messages, corr = add_to_messages(col_got, rows)
     got = exchange(messages, plane)
     residual = residual_of(corr, first, start_vectors, total)
     return residual, second_of(got, corr, first, diag, total)

time: 155 us -> 151 us (0.974)
  blocking collectives: 70.9 us -> 37.9 us
  waiting for transfers between devices: 31 us -> 46.8 us
  starting transfers between devices: 34.5 us -> 50 us
  Pallas kernels: 13.6 us -> 10.5 us
    all_to_all x4 -> x3, blocking collectives: 70.9 us -> 37.9 us  [exchange(): return lax.all_to_all(parts, axis, 0, 0, tiled=True)]
    all_to_all x5 -> x6, waiting for transfers between devices: 25.7 us -> 41.5 us  [exchange(): return lax.all_to_all(parts, axis, 0, 0, tiled=True)]
    all_to_all x5 -> x6, starting transfers between devices: 26.9 us -> 42.3 us  [exchange(): return lax.all_to_all(parts, axis, 0, 0, tiled=True)]
    pallas_call x2, Pallas kernels: 4.54 us -> 1.59 us  [upper_products(): pl.pallas_call(kernel, out_shape=arrays((row_blocks, vectors, size))[0],...]
    pallas_call x2 -> x3, Pallas kernels: 4.13 us -> 3.29 us  [the longest x2 1.72 us: lower_products(): pl.pallas_call(kernel, out_shape=arrays(shape, shape), in_specs=[SMEM] +...]
  transfers between devices with their start and end apart: 9 -> 10, of which waited for: 9 -> 10; matrix products, arithmetic and copies ran while one was open for 0% -> 0% of each run, Pallas kernels for 7% -> 5%
where the time goes in v5:
time: 151 us; the launch traced here: 149 us
  starting transfers between devices  50 us (33%)
  waiting for transfers between devices  46.8 us (31%)
  blocking collectives  37.9 us (25%)
  Pallas kernels  10.5 us (7%)
  local copies, waits for them, and re-layouts  2.58 us (2%)
    all_to_all x6, starting transfers between devices, exchange(): return lax.all_to_all(parts, axis, 0, 0, tiled=True)  42.3 us
    all_to_all x6, waiting for transfers between devices, exchange(): return lax.all_to_all(parts, axis, 0, 0, tiled=True)  41.5 us
    all_to_all x3, blocking collectives, exchange(): return lax.all_to_all(parts, axis, 0, 0, tiled=True)  37.9 us
    ppermute x4, starting transfers between devices, swap_cores(): return lax.ppermute(piece, 'core', [(0, 1), (1, 0)])  7.68 us
    ppermute x4, waiting for transfers between devices, swap_cores(): return lax.ppermute(piece, 'core', [(0, 1), (1, 0)])  5.3 us
  transfers between devices with their start and end apart: 10, of which 10 were waited for; matrix products, arithmetic and copies ran while one was open for 0% of the time, Pallas kernels for 5%

profile of v5, /device:TPU:6, one launch (start us, length us, event | category | flops | bytes accessed | tf_op | source)
XLA Modules:
  0.0 149.2 jit_solution(12672651475406700015)
XLA Ops:
  0.6 0.0 copy-start.1
  0.6 0.7 copy-done.1
  1.3 0.7 start_copies.1
  2.0 18.4 %all-to-all-start = ((f32[48,8,128]{2,1,0:T(8,128)}), f32[48,8,128]{2,1,0:T(8,128)S(1)}, u32[]{:S(2)}, u32[]{:S(2)}) async-start(f32[48,8,128]{2,1,0:T(8,128)} %start_copies.1), calls=%async_computation | async-start | bytes 393216 | tf_op jit(solution)/shard_map/all_to_all | solution.py:282
  21.1 0.0 copy-start.2
  21.1 0.0 copy-start.3
  21.1 0.0 copy-start.4
  21.1 0.0 copy-start.5
  21.1 0.6 copy-done.2
  21.8 0.0 copy-done.3
  21.8 0.0 copy-done.4
  21.8 0.0 copy-done.5
  21.8 0.0 copy-start
  21.8 1.2 copy-done
  23.0 1.6 %prepare.1 = (bf16[16,128,256]{2,1,0:T(8,128)(2,1)S(1)}, bf16[16,128,256]{2,1,0:T(8,128)(2,1)S(1)}, s32[64]{0:T(128)S(1)}, f32[8,128]{1,0:T(8,128)S(1)}) custom-call(s32[16]{0:T(128)S(1)} %bitcast.13, s32[16]{0:T(128)S(1)} %bitcast.14, s32[1]{0:T(128)} %bitcast.7.n, f32[16,128,128]{2,1,0:T(8,128)S(1)} %bitcast.8, f32[8,128]{1,0:T(8,128)S(1)} %copy-done.2, ...), custom_call_target="tpu_custom_call" | custom-call | flops 2097152 | bytes 3145728 | tf_op jit(solution)/shard_map/prepare/pallas_call | solution.py:42
  24.6 10.5 %all-to-all-done.piece.x.rest_0_ = f32[48,8,128]{2,1,0:T(8,128)S(1)} async-done(((f32[48,8,128]{2,1,0:T(8,128)}), f32[48,8,128]{2,1,0:T(8,128)S(1)}, u32[]{:S(2)}, u32[]{:S(2)}) %all-to-all-start) | async-done | bytes 196640 | tf_op jit(solution)/shard_map/all_to_all | solution.py:282
  35.1 0.7 own_copies.1
  35.7 7.1 %all-to-all-start.1 = ((f32[8,4,8,128]{3,2,1,0:T(8,128)}), f32[8,4,8,128]{3,2,1,0:T(8,128)S(1)}, u32[]{:S(2)}, u32[]{:S(2)}) async-start(f32[8,4,8,128]{3,2,1,0:T(8,128)} %own_copies.1), calls=%async_computation.1 | async-start | bytes 262144 | tf_op jit(solution)/shard_map/all_to_all | solution.py:282
  42.8 0.8 lower.2
  43.7 1.9 %collective-permute-start.1 = (f32[8,4,8,128]{3,2,1,0:T(8,128)S(1)}, f32[8,4,8,128]{3,2,1,0:T(8,128)S(1)}, u32[]{:S(2)}, u32[]{:S(2)}) collective-permute-start(f32[8,4,8,128]{3,2,1,0:T(8,128)S(1)} %get-tuple-element.20), channel_id=1, source_target_pairs={{0,48},{48,0},{1,49},{49,1},{2,50},{50,2},{3,51},{51,3},{4,52},{52... | collective-permute-start | bytes 393224 | tf_op jit(solution)/shard_map/ppermute | solution.py:286
  45.6 1.3 collective-permute-done.1.b
  46.9 0.7 add.2
  47.6 4.4 %all-to-all-done.1.own = f32[8,4,8,128]{3,2,1,0:T(8,128)S(1)} async-done(((f32[8,4,8,128]{3,2,1,0:T(8,128)}), f32[8,4,8,128]{3,2,1,0:T(8,128)S(1)}, u32[]{:S(2)}, u32[]{:S(2)}) %all-to-all-start.1) | async-done | bytes 131104 | tf_op jit(solution)/shard_map/all_to_all | solution.py:282
  51.9 3.4 %all-to-all-start.3 = ((f32[8,4,8,128]{3,2,1,0:T(8,128)}), f32[8,4,8,128]{3,2,1,0:T(8,128)S(1)}, u32[]{:S(2)}, u32[]{:S(2)}) async-start(f32[8,4,8,128]{3,2,1,0:T(8,128)} %add.2), calls=%async_computation.3 | async-start | bytes 262144 | tf_op jit(solution)/shard_map/all_to_all | solution.py:282
  55.3 1.9 %collective-permute-start = (f32[8,4,8,128]{3,2,1,0:T(8,128)S(1)}, f32[8,4,8,128]{3,2,1,0:T(8,128)S(1)}, u32[]{:S(2)}, u32[]{:S(2)}) collective-permute-start(f32[8,4,8,128]{3,2,1,0:T(8,128)S(1)} %all-to-all-done.1.own), channel_id=1, source_target_pairs={{0,48},{48,0},{1,49},{49,1},{2,50},{50,2},{3,51},{51,3},{4,52},{52... | collective-permute-start | bytes 393224 | tf_op jit(solution)/shard_map/ppermute | solution.py:286
  57.2 1.3 collective-permute-done.other
  58.5 0.8 upper.2
  59.4 5.0 %all-to-all-done.3.cols = f32[8,4,8,128]{3,2,1,0:T(8,128)S(1)} async-done(((f32[8,4,8,128]{3,2,1,0:T(8,128)}), f32[8,4,8,128]{3,2,1,0:T(8,128)S(1)}, u32[]{:S(2)}, u32[]{:S(2)}) %all-to-all-start.3) | async-done | bytes 131104 | tf_op jit(solution)/shard_map/all_to_all | solution.py:282
  64.3 11.0 %all_to_all.45.rows = f32[12,4,8,128]{3,2,1,0:T(8,128)S(1)} all-to-all(f32[12,4,8,128]{3,2,1,0:T(8,128)S(1)} %bitcast.10), channel_id=1, replica_groups=mesh['y'=8,'core'=2,'col'=12,'split'=4] {'col'}, dimensions={0} | all-to-all | bytes 393216 | tf_op jit(solution)/shard_map/all_to_all | solution.py:282
  75.3 16.3 %all_to_all.46.p = f32[4,4,8,128]{3,2,1,0:T(8,128)S(1)} all-to-all(f32[4,4,8,128]{3,2,1,0:T(8,128)S(1)} %group_part.1), channel_id=1, replica_groups=mesh['y'=8,'core'=2,'col'=12,'split'=4] {'split'}, dimensions={0} | all-to-all | bytes 131072 | tf_op jit(solution)/shard_map/all_to_all | solution.py:282
  91.6 0.7 image_copies.1
  92.2 10.7 %all_to_all.47 = f32[12,4,8,128]{3,2,1,0:T(8,128)S(1)} all-to-all(f32[12,4,8,128]{3,2,1,0:T(8,128)S(1)} %get-tuple-element.21), channel_id=1, replica_groups=mesh['y'=8,'core'=2,'col'=12,'split'=4] {'col'}, dimensions={0} | all-to-all | bytes 393216 | tf_op jit(solution)/shard_map/all_to_all | solution.py:282
  103.0 3.4 %all-to-all-start.7 = ((f32[8,4,8,128]{3,2,1,0:T(8,128)}), f32[8,4,8,128]{3,2,1,0:T(8,128)S(1)}, u32[]{:S(2)}, u32[]{:S(2)}) async-start(f32[8,4,8,128]{3,2,1,0:T(8,128)} %get-tuple-element.24), calls=%async_computation.7 | async-start | bytes 262144 | tf_op jit(solution)/shard_map/all_to_all | solution.py:282
  106.3 0.9 lower.3
  107.2 1.9 %collective-permute-start.2 = (f32[8,5,8,128]{3,2,1,0:T(8,128)S(1)}, f32[8,5,8,128]{3,2,1,0:T(8,128)S(1)}, u32[]{:S(2)}, u32[]{:S(2)}) collective-permute-start(f32[8,5,8,128]{3,2,1,0:T(8,128)S(1)} %get-tuple-element.23), channel_id=1, source_target_pairs={{0,48},{48,0},{1,49},{49,1},{2,50},{50,2},{3,51},{51,3},{4,52},{52... | collective-permute-start | bytes 491528 | tf_op jit(solution)/shard_map/ppermute | solution.py:286
  109.2 1.4 collective-permute-done.2.b
  110.5 0.7 add.3
  111.2 4.1 %all-to-all-done.7.own = f32[8,4,8,128]{3,2,1,0:T(8,128)S(1)} async-done(((f32[8,4,8,128]{3,2,1,0:T(8,128)}), f32[8,4,8,128]{3,2,1,0:T(8,128)S(1)}, u32[]{:S(2)}, u32[]{:S(2)}) %all-to-all-start.7) | async-done | bytes 131104 | tf_op jit(solution)/shard_map/all_to_all | solution.py:282
  115.3 3.4 %all-to-all-start.6 = ((f32[8,5,8,128]{3,2,1,0:T(8,128)}), f32[8,5,8,128]{3,2,1,0:T(8,128)S(1)}, u32[]{:S(2)}, u32[]{:S(2)}) async-start(f32[8,5,8,128]{3,2,1,0:T(8,128)} %add.3), calls=%async_computation.6 | async-start | bytes 327680 | tf_op jit(solution)/shard_map/all_to_all | solution.py:282
  118.7 1.9 %collective-permute-start.3 = (f32[8,4,8,128]{3,2,1,0:T(8,128)S(1)}, f32[8,4,8,128]{3,2,1,0:T(8,128)S(1)}, u32[]{:S(2)}, u32[]{:S(2)}) collective-permute-start(f32[8,4,8,128]{3,2,1,0:T(8,128)S(1)} %all-to-all-done.7.own), channel_id=1, source_target_pairs={{0,48},{48,0},{1,49},{49,1},{2,50},{50,2},{3,51},{51,3},{4,52},{52... | collective-permute-start | bytes 393224 | tf_op jit(solution)/shard_map/ppermute | solution.py:286
  120.7 1.3 collective-permute-done.3.other
  122.0 0.8 upper.3.sums
  122.8 5.7 %all-to-all-done.6.got = f32[8,5,8,128]{3,2,1,0:T(8,128)S(1)} async-done(((f32[8,5,8,128]{3,2,1,0:T(8,128)}), f32[8,5,8,128]{3,2,1,0:T(8,128)S(1)}, u32[]{:S(2)}, u32[]{:S(2)}) %all-to-all-start.6) | async-done | bytes 163872 | tf_op jit(solution)/shard_map/all_to_all | solution.py:282
  128.4 0.7 add_to_messages.1
  129.1 6.7 %all-to-all-start.8 = ((f32[48,8,128]{2,1,0:T(8,128)}), f32[48,8,128]{2,1,0:T(8,128)S(1)}, u32[]{:S(2)}, u32[]{:S(2)}) async-start(f32[48,8,128]{2,1,0:T(8,128)} %get-tuple-element.27), calls=%async_computation.8 | async-start | bytes 393216 | tf_op jit(solution)/shard_map/all_to_all | solution.py:282
  135.8 0.7 residual.1
  136.5 11.9 %all-to-all-done.8.g = f32[48,8,128]{2,1,0:T(8,128)S(1)} async-done(((f32[48,8,128]{2,1,0:T(8,128)}), f32[48,8,128]{2,1,0:T(8,128)S(1)}, u32[]{:S(2)}, u32[]{:S(2)}) %all-to-all-start.8) | async-done | bytes 196640 | tf_op jit(solution)/shard_map/all_to_all | solution.py:282
  148.5 0.7 second.1
  (1 shorter events, 0.0 us)
Async XLA Ops:
  0.6 0.7 copy-start.1
  2.0 33.1 %all-to-all-start = ((f32[48,8,128]{2,1,0:T(8,128)}), f32[48,8,128]{2,1,0:T(8,128)S(1)}, u32[]{:S(2)}, u32[]{:S(2)}) async-start(f32[48,8,128]{2,1,0:T(8,128)} %start_copies.1), calls=%async_computation | async-start | bytes 393216 | tf_op jit(solution)/shard_map/all_to_all | solution.py:282
  21.1 0.7 copy-start.2
  21.1 0.7 copy-start.3
  21.1 0.7 copy-start.4
  21.1 0.7 copy-start.5
  21.8 1.2 copy-start
  35.7 16.2 %all-to-all-start.1 = ((f32[8,4,8,128]{3,2,1,0:T(8,128)}), f32[8,4,8,128]{3,2,1,0:T(8,128)S(1)}, u32[]{:S(2)}, u32[]{:S(2)}) async-start(f32[8,4,8,128]{3,2,1,0:T(8,128)} %own_copies.1), calls=%async_computation.1 | async-start | bytes 262144 | tf_op jit(solution)/shard_map/all_to_all | solution.py:282
  43.7 3.2 %collective-permute-start.1 = (f32[8,4,8,128]{3,2,1,0:T(8,128)S(1)}, f32[8,4,8,128]{3,2,1,0:T(8,128)S(1)}, u32[]{:S(2)}, u32[]{:S(2)}) collective-permute-start(f32[8,4,8,128]{3,2,1,0:T(8,128)S(1)} %get-tuple-element.20), channel_id=1, source_target_pairs={{0,48},{48,0},{1,49},{49,1},{2,50},{50,2},{3,51},{51,3},{4,52},{52... | collective-permute-start | bytes 393224 | tf_op jit(solution)/shard_map/ppermute | solution.py:286
  51.9 12.4 %all-to-all-start.3 = ((f32[8,4,8,128]{3,2,1,0:T(8,128)}), f32[8,4,8,128]{3,2,1,0:T(8,128)S(1)}, u32[]{:S(2)}, u32[]{:S(2)}) async-start(f32[8,4,8,128]{3,2,1,0:T(8,128)} %add.2), calls=%async_computation.3 | async-start | bytes 262144 | tf_op jit(solution)/shard_map/all_to_all | solution.py:282
  55.3 3.2 %collective-permute-start = (f32[8,4,8,128]{3,2,1,0:T(8,128)S(1)}, f32[8,4,8,128]{3,2,1,0:T(8,128)S(1)}, u32[]{:S(2)}, u32[]{:S(2)}) collective-permute-start(f32[8,4,8,128]{3,2,1,0:T(8,128)S(1)} %all-to-all-done.1.own), channel_id=1, source_target_pairs={{0,48},{48,0},{1,49},{49,1},{2,50},{50,2},{3,51},{51,3},{4,52},{52... | collective-permute-start | bytes 393224 | tf_op jit(solution)/shard_map/ppermute | solution.py:286
  103.0 12.4 %all-to-all-start.7 = ((f32[8,4,8,128]{3,2,1,0:T(8,128)}), f32[8,4,8,128]{3,2,1,0:T(8,128)S(1)}, u32[]{:S(2)}, u32[]{:S(2)}) async-start(f32[8,4,8,128]{3,2,1,0:T(8,128)} %get-tuple-element.24), calls=%async_computation.7 | async-start | bytes 262144 | tf_op jit(solution)/shard_map/all_to_all | solution.py:282
  107.2 3.3 %collective-permute-start.2 = (f32[8,5,8,128]{3,2,1,0:T(8,128)S(1)}, f32[8,5,8,128]{3,2,1,0:T(8,128)S(1)}, u32[]{:S(2)}, u32[]{:S(2)}) collective-permute-start(f32[8,5,8,128]{3,2,1,0:T(8,128)S(1)} %get-tuple-element.23), channel_id=1, source_target_pairs={{0,48},{48,0},{1,49},{49,1},{2,50},{50,2},{3,51},{51,3},{4,52},{52... | collective-permute-start | bytes 491528 | tf_op jit(solution)/shard_map/ppermute | solution.py:286
  115.3 13.1 %all-to-all-start.6 = ((f32[8,5,8,128]{3,2,1,0:T(8,128)}), f32[8,5,8,128]{3,2,1,0:T(8,128)S(1)}, u32[]{:S(2)}, u32[]{:S(2)}) async-start(f32[8,5,8,128]{3,2,1,0:T(8,128)} %add.3), calls=%async_computation.6 | async-start | bytes 327680 | tf_op jit(solution)/shard_map/all_to_all | solution.py:282
  118.7 3.2 %collective-permute-start.3 = (f32[8,4,8,128]{3,2,1,0:T(8,128)S(1)}, f32[8,4,8,128]{3,2,1,0:T(8,128)S(1)}, u32[]{:S(2)}, u32[]{:S(2)}) collective-permute-start(f32[8,4,8,128]{3,2,1,0:T(8,128)S(1)} %all-to-all-done.7.own), channel_id=1, source_target_pairs={{0,48},{48,0},{1,49},{49,1},{2,50},{50,2},{3,51},{51,3},{4,52},{52... | collective-permute-start | bytes 393224 | tf_op jit(solution)/shard_map/ppermute | solution.py:286
  129.1 19.3 %all-to-all-start.8 = ((f32[48,8,128]{2,1,0:T(8,128)}), f32[48,8,128]{2,1,0:T(8,128)S(1)}, u32[]{:S(2)}, u32[]{:S(2)}) async-start(f32[48,8,128]{2,1,0:T(8,128)} %get-tuple-element.27), calls=%async_computation.8 | async-start | bytes 393216 | tf_op jit(solution)/shard_map/all_to_all | solution.py:282

commit v6 on v5

--- a/solution.py
+++ b/solution.py
@@ -31,6 +31,7 @@
             table[slots + t] = jnp.where(lax.rem(row, jnp.int32(2)) == core, 0, 1)
             table[2 * slots + t] = lax.div(row, jnp.int32(2))
             table[3 * slots + t] = split
+            table[4 * slots + t] = lax.rem(row, jnp.int32(2))
             block = u[t] * jnp.where(t < n[0], 1.0, 0.0).astype(jnp.float32)
             for out, x in ((lower, block), (upper, block.T)):
                 high, low = halves(x)
@@ -42,7 +43,7 @@
     return pl.pallas_call(
         kernel,
         out_shape=(
-            both, both, jax.ShapeDtypeStruct((4 * slots,), jnp.int32),
+            both, both, jax.ShapeDtypeStruct((5 * slots,), jnp.int32),
             jax.ShapeDtypeStruct(start.shape, jnp.float32),
         ),
         in_specs=[SMEM] * 3 + [VMEM] * 3,
@@ -100,27 +101,25 @@
     )(start)
 
 
-def upper_products(table, blocks, own_cols, other_cols, row_blocks):
-    ys, splits, vectors, size = own_cols.shape
+def upper_products(table, blocks, cols, row_blocks):
+    _, _, _, vectors, size = cols.shape
     slots = blocks.shape[0]
 
-    def kernel(at, u, own, other, out, both):
-        both[0], both[1] = own[...], other[...]
+    def kernel(at, u, x, out):
         out[...] = jnp.zeros_like(out)
         for t in range(slots):
-            x = both[at[slots + t], at[2 * slots + t], at[3 * slots + t]]
-            out[at[t]] += product(x, u[t])
+            place = at[4 * slots + t], at[2 * slots + t], at[3 * slots + t]
+            out[at[t]] += product(x[place], u[t])
 
     return pl.pallas_call(
         kernel,
         out_shape=arrays((row_blocks, vectors, size))[0],
-        in_specs=[SMEM] + [VMEM] * 3,
+        in_specs=[SMEM] + [VMEM] * 2,
         out_specs=VMEM,
-        scratch_shapes=[pltpu.VMEM((2, ys, splits, vectors, size), jnp.float32)],
         compiler_params=PARAMS,
         cost_estimate=cost(blocks, vectors),
         name="upper",
-    )(table, blocks, own_cols, other_cols)
+    )(table, blocks, cols)
 
 
 def lower_products(table, blocks, row_piece, start_piece, ys, splits):
@@ -155,14 +154,14 @@
     )(table, blocks, row_piece, *((start_piece,) if with_corr else ()))
 
 
-def add(one, two):
+def add_from_other(own, cores):
     def kernel(a, b, out):
-        out[...] = a[...] + b[...]
-
-    return pl.pallas_call(
-        kernel, out_shape=arrays(one.shape)[0], in_specs=[VMEM] * 2, out_specs=VMEM,
-        compiler_params=PARAMS, name="add",
-    )(one, two)
+        out[...] = a[...] + b[1 - lax.axis_index("core")]
+
+    return pl.pallas_call(
+        kernel, out_shape=arrays(own.shape)[0], in_specs=[VMEM] * 2, out_specs=VMEM,
+        compiler_params=PARAMS, name="add_from_other",
+    )(own, cores)
 
 
 def own_copies(row_piece, prepared, splits, copies):
@@ -282,8 +281,8 @@
     return lax.all_to_all(parts, axis, 0, 0, tiled=True)
 
 
-def swap_cores(piece):
-    return lax.ppermute(piece, "core", [(0, 1), (1, 0)])
+def both_cores(piece):
+    return lax.all_gather(piece, "core", axis=0, tiled=False)
 
 
 def on_device(start_vectors, diag_energy, matrix_blocks, block_rows, block_cols, counts):
@@ -304,8 +303,8 @@
     )
     own_cols = exchange(own_copies(start_row, scaled, splits, ys), "y")
     own, other = lower_products(table, lower, start_row, None, ys, splits)
-    col_got = exchange(add(own, swap_cores(other)), "y")
-    rows = upper_products(table, upper, own_cols, swap_cores(own_cols), cols * splits)
+    col_got = exchange(add_from_other(own, both_cores(other)), "y")
+    rows = upper_products(table, upper, both_cores(own_cols), cols * splits)
     row_got = exchange(rows.reshape(cols, splits, vectors, size), "col")
     parts = exchange(group_part(row_got, col_got, scaled), "split")
 
@@ -313,8 +312,8 @@
     first_row = exchange(col_copies, "col").reshape(cols * splits, vectors, size)
     own_cols = exchange(y_copies, "y")
     own, other = lower_products(table, lower, first_row, start_row, ys, splits)
-    col_got = exchange(add(own, swap_cores(other)), "y")
-    rows = upper_products(table, upper, own_cols, swap_cores(own_cols), cols * splits)
+    col_got = exchange(add_from_other(own, both_cores(other)), "y")
+    rows = upper_products(table, upper, both_cores(own_cols), cols * splits)
     messages, corr = add_to_messages(col_got, rows)
     got = exchange(messages, plane)
     residual = residual_of(corr, first, start_vectors, total)

time: 151 us -> 150 us (level)
  blocking collectives: 37.9 us -> 46 us
  starting transfers between devices: 50 us -> 42.3 us
    all_gather x0 -> x4, blocking collectives: none -> 8.03 us  [both_cores(): return lax.all_gather(piece, 'core', axis=0, tiled=False)]
    ppermute x4 -> x0, starting transfers between devices: 7.68 us -> none  [swap_cores(): return lax.ppermute(piece, 'core', [(0, 1), (1, 0)])]
    ppermute x4 -> x0, waiting for transfers between devices: 5.3 us -> none  [swap_cores(): return lax.ppermute(piece, 'core', [(0, 1), (1, 0)])]
    all_to_all x6, waiting for transfers between devices: 41.5 us -> 46.4 us  [exchange(): return lax.all_to_all(parts, axis, 0, 0, tiled=True)]
  transfers between devices with their start and end apart: 10 -> 6, of which waited for: 10 -> 6; matrix products, arithmetic and copies ran while one was open for 0% -> 0% of each run, Pallas kernels for 5% -> 5%
where the time goes in v6:
time: 150 us; the launch traced here: 149 us
  waiting for transfers between devices  46.4 us (31%)
  blocking collectives  46 us (31%)
  starting transfers between devices  42.3 us (28%)
  Pallas kernels  10.4 us (7%)
  local copies, waits for them, and re-layouts  2.58 us (2%)
    all_to_all x6, waiting for transfers between devices, exchange(): return lax.all_to_all(parts, axis, 0, 0, tiled=True)  46.4 us
    all_to_all x6, starting transfers between devices, exchange(): return lax.all_to_all(parts, axis, 0, 0, tiled=True)  42.3 us
    all_to_all x3, blocking collectives, exchange(): return lax.all_to_all(parts, axis, 0, 0, tiled=True)  37.9 us
    all_gather x4, blocking collectives, both_cores(): return lax.all_gather(piece, 'core', axis=0, tiled=False)  8.03 us
  transfers between devices with their start and end apart: 6, of which 6 were waited for; matrix products, arithmetic and copies ran while one was open for 0% of the time, Pallas kernels for 5%

profile of v6, /device:TPU:6, one launch (start us, length us, event | category | flops | bytes accessed | tf_op | source)
XLA Modules:
  0.0 149.1 jit_solution(9205959863529128916)
XLA Ops:
  0.6 0.0 copy-start.1
  0.6 0.7 copy-done.1
  1.3 0.7 start_copies.1
  2.0 18.4 %all-to-all-start = ((f32[48,8,128]{2,1,0:T(8,128)}), f32[48,8,128]{2,1,0:T(8,128)S(1)}, u32[]{:S(2)}, u32[]{:S(2)}) async-start(f32[48,8,128]{2,1,0:T(8,128)} %start_copies.1), calls=%async_computation | async-start | bytes 393216 | tf_op jit(solution)/shard_map/all_to_all | solution.py:281
  21.1 0.0 copy-start.2
  21.1 0.0 copy-start.3
  21.1 0.0 copy-start.4
  21.1 0.0 copy-start.5
  21.1 0.6 copy-done.2
  21.8 0.0 copy-done.3
  21.8 0.0 copy-done.4
  21.8 0.0 copy-done.5
  21.8 0.0 copy-start
  21.8 1.2 copy-done
  23.0 1.6 %prepare.1 = (bf16[16,128,256]{2,1,0:T(8,128)(2,1)S(1)}, bf16[16,128,256]{2,1,0:T(8,128)(2,1)S(1)}, s32[80]{0:T(128)S(1)}, f32[8,128]{1,0:T(8,128)S(1)}) custom-call(s32[16]{0:T(128)S(1)} %bitcast.21, s32[16]{0:T(128)S(1)} %bitcast.22, s32[1]{0:T(128)} %bitcast.11.n, f32[16,128,128]{2,1,0:T(8,128)S(1)} %bitcast.13, f32[8,128]{1,0:T(8,128)S(1)} %copy-done.2, ...), custom_call_target="tpu_custom_call" | custom-call | flops 2097152 | bytes 3145728 | tf_op jit(solution)/shard_map/prepare/pallas_call | solution.py:43
  24.6 10.5 %all-to-all-done.piece.x.rest_0_ = f32[48,8,128]{2,1,0:T(8,128)S(1)} async-done(((f32[48,8,128]{2,1,0:T(8,128)}), f32[48,8,128]{2,1,0:T(8,128)S(1)}, u32[]{:S(2)}, u32[]{:S(2)}) %all-to-all-start) | async-done | bytes 196640 | tf_op jit(solution)/shard_map/all_to_all | solution.py:281
  35.1 0.7 own_copies.1
  35.7 7.1 %all-to-all-start.1 = ((f32[8,4,8,128]{3,2,1,0:T(8,128)}), f32[8,4,8,128]{3,2,1,0:T(8,128)S(1)}, u32[]{:S(2)}, u32[]{:S(2)}) async-start(f32[8,4,8,128]{3,2,1,0:T(8,128)} %own_copies.1), calls=%async_computation.1 | async-start | bytes 262144 | tf_op jit(solution)/shard_map/all_to_all | solution.py:281
  42.8 0.8 lower.2
  43.7 2.0 %all-gather.1 = f32[16,4,8,128]{3,2,1,0:T(8,128)S(1)} all-gather(f32[8,4,8,128]{3,2,1,0:T(8,128)S(1)} %get-tuple-element.20), channel_id=3, replica_groups=mesh['y'=8,'core'=2,'col'=12,'split'=4] {'core'}, dimensions={0}, use_global_device_ids=true | all-gather | bytes 393216 | tf_op jit(solution)/shard_map/all_gather | solution.py:285
  45.7 0.7 add_from_other.2
  46.3 5.6 %all-to-all-done.1 = f32[8,4,8,128]{3,2,1,0:T(8,128)S(1)} async-done(((f32[8,4,8,128]{3,2,1,0:T(8,128)}), f32[8,4,8,128]{3,2,1,0:T(8,128)S(1)}, u32[]{:S(2)}, u32[]{:S(2)}) %all-to-all-start.1) | async-done | bytes 131104 | tf_op jit(solution)/shard_map/all_to_all | solution.py:281
  51.9 3.4 %all-to-all-start.3 = ((f32[8,4,8,128]{3,2,1,0:T(8,128)}), f32[8,4,8,128]{3,2,1,0:T(8,128)S(1)}, u32[]{:S(2)}, u32[]{:S(2)}) async-start(f32[8,4,8,128]{3,2,1,0:T(8,128)} %add_from_other.2), calls=%async_computation.3 | async-start | bytes 262144 | tf_op jit(solution)/shard_map/all_to_all | solution.py:281
  55.3 2.0 %all-gather = f32[16,4,8,128]{3,2,1,0:T(8,128)S(1)} all-gather(f32[8,4,8,128]{3,2,1,0:T(8,128)S(1)} %all-to-all-done.1), channel_id=2, replica_groups=mesh['y'=8,'core'=2,'col'=12,'split'=4] {'core'}, dimensions={0}, use_global_device_ids=true | all-gather | bytes 393216 | tf_op jit(solution)/shard_map/all_gather | solution.py:285
  57.3 0.8 upper.2
  58.1 6.2 %all-to-all-done.3.cols = f32[8,4,8,128]{3,2,1,0:T(8,128)S(1)} async-done(((f32[8,4,8,128]{3,2,1,0:T(8,128)}), f32[8,4,8,128]{3,2,1,0:T(8,128)S(1)}, u32[]{:S(2)}, u32[]{:S(2)}) %all-to-all-start.3) | async-done | bytes 131104 | tf_op jit(solution)/shard_map/all_to_all | solution.py:281
  64.3 11.0 %all_to_all.45.rows = f32[12,4,8,128]{3,2,1,0:T(8,128)S(1)} all-to-all(f32[12,4,8,128]{3,2,1,0:T(8,128)S(1)} %bitcast.18), channel_id=1, replica_groups=mesh['y'=8,'core'=2,'col'=12,'split'=4] {'col'}, dimensions={0} | all-to-all | bytes 393216 | tf_op jit(solution)/shard_map/all_to_all | solution.py:281
  75.3 16.3 %all_to_all.46.p = f32[4,4,8,128]{3,2,1,0:T(8,128)S(1)} all-to-all(f32[4,4,8,128]{3,2,1,0:T(8,128)S(1)} %group_part.1), channel_id=1, replica_groups=mesh['y'=8,'core'=2,'col'=12,'split'=4] {'split'}, dimensions={0} | all-to-all | bytes 131072 | tf_op jit(solution)/shard_map/all_to_all | solution.py:281
  91.5 0.7 image_copies.1
  92.2 10.7 %all_to_all.47 = f32[12,4,8,128]{3,2,1,0:T(8,128)S(1)} all-to-all(f32[12,4,8,128]{3,2,1,0:T(8,128)S(1)} %get-tuple-element.21), channel_id=1, replica_groups=mesh['y'=8,'core'=2,'col'=12,'split'=4] {'col'}, dimensions={0} | all-to-all | bytes 393216 | tf_op jit(solution)/shard_map/all_to_all | solution.py:281
  102.9 3.4 %all-to-all-start.7 = ((f32[8,4,8,128]{3,2,1,0:T(8,128)}), f32[8,4,8,128]{3,2,1,0:T(8,128)S(1)}, u32[]{:S(2)}, u32[]{:S(2)}) async-start(f32[8,4,8,128]{3,2,1,0:T(8,128)} %get-tuple-element.24), calls=%async_computation.7 | async-start | bytes 262144 | tf_op jit(solution)/shard_map/all_to_all | solution.py:281
  106.3 0.9 lower.3
  107.2 2.0 %all-gather.2 = f32[16,5,8,128]{3,2,1,0:T(8,128)S(1)} all-gather(f32[8,5,8,128]{3,2,1,0:T(8,128)S(1)} %get-tuple-element.23), channel_id=4, replica_groups=mesh['y'=8,'core'=2,'col'=12,'split'=4] {'core'}, dimensions={0}, use_global_device_ids=true | all-gather | bytes 491520 | tf_op jit(solution)/shard_map/all_gather | solution.py:285
  109.3 0.7 add_from_other.3
  109.9 5.4 %all-to-all-done.7 = f32[8,4,8,128]{3,2,1,0:T(8,128)S(1)} async-done(((f32[8,4,8,128]{3,2,1,0:T(8,128)}), f32[8,4,8,128]{3,2,1,0:T(8,128)S(1)}, u32[]{:S(2)}, u32[]{:S(2)}) %all-to-all-start.7) | async-done | bytes 131104 | tf_op jit(solution)/shard_map/all_to_all | solution.py:281
  115.3 3.4 %all-to-all-start.6 = ((f32[8,5,8,128]{3,2,1,0:T(8,128)}), f32[8,5,8,128]{3,2,1,0:T(8,128)S(1)}, u32[]{:S(2)}, u32[]{:S(2)}) async-start(f32[8,5,8,128]{3,2,1,0:T(8,128)} %add_from_other.3), calls=%async_computation.6 | async-start | bytes 327680 | tf_op jit(solution)/shard_map/all_to_all | solution.py:281
  118.7 2.0 %all-gather.3 = f32[16,4,8,128]{3,2,1,0:T(8,128)S(1)} all-gather(f32[8,4,8,128]{3,2,1,0:T(8,128)S(1)} %all-to-all-done.7), channel_id=5, replica_groups=mesh['y'=8,'core'=2,'col'=12,'split'=4] {'core'}, dimensions={0}, use_global_device_ids=true | all-gather | bytes 393216 | tf_op jit(solution)/shard_map/all_gather | solution.py:285
  120.7 0.8 upper.3.sums
  121.5 6.6 %all-to-all-done.6.got = f32[8,5,8,128]{3,2,1,0:T(8,128)S(1)} async-done(((f32[8,5,8,128]{3,2,1,0:T(8,128)}), f32[8,5,8,128]{3,2,1,0:T(8,128)S(1)}, u32[]{:S(2)}, u32[]{:S(2)}) %all-to-all-start.6) | async-done | bytes 163872 | tf_op jit(solution)/shard_map/all_to_all | solution.py:281
  128.0 0.7 add_to_messages.1
  128.7 6.7 %all-to-all-start.8 = ((f32[48,8,128]{2,1,0:T(8,128)}), f32[48,8,128]{2,1,0:T(8,128)S(1)}, u32[]{:S(2)}, u32[]{:S(2)}) async-start(f32[48,8,128]{2,1,0:T(8,128)} %get-tuple-element.27), calls=%async_computation.8 | async-start | bytes 393216 | tf_op jit(solution)/shard_map/all_to_all | solution.py:281
  135.4 0.7 residual.1
  136.1 12.2 %all-to-all-done.8.g = f32[48,8,128]{2,1,0:T(8,128)S(1)} async-done(((f32[48,8,128]{2,1,0:T(8,128)}), f32[48,8,128]{2,1,0:T(8,128)S(1)}, u32[]{:S(2)}, u32[]{:S(2)}) %all-to-all-start.8) | async-done | bytes 196640 | tf_op jit(solution)/shard_map/all_to_all | solution.py:281
  148.4 0.7 second.1
  (1 shorter events, 0.0 us)
Async XLA Ops:
  0.6 0.7 copy-start.1
  2.0 33.1 %all-to-all-start = ((f32[48,8,128]{2,1,0:T(8,128)}), f32[48,8,128]{2,1,0:T(8,128)S(1)}, u32[]{:S(2)}, u32[]{:S(2)}) async-start(f32[48,8,128]{2,1,0:T(8,128)} %start_copies.1), calls=%async_computation | async-start | bytes 393216 | tf_op jit(solution)/shard_map/all_to_all | solution.py:281
  21.1 0.7 copy-start.2
  21.1 0.7 copy-start.3
  21.1 0.7 copy-start.4
  21.1 0.7 copy-start.5
  21.8 1.2 copy-start
  35.7 16.2 %all-to-all-start.1 = ((f32[8,4,8,128]{3,2,1,0:T(8,128)}), f32[8,4,8,128]{3,2,1,0:T(8,128)S(1)}, u32[]{:S(2)}, u32[]{:S(2)}) async-start(f32[8,4,8,128]{3,2,1,0:T(8,128)} %own_copies.1), calls=%async_computation.1 | async-start | bytes 262144 | tf_op jit(solution)/shard_map/all_to_all | solution.py:281
  51.9 12.4 %all-to-all-start.3 = ((f32[8,4,8,128]{3,2,1,0:T(8,128)}), f32[8,4,8,128]{3,2,1,0:T(8,128)S(1)}, u32[]{:S(2)}, u32[]{:S(2)}) async-start(f32[8,4,8,128]{3,2,1,0:T(8,128)} %add_from_other.2), calls=%async_computation.3 | async-start | bytes 262144 | tf_op jit(solution)/shard_map/all_to_all | solution.py:281
  102.9 12.4 %all-to-all-start.7 = ((f32[8,4,8,128]{3,2,1,0:T(8,128)}), f32[8,4,8,128]{3,2,1,0:T(8,128)S(1)}, u32[]{:S(2)}, u32[]{:S(2)}) async-start(f32[8,4,8,128]{3,2,1,0:T(8,128)} %get-tuple-element.24), calls=%async_computation.7 | async-start | bytes 262144 | tf_op jit(solution)/shard_map/all_to_all | solution.py:281
  115.3 12.7 %all-to-all-start.6 = ((f32[8,5,8,128]{3,2,1,0:T(8,128)}), f32[8,5,8,128]{3,2,1,0:T(8,128)S(1)}, u32[]{:S(2)}, u32[]{:S(2)}) async-start(f32[8,5,8,128]{3,2,1,0:T(8,128)} %add_from_other.3), calls=%async_computation.6 | async-start | bytes 327680 | tf_op jit(solution)/shard_map/all_to_all | solution.py:281
  128.7 19.6 %all-to-all-start.8 = ((f32[48,8,128]{2,1,0:T(8,128)}), f32[48,8,128]{2,1,0:T(8,128)S(1)}, u32[]{:S(2)}, u32[]{:S(2)}) async-start(f32[48,8,128]{2,1,0:T(8,128)} %get-tuple-element.27), calls=%async_computation.8 | async-start | bytes 393216 | tf_op jit(solution)/shard_map/all_to_all | solution.py:281

commit v7 on v6

--- a/solution.py
+++ b/solution.py
@@ -23,7 +23,7 @@
 def prepare(row_ids, col_ids, count, blocks, start, diag, splits):
     slots, size, _ = blocks.shape
 
-    def kernel(r, c, n, u, v, d, lower, upper, table, scaled):
+    def kernel(r, c, n, u, v, d, lower, upper, table, scaled, own_start, own_diag):
         core = lax.axis_index("core")
         for t in range(slots):
             row, split = lax.div(c[t], jnp.int32(splits)), lax.rem(c[t], jnp.int32(splits))
@@ -38,16 +38,18 @@
                 out[t, :, :size] = high
                 out[t, :, size:] = low
         scaled[...] = v[...] * d[...]
+        own_start[...] = v[...]
+        own_diag[...] = jnp.broadcast_to(d[...], v.shape)
 
     both = jax.ShapeDtypeStruct((slots, size, 2 * size), jnp.bfloat16)
     return pl.pallas_call(
         kernel,
         out_shape=(
             both, both, jax.ShapeDtypeStruct((5 * slots,), jnp.int32),
-            jax.ShapeDtypeStruct(start.shape, jnp.float32),
+            *arrays(*[start.shape] * 3),
         ),
         in_specs=[SMEM] * 3 + [VMEM] * 3,
-        out_specs=(VMEM, VMEM, SMEM, VMEM),
+        out_specs=(VMEM, VMEM, SMEM, VMEM, VMEM, VMEM),
         compiler_params=PARAMS,
         cost_estimate=pl.CostEstimate(
             flops=8 * blocks.size, bytes_accessed=12 * blocks.size, transcendentals=0
@@ -253,28 +255,19 @@
     )
 
 
-def residual_of(corr, first, start, total):
-    def kernel(c, f, v, out):
-        out[...] = subtract(c[...], f[...], v[...], total)
-
-    return pl.pallas_call(
-        kernel, out_shape=arrays(first.shape)[0], in_specs=[VMEM] * 3, out_specs=VMEM,
-        compiler_params=PARAMS, name="residual",
-    )(corr, first, start)
-
-
-def second_of(got, corr, first, diag, total):
-    def kernel(g, c, f, d, out):
+def results(got, corr, first, start, diag, total):
+    def kernel(g, c, f, v, d, residual, second):
         value = f[...]
         image = d[...] * value
         for k in range(g.shape[0]):
             image += g[k]
-        out[...] = subtract(c[...], image, value, total)
-
-    return pl.pallas_call(
-        kernel, out_shape=arrays(first.shape)[0], in_specs=[VMEM] * 4, out_specs=VMEM,
-        compiler_params=PARAMS, name="second",
-    )(got, corr, first, diag)
+        residual[...] = subtract(c[...], value, v[...], total)
+        second[...] = subtract(c[...], image, value, total)
+
+    return pl.pallas_call(
+        kernel, out_shape=arrays(first.shape, first.shape), in_specs=[VMEM] * 5,
+        out_specs=(VMEM, VMEM), compiler_params=PARAMS, name="results",
+    )(got, corr, first, start, diag)
 
 
 def exchange(parts, axis):
@@ -298,7 +291,7 @@
     plane = ("col", "split")
 
     start_row = exchange(start_copies(start_vectors, cols * splits), plane)
-    lower, upper, table, scaled = prepare(
+    lower, upper, table, scaled, own_start, own_diag = prepare(
         row_ids, col_ids, count, blocks, start_vectors, diag, splits
     )
     own_cols = exchange(own_copies(start_row, scaled, splits, ys), "y")
@@ -316,8 +309,7 @@
     rows = upper_products(table, upper, both_cores(own_cols), cols * splits)
     messages, corr = add_to_messages(col_got, rows)
     got = exchange(messages, plane)
-    residual = residual_of(corr, first, start_vectors, total)
-    return residual, second_of(got, corr, first, diag, total)
+    return results(got, corr, first, own_start, own_diag, total)
 
 
 def solution(mesh):

time: 150 us -> 149 us (level)
  blocking collectives: 46 us -> 65.4 us
  waiting for transfers between devices: 46.4 us -> 34.2 us
  starting transfers between devices: 42.3 us -> 35.7 us
    all_to_all x3 -> x4, blocking collectives: 37.9 us -> 57.3 us  [exchange(): return lax.all_to_all(parts, axis, 0, 0, tiled=True)]
    all_to_all x6 -> x5, waiting for transfers between devices: 46.4 us -> 34.2 us  [exchange(): return lax.all_to_all(parts, axis, 0, 0, tiled=True)]
    all_to_all x6 -> x5, starting transfers between devices: 42.3 us -> 35.7 us  [exchange(): return lax.all_to_all(parts, axis, 0, 0, tiled=True)]
  transfers between devices with their start and end apart: 6 -> 5, of which waited for: 6 -> 5; matrix products, arithmetic and copies ran while one was open for 0% -> 0% of each run, Pallas kernels for 5% -> 4%
where the time goes in v7:
time: 149 us; the launch traced here: 148 us
  blocking collectives  65.4 us (44%)
  starting transfers between devices  35.7 us (24%)
  waiting for transfers between devices  34.2 us (23%)
  Pallas kernels  9.06 us (6%)
  local copies, waits for them, and re-layouts  2.58 us (2%)
    all_to_all x4, blocking collectives, exchange(): return lax.all_to_all(parts, axis, 0, 0, tiled=True)  57.3 us
    all_to_all x5, starting transfers between devices, exchange(): return lax.all_to_all(parts, axis, 0, 0, tiled=True)  35.7 us
    all_to_all x5, waiting for transfers between devices, exchange(): return lax.all_to_all(parts, axis, 0, 0, tiled=True)  34.2 us
    all_gather x4, blocking collectives, both_cores(): return lax.all_gather(piece, 'core', axis=0, tiled=False)  8.03 us
  transfers between devices with their start and end apart: 5, of which 5 were waited for; matrix products, arithmetic and copies ran while one was open for 0% of the time, Pallas kernels for 4%

profile of v7, /device:TPU:6, one launch (start us, length us, event | category | flops | bytes accessed | tf_op | source)
XLA Modules:
  0.0 148.2 jit_solution(15052193717179278237)
XLA Ops:
  0.6 0.0 copy-start.1
  0.6 0.7 copy-done.1
  1.3 0.7 start_copies.1
  2.0 18.4 %all-to-all-start = ((f32[48,8,128]{2,1,0:T(8,128)}), f32[48,8,128]{2,1,0:T(8,128)S(1)}, u32[]{:S(2)}, u32[]{:S(2)}) async-start(f32[48,8,128]{2,1,0:T(8,128)} %start_copies.1), calls=%async_computation | async-start | bytes 393216 | tf_op jit(solution)/shard_map/all_to_all | solution.py:274
  21.1 0.0 copy-start.2
  21.1 0.0 copy-start.3
  21.1 0.0 copy-start.4
  21.1 0.0 copy-start.5
  21.1 0.6 copy-done.2
  21.8 0.0 copy-done.3
  21.8 0.0 copy-done.4
  21.8 0.0 copy-done.5
  21.8 0.0 copy-start
  21.8 1.2 copy-done
  23.0 1.6 %prepare.1 = (bf16[16,128,256]{2,1,0:T(8,128)(2,1)S(1)}, bf16[16,128,256]{2,1,0:T(8,128)(2,1)S(1)}, s32[80]{0:T(128)S(1)}, f32[8,128]{1,0:T(8,128)S(1)}, f32[8,128]{1,0:T(8,128)S(1)}, /*index=5*/f32[8,128]{1,0:T(8,128)S(1)}) custom-call(s32[16]{0:T(128)S(1)} %bitcast.19, s32[16]{0:T(128)S(1)} %bitcast.20, s32[1]{0:T(128)} %bitcast.11.n, ...), custom_call_target="tpu_custom_call" | custom-call | flops 2097152 | bytes 3145728 | tf_op jit(solution)/shard_map/prepare/pallas_call | solution.py:45
  24.6 10.5 %all-to-all-done.piece.x.rest_0_ = f32[48,8,128]{2,1,0:T(8,128)S(1)} async-done(((f32[48,8,128]{2,1,0:T(8,128)}), f32[48,8,128]{2,1,0:T(8,128)S(1)}, u32[]{:S(2)}, u32[]{:S(2)}) %all-to-all-start) | async-done | bytes 196640 | tf_op jit(solution)/shard_map/all_to_all | solution.py:274
  35.1 0.7 own_copies.1
  35.7 7.1 %all-to-all-start.1 = ((f32[8,4,8,128]{3,2,1,0:T(8,128)}), f32[8,4,8,128]{3,2,1,0:T(8,128)S(1)}, u32[]{:S(2)}, u32[]{:S(2)}) async-start(f32[8,4,8,128]{3,2,1,0:T(8,128)} %own_copies.1), calls=%async_computation.1 | async-start | bytes 262144 | tf_op jit(solution)/shard_map/all_to_all | solution.py:274
  42.8 0.8 lower.2
  43.7 2.0 %all-gather.1 = f32[16,4,8,128]{3,2,1,0:T(8,128)S(1)} all-gather(f32[8,4,8,128]{3,2,1,0:T(8,128)S(1)} %get-tuple-element.22), channel_id=3, replica_groups=mesh['y'=8,'core'=2,'col'=12,'split'=4] {'core'}, dimensions={0}, use_global_device_ids=true | all-gather | bytes 393216 | tf_op jit(solution)/shard_map/all_gather | solution.py:278
  45.6 0.7 add_from_other.2
  46.3 5.6 %all-to-all-done.1 = f32[8,4,8,128]{3,2,1,0:T(8,128)S(1)} async-done(((f32[8,4,8,128]{3,2,1,0:T(8,128)}), f32[8,4,8,128]{3,2,1,0:T(8,128)S(1)}, u32[]{:S(2)}, u32[]{:S(2)}) %all-to-all-start.1) | async-done | bytes 131104 | tf_op jit(solution)/shard_map/all_to_all | solution.py:274
  51.9 3.4 %all-to-all-start.3 = ((f32[8,4,8,128]{3,2,1,0:T(8,128)}), f32[8,4,8,128]{3,2,1,0:T(8,128)S(1)}, u32[]{:S(2)}, u32[]{:S(2)}) async-start(f32[8,4,8,128]{3,2,1,0:T(8,128)} %add_from_other.2), calls=%async_computation.3 | async-start | bytes 262144 | tf_op jit(solution)/shard_map/all_to_all | solution.py:274
  55.3 2.0 %all-gather = f32[16,4,8,128]{3,2,1,0:T(8,128)S(1)} all-gather(f32[8,4,8,128]{3,2,1,0:T(8,128)S(1)} %all-to-all-done.1), channel_id=2, replica_groups=mesh['y'=8,'core'=2,'col'=12,'split'=4] {'core'}, dimensions={0}, use_global_device_ids=true | all-gather | bytes 393216 | tf_op jit(solution)/shard_map/all_gather | solution.py:278
  57.3 0.8 upper.2
  58.1 6.2 %all-to-all-done.3.cols = f32[8,4,8,128]{3,2,1,0:T(8,128)S(1)} async-done(((f32[8,4,8,128]{3,2,1,0:T(8,128)}), f32[8,4,8,128]{3,2,1,0:T(8,128)S(1)}, u32[]{:S(2)}, u32[]{:S(2)}) %all-to-all-start.3) | async-done | bytes 131104 | tf_op jit(solution)/shard_map/all_to_all | solution.py:274
  64.3 11.0 %all_to_all.45.rows = f32[12,4,8,128]{3,2,1,0:T(8,128)S(1)} all-to-all(f32[12,4,8,128]{3,2,1,0:T(8,128)S(1)} %bitcast.18), channel_id=1, replica_groups=mesh['y'=8,'core'=2,'col'=12,'split'=4] {'col'}, dimensions={0} | all-to-all | bytes 393216 | tf_op jit(solution)/shard_map/all_to_all | solution.py:274
  75.3 16.3 %all_to_all.46.p = f32[4,4,8,128]{3,2,1,0:T(8,128)S(1)} all-to-all(f32[4,4,8,128]{3,2,1,0:T(8,128)S(1)} %group_part.1), channel_id=1, replica_groups=mesh['y'=8,'core'=2,'col'=12,'split'=4] {'split'}, dimensions={0} | all-to-all | bytes 131072 | tf_op jit(solution)/shard_map/all_to_all | solution.py:274
  91.5 0.7 image_copies.1
  92.2 10.7 %all_to_all.47 = f32[12,4,8,128]{3,2,1,0:T(8,128)S(1)} all-to-all(f32[12,4,8,128]{3,2,1,0:T(8,128)S(1)} %get-tuple-element.23), channel_id=1, replica_groups=mesh['y'=8,'core'=2,'col'=12,'split'=4] {'col'}, dimensions={0} | all-to-all | bytes 393216 | tf_op jit(solution)/shard_map/all_to_all | solution.py:274
  102.9 3.4 %all-to-all-start.7 = ((f32[8,4,8,128]{3,2,1,0:T(8,128)}), f32[8,4,8,128]{3,2,1,0:T(8,128)S(1)}, u32[]{:S(2)}, u32[]{:S(2)}) async-start(f32[8,4,8,128]{3,2,1,0:T(8,128)} %get-tuple-element.26), calls=%async_computation.7 | async-start | bytes 262144 | tf_op jit(solution)/shard_map/all_to_all | solution.py:274
  106.3 0.9 lower.3
  107.2 2.0 %all-gather.2 = f32[16,5,8,128]{3,2,1,0:T(8,128)S(1)} all-gather(f32[8,5,8,128]{3,2,1,0:T(8,128)S(1)} %get-tuple-element.25), channel_id=4, replica_groups=mesh['y'=8,'core'=2,'col'=12,'split'=4] {'core'}, dimensions={0}, use_global_device_ids=true | all-gather | bytes 491520 | tf_op jit(solution)/shard_map/all_gather | solution.py:278
  109.3 0.7 add_from_other.3
  109.9 5.4 %all-to-all-done.7 = f32[8,4,8,128]{3,2,1,0:T(8,128)S(1)} async-done(((f32[8,4,8,128]{3,2,1,0:T(8,128)}), f32[8,4,8,128]{3,2,1,0:T(8,128)S(1)}, u32[]{:S(2)}, u32[]{:S(2)}) %all-to-all-start.7) | async-done | bytes 131104 | tf_op jit(solution)/shard_map/all_to_all | solution.py:274
  115.3 3.4 %all-to-all-start.6 = ((f32[8,5,8,128]{3,2,1,0:T(8,128)}), f32[8,5,8,128]{3,2,1,0:T(8,128)S(1)}, u32[]{:S(2)}, u32[]{:S(2)}) async-start(f32[8,5,8,128]{3,2,1,0:T(8,128)} %add_from_other.3), calls=%async_computation.6 | async-start | bytes 327680 | tf_op jit(solution)/shard_map/all_to_all | solution.py:274
  118.7 2.0 %all-gather.3 = f32[16,4,8,128]{3,2,1,0:T(8,128)S(1)} all-gather(f32[8,4,8,128]{3,2,1,0:T(8,128)S(1)} %all-to-all-done.7), channel_id=5, replica_groups=mesh['y'=8,'core'=2,'col'=12,'split'=4] {'core'}, dimensions={0}, use_global_device_ids=true | all-gather | bytes 393216 | tf_op jit(solution)/shard_map/all_gather | solution.py:278
  120.7 0.8 upper.3.sums
  121.5 6.6 %all-to-all-done.6.got = f32[8,5,8,128]{3,2,1,0:T(8,128)S(1)} async-done(((f32[8,5,8,128]{3,2,1,0:T(8,128)}), f32[8,5,8,128]{3,2,1,0:T(8,128)S(1)}, u32[]{:S(2)}, u32[]{:S(2)}) %all-to-all-start.6) | async-done | bytes 163872 | tf_op jit(solution)/shard_map/all_to_all | solution.py:274
  128.1 19.4 %all_to_all.48.g = f32[48,8,128]{2,1,0:T(8,128)S(1)} all-to-all(f32[48,8,128]{2,1,0:T(8,128)S(1)} %get-tuple-element.27), channel_id=1, replica_groups=mesh['y'=8,'core'=2,'col'=12,'split'=4] {'col','split'}, dimensions={0} | all-to-all | bytes 393216 | tf_op jit(solution)/shard_map/all_to_all | solution.py:274
  147.5 0.7 results.1
  (2 shorter events, 0.1 us)
Async XLA Ops:
  0.6 0.7 copy-start.1
  2.0 33.1 %all-to-all-start = ((f32[48,8,128]{2,1,0:T(8,128)}), f32[48,8,128]{2,1,0:T(8,128)S(1)}, u32[]{:S(2)}, u32[]{:S(2)}) async-start(f32[48,8,128]{2,1,0:T(8,128)} %start_copies.1), calls=%async_computation | async-start | bytes 393216 | tf_op jit(solution)/shard_map/all_to_all | solution.py:274
  21.1 0.7 copy-start.2
  21.1 0.7 copy-start.3
  21.1 0.7 copy-start.4
  21.1 0.7 copy-start.5
  21.8 1.2 copy-start
  35.7 16.2 %all-to-all-start.1 = ((f32[8,4,8,128]{3,2,1,0:T(8,128)}), f32[8,4,8,128]{3,2,1,0:T(8,128)S(1)}, u32[]{:S(2)}, u32[]{:S(2)}) async-start(f32[8,4,8,128]{3,2,1,0:T(8,128)} %own_copies.1), calls=%async_computation.1 | async-start | bytes 262144 | tf_op jit(solution)/shard_map/all_to_all | solution.py:274
  51.9 12.4 %all-to-all-start.3 = ((f32[8,4,8,128]{3,2,1,0:T(8,128)}), f32[8,4,8,128]{3,2,1,0:T(8,128)S(1)}, u32[]{:S(2)}, u32[]{:S(2)}) async-start(f32[8,4,8,128]{3,2,1,0:T(8,128)} %add_from_other.2), calls=%async_computation.3 | async-start | bytes 262144 | tf_op jit(solution)/shard_map/all_to_all | solution.py:274
  102.9 12.4 %all-to-all-start.7 = ((f32[8,4,8,128]{3,2,1,0:T(8,128)}), f32[8,4,8,128]{3,2,1,0:T(8,128)S(1)}, u32[]{:S(2)}, u32[]{:S(2)}) async-start(f32[8,4,8,128]{3,2,1,0:T(8,128)} %get-tuple-element.26), calls=%async_computation.7 | async-start | bytes 262144 | tf_op jit(solution)/shard_map/all_to_all | solution.py:274
  115.3 12.7 %all-to-all-start.6 = ((f32[8,5,8,128]{3,2,1,0:T(8,128)}), f32[8,5,8,128]{3,2,1,0:T(8,128)S(1)}, u32[]{:S(2)}, u32[]{:S(2)}) async-start(f32[8,5,8,128]{3,2,1,0:T(8,128)} %add_from_other.3), calls=%async_computation.6 | async-start | bytes 327680 | tf_op jit(solution)/shard_map/all_to_all | solution.py:274
